TPU v7x, 512 devices: a whole 4x4x16 slice. The times are simulated.
512 devices in a mesh: dp: 32 (over x, z_lo), tensor: 16 (over y, z_hi, core).
Axes of the slice: x: 4, y: 4, z: 16 (z_hi: 2, z_lo: 8; z = z_hi * 8 + z_lo), core: 2. Of those that a mesh axis runs over, the one named last changes fastest.
Arguments:
- tokens: bfloat16 [1024, 8192], P('tensor', 'dp'), may hold values from -6 to 6
- out_grad: bfloat16 [1024, 8192], P('tensor', 'dp'), may hold values from -6 to 6
- gate_pre: bfloat16 [1024, 14336], P('dp', 'tensor'), may hold values from -8 to 8
- up_pre: bfloat16 [1024, 14336], P('dp', 'tensor'), may hold values from -6 to 6
- gate_weight: bfloat16 [8192, 14336], P('dp', 'tensor'), may hold values from -0.0625 to 0.0625
- up_weight: bfloat16 [8192, 14336], P('dp', 'tensor'), may hold values from -0.0625 to 0.0625
- down_weight: bfloat16 [14336, 8192], P('tensor', 'dp'), may hold values from -0.046875 to 0.046875
Outputs:
- gate_score: float32 [8192, 14336], P('dp', 'tensor')
- up_score: float32 [8192, 14336], P('dp', 'tensor')
- down_score: float32 [14336, 8192], P('tensor', 'dp')
- input_grad: bfloat16 [1024, 8192], P('tensor', 'dp')
All inputs are finite; a program needn't handle non-finite values.
Results may differ from a plain program's by a relative error of at most 0.0049.
Values may be sent and summed in bfloat16 or wider, within the bound.
No kernel may reach another device: no remote copies, remote signals or barrier semaphores. Data moves between devices by JAX's collectives and lax.ppermute only.
A program may use at most 64 MiB of HBM per device.

v0:
```python
import jax
import jax.numpy as jnp
from jax import lax
from jax.sharding import PartitionSpec as P


def gate_back(hidden_grad, gate_pre, up_pre):
    gate_float = gate_pre.astype(jnp.float32)
    up_float = up_pre.astype(jnp.float32)
    gate_sigmoid = 1.0 / (1.0 + jnp.exp(-gate_float))
    gate_grad = (
        hidden_grad * up_float * gate_sigmoid * (1.0 + gate_float * (1.0 - gate_sigmoid))
    ).astype(jnp.bfloat16)
    up_grad = (hidden_grad * gate_float * gate_sigmoid).astype(jnp.bfloat16)
    return (gate_grad, up_grad)


def activate(gate_pre, up_pre):
    gate_float = gate_pre.astype(jnp.float32)
    gate_sigmoid = 1.0 / (1.0 + jnp.exp(-gate_float))
    return (gate_float * gate_sigmoid * up_pre.astype(jnp.float32)).astype(jnp.bfloat16)


def on_device(tokens, out_grad, gate_pre, up_pre, gate_weight, up_weight, down_weight):
    grads_all = lax.all_gather(out_grad, "tensor", axis=0, tiled=True)
    gate_all, up_all = (
        lax.all_gather(gate_pre, "dp", axis=0, tiled=True),
        lax.all_gather(up_pre, "dp", axis=0, tiled=True),
    )
    active = activate(gate_all, up_all)
    partial_grad = jnp.einsum(
        "nd,fd->nf", grads_all, down_weight, preferred_element_type=jnp.float32
    )
    hidden_grad = lax.psum(partial_grad, "dp")
    gate_grad, up_grad = gate_back(hidden_grad, gate_all, up_all)
    down_sum = jnp.einsum("nf,nd->fd", active, grads_all, preferred_element_type=jnp.float32)
    piece = lax.all_gather(tokens, "tensor", axis=0, tiled=True)
    gate_rows = gate_grad
    up_rows = up_grad
    gate_sum = jnp.einsum("nd,nf->df", piece, gate_rows, preferred_element_type=jnp.float32)
    up_sum = jnp.einsum("nd,nf->df", piece, up_rows, preferred_element_type=jnp.float32)
    gate_rows = gate_grad
    up_rows = up_grad
    input_grad = lax.psum_scatter(
        jnp.einsum("nf,df->nd", gate_rows, gate_weight, preferred_element_type=jnp.float32)
        + jnp.einsum("nf,df->nd", up_rows, up_weight, preferred_element_type=jnp.float32),
        "tensor",
        scatter_dimension=0,
        tiled=True,
    ).astype(jnp.bfloat16)
    gate_score = jnp.abs(gate_weight.astype(jnp.float32) * gate_sum)
    up_score = jnp.abs(up_weight.astype(jnp.float32) * up_sum)
    down_score = jnp.abs(down_weight.astype(jnp.float32) * down_sum)
    return (gate_score, up_score, down_score, input_grad)


def solution(mesh):
    return jax.shard_map(
        on_device,
        mesh=mesh,
        in_specs=(
            P("tensor", "dp"),
            P("tensor", "dp"),
            P("dp", "tensor"),
            P("dp", "tensor"),
            P("dp", "tensor"),
            P("dp", "tensor"),
            P("tensor", "dp"),
        ),
        out_specs=(P("dp", "tensor"), P("dp", "tensor"), P("tensor", "dp"), P("tensor", "dp")),
        check_vma=False,
    )
```

profile of v0, /device:TPU:2, one launch (start us, length us, event | category | flops | bytes accessed | tf_op | source)
XLA Modules:
  0.0 1072.5 jit_solution(16701409394368995680)
XLA Ops:
  7.2 0.7 all-gather.3.cloned.1.call-update
  7.9 0.0 all-gather.5.cloned.1.call-start
  7.9 0.7 all-gather.5.cloned.1.call-update
  8.6 0.0 all-reduce.2.cloned.1.call-start
  8.7 62.0 %all_gather.12 = bf16[1024,256]{1,0:T(8,128)(2,1)S(1)} all-gather(bf16[64,256]{1,0:T(8,128)(2,1)} %param.8), channel_id=1, replica_groups=mesh['dp'=32,'tensor'=16] {'tensor'}, dimensions={0}, use_global_device_ids=true | all-gather | bytes 557056 | tf_op jit(solution)/shard_map/all_gather | solution.py:25
  70.7 3.7 fusion.23
  74.4 0.0 reduce-scatter.2.cloned.1.call-start
  74.5 1.0 copy.11
  75.5 1.0 copy.12
  76.4 148.6 %all-gather.3.cloned.1.call-done = bf16[1024,896]{1,0:T(8,128)(2,1)} async-done(((bf16[32,896]{1,0:T(8,128)(2,1)}), bf16[1024,896]{1,0:T(8,128)(2,1)}) %all-gather.3.cloned.1.call-update) | async-done | bytes 1835024 | tf_op jit(solution)/shard_map/all_gather | solution.py:28
  225.0 228.3 %all-gather.5.cloned.1.call-done = bf16[1024,896]{1,0:T(8,128)(2,1)} async-done(((bf16[32,896]{1,0:T(8,128)(2,1)}), bf16[1024,896]{1,0:T(8,128)(2,1)}) %all-gather.5.cloned.1.call-update) | async-done | bytes 1835024 | tf_op jit(solution)/shard_map/all_gather | solution.py:27
  453.4 479.8 %all-reduce.2.cloned.1.call-done = f32[1024,896]{1,0:T(8,128)} async-done(((f32[1024,896]{1,0:T(8,128)}), f32[1024,896]{1,0:T(8,128)}) %all-reduce.2.cloned.1.call-update) | async-done | bytes 3670032 | tf_op jit(solution)/shard_map/psum | solution.py:34
  933.2 4.0 fusion.9
  937.3 0.7 fusion.24
  938.0 0.5 copy-done
  938.5 1.7 convolution_add_fusion
  940.2 49.9 %all_gather.15 = bf16[1024,256]{1,0:T(8,128)(2,1)S(1)} all-gather(bf16[64,256]{1,0:T(8,128)(2,1)S(1)} %copy-done.4), channel_id=1, replica_groups=mesh['dp'=32,'tensor'=16] {'tensor'}, dimensions={0}, use_global_device_ids=true | all-gather | bytes 557056 | tf_op jit(solution)/shard_map/all_gather | solution.py:37
  990.2 4.4 fusion.19
  994.6 0.7 fusion.13
  995.3 1.2 copy.13
  996.5 2.2 fusion.15
  998.8 1.2 copy.14
  1000.0 64.5 %reduce-scatter.2.cloned.1.call-done = f32[64,256]{1,0:T(8,128)} async-done(((f32[1024,256]{1,0:T(8,128)}), f32[64,256]{1,0:T(8,128)}) %reduce-scatter.2.cloned.1.call-update) | async-done | bytes 65552 | tf_op jit(solution)/shard_map/reduce_scatter | solution.py:44
  1064.5 1.5 convert_element_type.37
  (12 shorter events, 0.1 us)
Async XLA Ops:
  7.2 217.9 %all-gather.3.cloned.1.call-start = ((), (), s32[]{:S(2)}) async-start(), calls=%async_computation.2 | async-start | bytes 1892352 | tf_op jit(solution)/shard_map/all_gather | solution.py:28
  7.9 445.5 %all-gather.5.cloned.1.call-start = ((), (), s32[]{:S(2)}) async-start(), calls=%async_computation.3 | async-start | bytes 1892352 | tf_op jit(solution)/shard_map/all_gather | solution.py:27
  8.6 924.6 %all-reduce.2.cloned.1.call-start = ((), (), s32[]{:S(2)}) async-start(), calls=%async_computation.1 | async-start | bytes 7340032 | tf_op jit(solution)/shard_map/psum | solution.py:34
  70.7 3.8 copy-start.2
  70.7 4.8 copy-start.1
  74.4 990.1 %reduce-scatter.2.cloned.1.call-start = ((), (), s32[]{:S(2)}) async-start(), calls=%async_computation.4 | async-start | bytes 1114112 | tf_op jit(solution)/shard_map/reduce_scatter | solution.py:44
  937.2 1.3 copy-start
  937.2 3.0 copy-start.4
  990.2 4.4 copy-start.3
Sparse Core Ops, SparseCore 0:
  10.1 214.9 all-gather.2
  227.1 226.2 all-gather.4
  456.3 476.8 all-reduce.1
  940.4 124.1 reduce-scatter.1
where the time goes:
time: 1070 us
  waiting for transfers between devices  923 us (86%)
  blocking collectives  112 us (10%)
  between operations  13.8 us (1%)
  matrix products  13.5 us (1%)
    psum x1, waiting for transfers between devices, on_device(): hidden_grad = lax.psum(partial_grad, 'dp')  480 us
    all_gather x1, waiting for transfers between devices, on_device(): lax.all_gather(gate_pre, 'dp', axis=0, tiled=True)  228 us
    all_gather x1, waiting for transfers between devices, on_device(): lax.all_gather(up_pre, 'dp', axis=0, tiled=True)  149 us
    reduce_scatter x1, waiting for transfers between devices, on_device(): lax.psum_scatter(jnp.einsum('nf,df->nd', gate_rows, gate_weight, preferre...  64.5 us
    all_gather x1, blocking collectives, on_device(): grads_all = lax.all_gather(out_grad, 'tensor', axis=0, tiled=True)  62 us
    all_gather x1, blocking collectives, on_device(): piece = lax.all_gather(tokens, 'tensor', axis=0, tiled=True)  49.9 us
  transfers between devices with their start and end apart: 4, of which 4 were waited for; matrix products, arithmetic and copies ran while one was open for 1% of the time, Pallas kernels for 0%

commit v1 on v0

v1 whole, which is shorter than its diff:
```python
import jax
import jax.numpy as jnp
from jax import lax
from jax.sharding import PartitionSpec as P

X, ZL, Y, ZH, C = 4, 8, 4, 2, 2
X_GROUPS = [[x * ZL + z for x in range(X)] for z in range(ZL)]
Z_GROUPS = [[x * ZL + z for z in range(ZL)] for x in range(X)]
ZH_GROUPS = [[(y * ZH + h) * C + c for h in range(ZH)] for y in range(Y) for c in range(C)]
Y_GROUPS = [[(y * ZH + h) * C + c for y in range(Y)] for h in range(ZH) for c in range(C)]
C_GROUPS = [[(y * ZH + h) * C + c for c in range(C)] for y in range(Y) for h in range(ZH)]
YZH_GROUPS = [[(y * ZH + h) * C + c for y in range(Y) for h in range(ZH)] for c in range(C)]


def exchange(blocks, axis, groups):
    return lax.all_to_all(blocks, axis, 0, 0, axis_index_groups=groups, tiled=True)


def gather(block, axis, groups):
    copies = jnp.broadcast_to(block[None], (len(groups[0]),) + block.shape)
    return exchange(copies, axis, groups)


def add_up(blocks, axis, groups):
    return jnp.sum(exchange(blocks, axis, groups).astype(jnp.float32), axis=0)


def on_device(tokens, out_grad, gate_pre, up_pre, gate_weight, up_weight, down_weight):
    rows, feats = out_grad.shape
    toks, hid = gate_pre.shape
    n = rows * Y * ZH * C

    both = jnp.stack([out_grad, tokens])
    both = gather(both, "tensor", ZH_GROUPS)
    both = gather(both, "tensor", Y_GROUPS)
    both = gather(both, "tensor", C_GROUPS)
    both = both.transpose(3, 1, 2, 0, 4, 5).reshape(2, n, feats)
    grads_all, tokens_all = both[0], both[1]

    saved = jnp.stack([gate_pre, up_pre])
    saved = gather(saved, "dp", Z_GROUPS)
    saved = gather(saved, "dp", X_GROUPS)
    gate_all = saved[:, :, 0].reshape(n, hid)
    up_all = saved[:, :, 1].reshape(n, hid)

    partial = jnp.einsum(
        "nd,fd->nf", grads_all, down_weight, preferred_element_type=jnp.float32
    ).astype(jnp.bfloat16)
    hidden = add_up(partial.reshape(X, ZL * toks, hid), "dp", X_GROUPS).astype(jnp.bfloat16)
    hidden = add_up(hidden.reshape(ZL, toks, hid), "dp", Z_GROUPS).astype(jnp.bfloat16)
    hidden = gather(hidden, "dp", Z_GROUPS)
    hidden = gather(hidden, "dp", X_GROUPS).reshape(n, hid).astype(jnp.float32)

    gate_float = gate_all.astype(jnp.float32)
    up_float = up_all.astype(jnp.float32)
    gate_sigmoid = 1.0 / (1.0 + jnp.exp(-gate_float))
    active = (gate_float * gate_sigmoid * up_float).astype(jnp.bfloat16)
    gate_grad = (
        hidden * up_float * gate_sigmoid * (1.0 + gate_float * (1.0 - gate_sigmoid))
    ).astype(jnp.bfloat16)
    up_grad = (hidden * gate_float * gate_sigmoid).astype(jnp.bfloat16)

    partial_in = jnp.einsum(
        "nf,df->nd", gate_grad, gate_weight, preferred_element_type=jnp.float32
    ) + jnp.einsum("nf,df->nd", up_grad, up_weight, preferred_element_type=jnp.float32)
    partial_in = partial_in.reshape(Y * ZH, C, rows, feats).transpose(1, 0, 2, 3)
    partial_in = add_up(partial_in, "tensor", C_GROUPS).astype(jnp.bfloat16)
    input_grad = add_up(partial_in, "tensor", YZH_GROUPS).astype(jnp.bfloat16)

    down_sum = jnp.einsum("nf,nd->fd", active, grads_all, preferred_element_type=jnp.float32)
    gate_sum = jnp.einsum("nd,nf->df", tokens_all, gate_grad, preferred_element_type=jnp.float32)
    up_sum = jnp.einsum("nd,nf->df", tokens_all, up_grad, preferred_element_type=jnp.float32)
    gate_score = jnp.abs(gate_weight.astype(jnp.float32) * gate_sum)
    up_score = jnp.abs(up_weight.astype(jnp.float32) * up_sum)
    down_score = jnp.abs(down_weight.astype(jnp.float32) * down_sum)
    return (gate_score, up_score, down_score, input_grad)


def solution(mesh):
    return jax.shard_map(
        on_device,
        mesh=mesh,
        in_specs=(
            P("tensor", "dp"),
            P("tensor", "dp"),
            P("dp", "tensor"),
            P("dp", "tensor"),
            P("dp", "tensor"),
            P("dp", "tensor"),
            P("tensor", "dp"),
        ),
        out_specs=(P("dp", "tensor"), P("dp", "tensor"), P("tensor", "dp"), P("tensor", "dp")),
        check_vma=False,
    )
```

time: 1070 us -> 297 us (0.28)
  the two profiles are of different devices: /device:TPU:2 before, /device:TPU:33 now
where the time goes in v1:
time: 297 us; the launch traced here: 296 us
  blocking collectives  127 us (43%)
  waiting for transfers between devices  115 us (39%)
  starting transfers between devices  25.2 us (8%)
  other arithmetic  16.1 us (5%)
  matrix products  7.17 us (2%)
  local copies, waits for them, and re-layouts  4.99 us (2%)
    all_to_all x6, blocking collectives, exchange(): lax.all_to_all(blocks, axis, 0, 0, axis_index_groups=groups, tiled=True)  127 us
    all_to_all x5, waiting for transfers between devices, exchange(): lax.all_to_all(blocks, axis, 0, 0, axis_index_groups=groups, tiled=True)  115 us
    all_to_all x5, starting transfers between devices, exchange(): lax.all_to_all(blocks, axis, 0, 0, axis_index_groups=groups, tiled=True)  25.2 us
    convert_element_type x2, other arithmetic, on_device(): up_grad = (hidden * gate_float * gate_sigmoid).astype(jnp.bfloat16)  7.13 us
  transfers between devices with their start and end apart: 5, of which 5 were waited for; matrix products, arithmetic and copies ran while one was open for 5% of the time, Pallas kernels for 0%

profile of v1, /device:TPU:33, one launch (start us, length us, event | category | flops | bytes accessed | tf_op | source)
XLA Modules:
  0.0 296.0 jit_solution(10511533810546887737)
XLA Ops:
  1.4 25.7 %all_to_all.55 = bf16[2,2,64,256]{3,2,1,0:T(8,128)(2,1)S(1)} all-to-all(bf16[2,2,64,256]{3,2,1,0:T(8,128)(2,1)S(1)} %broadcast_in_dim.14), channel_id=1, replica_groups={{0,2},{1,3},{4,6},{5,7},{8,10},{9,11},{12,14},{13,15},{16,18},{17,19},{..., dimensions={0} | all-to-all | bytes 262144 | tf_op jit(solution)/shard_map/all_to_all | solution.py:16
  27.2 10.9 %all_to_all.56 = bf16[4,2,2,64,256]{4,3,1,2,0:T(8,128)(2,1)S(1)} all-to-all(bf16[4,2,2,64,256]{4,3,1,2,0:T(8,128)(2,1)S(1)} %broadcast_in_dim.15), channel_id=1, replica_groups={{0,4,8,12},{1,5,9,13},{2,6,10,14},{3,7,11,15},{16,20,24,28},{17,21,25,2..., dimensions={0} | all-to-all | bytes 1048576 | tf_op jit(solution)/shard_map/all_to_all | solution.py:16
  38.3 11.0 %all_to_all.57 = bf16[2,4,2,2,64,256]{5,4,2,1,3,0:T(8,128)(2,1)S(1)} all-to-all(bf16[2,4,2,2,64,256]{5,4,2,1,3,0:T(8,128)(2,1)S(1)} %broadcast_in_dim.16), channel_id=1, replica_groups={{0,1},{2,3},{4,5},{6,7},{8,9},{10,11},{12,13},{14,15},{16,17},{18,19},{..., dimensions={0} | all-to-all | bytes 2097152 | tf_op jit(solution)/shard_map/all_to_all | solution.py:16
  50.4 26.6 %all_to_all.58 = bf16[4,256,896]{2,1,0:T(8,128)(2,1)S(1)} all-to-all(bf16[4,256,896]{2,1,0:T(8,128)(2,1)S(1)} %bitcast.93), channel_id=1, replica_groups={{0,128,256,384},{16,144,272,400},{32,160,288,416},{48,176,304,432},{64,..., dimensions={0} | all-to-all | bytes 3670016 | tf_op jit(solution)/shard_map/all_to_all | solution.py:16
  78.1 3.4 %all-to-all-start.4 = ((bf16[8,32,896]{2,1,0:T(8,128)(2,1)}), bf16[8,32,896]{2,1,0:T(8,128)(2,1)S(1)}, u32[]{:S(2)}, u32[]{:S(2)}) async-start(bf16[8,32,896]{2,1,0:T(8,128)(2,1)} %bitcast.6), calls=%async_computation.4 | async-start | bytes 917504 | tf_op jit(solution)/shard_map/all_to_all | solution.py:16
  81.6 23.0 %all-to-all-done.4 = bf16[8,32,896]{2,1,0:T(8,128)(2,1)S(1)} async-done(((bf16[8,32,896]{2,1,0:T(8,128)(2,1)}), bf16[8,32,896]{2,1,0:T(8,128)(2,1)S(1)}, u32[]{:S(2)}, u32[]{:S(2)}) %all-to-all-start.4) | async-done | bytes 458784 | tf_op jit(solution)/shard_map/all_to_all | solution.py:16
  105.6 6.4 %all-to-all-start.7 = ((bf16[8,2,32,896]{3,2,1,0:T(8,128)(2,1)}), bf16[8,2,32,896]{3,2,1,0:T(8,128)(2,1)S(1)}, u32[]{:S(2)}, u32[]{:S(2)}) async-start(bf16[8,2,32,896]{3,2,1,0:T(8,128)(2,1)} %broadcast_in_dim.19), calls=%async_computation.7 | async-start | bytes 1835008 | tf_op jit(solution)/shard_map/all_to_all | solution.py:16
  112.1 40.9 %all-to-all-done.7 = bf16[8,2,32,896]{3,2,1,0:T(8,128)(2,1)S(1)} async-done(((bf16[8,2,32,896]{3,2,1,0:T(8,128)(2,1)}), bf16[8,2,32,896]{3,2,1,0:T(8,128)(2,1)S(1)}, u32[]{:S(2)}, u32[]{:S(2)}) %all-to-all-start.7) | async-done | bytes 917536 | tf_op jit(solution)/shard_map/all_to_all | solution.py:16
  153.8 8.3 %all-to-all-start.5 = ((bf16[8,32,896]{2,1,0:T(8,128)(2,1)}), bf16[8,32,896]{2,1,0:T(8,128)(2,1)S(1)}, u32[]{:S(2)}, u32[]{:S(2)}) async-start(bf16[8,32,896]{2,1,0:T(8,128)(2,1)} %broadcast_in_dim.17), calls=%async_computation.5 | async-start | bytes 917504 | tf_op jit(solution)/shard_map/all_to_all | solution.py:16
  162.2 23.0 %all-to-all-done.5 = bf16[8,32,896]{2,1,0:T(8,128)(2,1)S(1)} async-done(((bf16[8,32,896]{2,1,0:T(8,128)(2,1)}), bf16[8,32,896]{2,1,0:T(8,128)(2,1)S(1)}, u32[]{:S(2)}, u32[]{:S(2)}) %all-to-all-start.5) | async-done | bytes 458784 | tf_op jit(solution)/shard_map/all_to_all | solution.py:16
  185.5 44.2 %all_to_all.59 = bf16[4,8,2,32,896]{4,3,1,2,0:T(8,128)(2,1)} all-to-all(bf16[4,8,2,32,896]{4,3,1,2,0:T(8,128)(2,1)S(1)} %broadcast_in_dim.20), channel_id=1, replica_groups={{0,128,256,384},{16,144,272,400},{32,160,288,416},{48,176,304,432},{64,..., dimensions={0} | all-to-all | bytes 7340032 | tf_op jit(solution)/shard_map/all_to_all | solution.py:16
  229.8 1.5 broadcast_in_dim.18
  231.2 3.6 %all-to-all-start.6 = ((bf16[4,8,32,896]{3,2,1,0:T(8,128)(2,1)}), bf16[4,8,32,896]{3,2,1,0:T(8,128)(2,1)S(1)}, u32[]{:S(2)}, u32[]{:S(2)}) async-start(bf16[4,8,32,896]{3,2,1,0:T(8,128)(2,1)} %broadcast_in_dim.18), calls=%async_computation.6 | async-start | bytes 3670016 | tf_op jit(solution)/shard_map/all_to_all | solution.py:16
  234.8 3.2 %fusion.25 = bf16[4,8,1,32,896]{4,3,1,2,0:T(8,128)(2,1)S(1)} fusion(bf16[4,8,2,32,896]{4,3,1,2,0:T(8,128)(2,1)} %all_to_all.59), kind=kLoop, calls=%fused_computation.33 | loop fusion | flops 7340032 | bytes 5505024 | tf_op jit(solution)/shard_map/convert_element_type | solution.py:57
  238.0 1.6 fusion.26
  240.4 2.3 slice_convert_fusion
  242.7 12.3 %all-to-all-done.6 = bf16[4,8,32,896]{3,2,1,0:T(8,128)(2,1)S(1)} async-done(((bf16[4,8,32,896]{3,2,1,0:T(8,128)(2,1)}), bf16[4,8,32,896]{3,2,1,0:T(8,128)(2,1)S(1)}, u32[]{:S(2)}, u32[]{:S(2)}) %all-to-all-start.6) | async-done | bytes 1835040 | tf_op jit(solution)/shard_map/all_to_all | solution.py:16
  255.0 3.6 %fusion.22 = (bf16[1024,896]{1,0:T(8,128)(2,1)S(1)}, bf16[1024,896]{1,0:T(8,128)(2,1)S(1)}) fusion(bf16[4,8,32,896]{3,2,1,0:T(8,128)(2,1)S(1)} %all-to-all-done.6, bf16[4,8,2,32,896]{4,3,1,2,0:T(8,128)(2,1)} %all_to_all.59, f32[4,8,1,32,896]{4,3,1,2,0:T(8,128)} %slice_convert_fusion), kind=kLoop, calls=%fused_computation.28 | loop fusion | flops 13762560 | bytes 11010048 | tf_op jit(solution)/shard_map/convert_element_type | solution.py:61
  260.3 8.4 %all_to_all.60 = f32[2,8,64,256]{3,2,1,0:T(8,128)S(1)} all-to-all(f32[2,8,64,256]{3,2,1,0:T(8,128)S(1)} %bitcast.99), channel_id=1, replica_groups={{0,1},{2,3},{4,5},{6,7},{8,9},{10,11},{12,13},{14,15},{16,17},{18,19},{..., dimensions={0} | all-to-all | bytes 2097152 | tf_op jit(solution)/shard_map/all_to_all | solution.py:16
  269.6 3.4 %all-to-all-start.10 = ((bf16[8,64,256]{2,1,0:T(8,128)(2,1)}), bf16[8,64,256]{2,1,0:T(8,128)(2,1)S(1)}, u32[]{:S(2)}, u32[]{:S(2)}) async-start(bf16[8,64,256]{2,1,0:T(8,128)(2,1)} %reduce_sum.47), calls=%async_computation.10 | async-start | bytes 524288 | tf_op jit(solution)/shard_map/all_to_all | solution.py:16
  273.0 3.5 %fusion.10 = (bf16[4,8,32,896]{3,2,1,0:T(8,128)(2,1)S(1)}, bf16[4,8,32,896]{3,2,1,0:T(8,128)(2,1)S(1)}) fusion(bf16[4,8,32,896]{3,2,1,0:T(8,128)(2,1)S(1)} %all-to-all-done.6, bf16[4,8,2,32,896]{4,3,1,2,0:T(8,128)(2,1)} %all_to_all.59), kind=kLoop, calls=%fused_computation.16 | loop fusion | flops 14680064 | bytes 9175040 | tf_op jit(solution)/shard_map/convert_element_type | solution.py:61
  276.5 1.7 fusion.27
  278.2 1.7 fusion.28
  279.8 15.5 %all-to-all-done.10 = bf16[8,64,256]{2,1,0:T(8,128)(2,1)S(1)} async-done(((bf16[8,64,256]{2,1,0:T(8,128)(2,1)}), bf16[8,64,256]{2,1,0:T(8,128)(2,1)S(1)}, u32[]{:S(2)}, u32[]{:S(2)}) %all-to-all-start.10) | async-done | bytes 262176 | tf_op jit(solution)/shard_map/all_to_all | solution.py:16
  (39 shorter events, 9.3 us)
Async XLA Ops:
  38.2 11.4 %copy-start.5 = (bf16[896,256]{1,0:T(8,128)(2,1)S(1)}, bf16[896,256]{1,0:T(8,128)(2,1)}, u32[]{:S(2)}) copy-start(bf16[896,256]{1,0:T(8,128)(2,1)} %param.13) | copy-start | bytes 1376260
  50.4 31.2 %copy-start.7 = (bf16[32,896]{1,0:T(8,128)(2,1)S(1)}, bf16[32,896]{1,0:T(8,128)(2,1)}, u32[]{:S(2)}) copy-start(bf16[32,896]{1,0:T(8,128)(2,1)} %param.10) | copy-start | bytes 172036
  50.4 31.2 %copy-start.8 = (bf16[32,896]{1,0:T(8,128)(2,1)S(1)}, bf16[32,896]{1,0:T(8,128)(2,1)}, u32[]{:S(2)}) copy-start(bf16[32,896]{1,0:T(8,128)(2,1)} %param.9) | copy-start | bytes 172036
  78.1 26.5 %all-to-all-start.4 = ((bf16[8,32,896]{2,1,0:T(8,128)(2,1)}), bf16[8,32,896]{2,1,0:T(8,128)(2,1)S(1)}, u32[]{:S(2)}, u32[]{:S(2)}) async-start(bf16[8,32,896]{2,1,0:T(8,128)(2,1)} %bitcast.6), calls=%async_computation.4 | async-start | bytes 917504 | tf_op jit(solution)/shard_map/all_to_all | solution.py:16
  105.6 47.4 %all-to-all-start.7 = ((bf16[8,2,32,896]{3,2,1,0:T(8,128)(2,1)}), bf16[8,2,32,896]{3,2,1,0:T(8,128)(2,1)S(1)}, u32[]{:S(2)}, u32[]{:S(2)}) async-start(bf16[8,2,32,896]{3,2,1,0:T(8,128)(2,1)} %broadcast_in_dim.19), calls=%async_computation.7 | async-start | bytes 1835008 | tf_op jit(solution)/shard_map/all_to_all | solution.py:16
  153.8 31.4 %all-to-all-start.5 = ((bf16[8,32,896]{2,1,0:T(8,128)(2,1)}), bf16[8,32,896]{2,1,0:T(8,128)(2,1)S(1)}, u32[]{:S(2)}, u32[]{:S(2)}) async-start(bf16[8,32,896]{2,1,0:T(8,128)(2,1)} %broadcast_in_dim.17), calls=%async_computation.5 | async-start | bytes 917504 | tf_op jit(solution)/shard_map/all_to_all | solution.py:16
  231.2 23.8 %all-to-all-start.6 = ((bf16[4,8,32,896]{3,2,1,0:T(8,128)(2,1)}), bf16[4,8,32,896]{3,2,1,0:T(8,128)(2,1)S(1)}, u32[]{:S(2)}, u32[]{:S(2)}) async-start(bf16[4,8,32,896]{3,2,1,0:T(8,128)(2,1)} %broadcast_in_dim.18), calls=%async_computation.6 | async-start | bytes 3670016 | tf_op jit(solution)/shard_map/all_to_all | solution.py:16
  234.8 3.2 %copy-start.6 = (bf16[896,256]{1,0:T(8,128)(2,1)S(1)}, bf16[896,256]{1,0:T(8,128)(2,1)}, u32[]{:S(2)}) copy-start(bf16[896,256]{1,0:T(8,128)(2,1)} %param.13) | copy-start | bytes 1376260
  238.0 2.4 copy-start
  242.7 16.0 %copy-start.3 = (bf16[256,896]{1,0:T(8,128)(2,1)S(1)}, bf16[256,896]{1,0:T(8,128)(2,1)}, u32[]{:S(2)}) copy-start(bf16[256,896]{1,0:T(8,128)(2,1)} %param.11) | copy-start | bytes 1376260
  242.7 16.8 %copy-start.1 = (bf16[256,896]{1,0:T(8,128)(2,1)S(1)}, bf16[256,896]{1,0:T(8,128)(2,1)}, u32[]{:S(2)}) copy-start(bf16[256,896]{1,0:T(8,128)(2,1)} %param.12) | copy-start | bytes 1376260
  269.6 25.7 %all-to-all-start.10 = ((bf16[8,64,256]{2,1,0:T(8,128)(2,1)}), bf16[8,64,256]{2,1,0:T(8,128)(2,1)S(1)}, u32[]{:S(2)}, u32[]{:S(2)}) async-start(bf16[8,64,256]{2,1,0:T(8,128)(2,1)} %reduce_sum.47), calls=%async_computation.10 | async-start | bytes 524288 | tf_op jit(solution)/shard_map/all_to_all | solution.py:16
  273.0 3.5 %copy-start.2 = (bf16[256,896]{1,0:T(8,128)(2,1)S(1)}, bf16[256,896]{1,0:T(8,128)(2,1)}, u32[]{:S(2)}) copy-start(bf16[256,896]{1,0:T(8,128)(2,1)} %param.12) | copy-start | bytes 1376260
  276.5 1.7 copy-start.4

commit v2 on v1

--- a/solution.py
+++ b/solution.py
@@ -6,10 +6,13 @@
 X, ZL, Y, ZH, C = 4, 8, 4, 2, 2
 X_GROUPS = [[x * ZL + z for x in range(X)] for z in range(ZL)]
 Z_GROUPS = [[x * ZL + z for z in range(ZL)] for x in range(X)]
-ZH_GROUPS = [[(y * ZH + h) * C + c for h in range(ZH)] for y in range(Y) for c in range(C)]
 Y_GROUPS = [[(y * ZH + h) * C + c for y in range(Y)] for h in range(ZH) for c in range(C)]
 C_GROUPS = [[(y * ZH + h) * C + c for c in range(C)] for y in range(Y) for h in range(ZH)]
 YZH_GROUPS = [[(y * ZH + h) * C + c for y in range(Y) for h in range(ZH)] for c in range(C)]
+ZH_SWAP = [(t, t ^ C) for t in range(Y * ZH * C)]
+C_SWAP = [(t, t ^ 1) for t in range(Y * ZH * C)]
+X_UP = [(x * ZL + z, (x + 1) % X * ZL + z) for x in range(X) for z in range(ZL)]
+X_DOWN = [(x * ZL + z, (x - 1) % X * ZL + z) for x in range(X) for z in range(ZL)]
 
 
 def exchange(blocks, axis, groups):
@@ -25,31 +28,66 @@
     return jnp.sum(exchange(blocks, axis, groups).astype(jnp.float32), axis=0)
 
 
+def pair(block, axis, perm, bit, dim):
+    other = lax.ppermute(block, axis, perm)
+    first = jnp.where(bit == 0, block, other)
+    second = jnp.where(bit == 0, other, block)
+    return jnp.stack([first, second], axis=dim)
+
+
 def on_device(tokens, out_grad, gate_pre, up_pre, gate_weight, up_weight, down_weight):
     rows, feats = out_grad.shape
     toks, hid = gate_pre.shape
     n = rows * Y * ZH * C
+    dp, tensor = lax.axis_index("dp"), lax.axis_index("tensor")
+    x, z = dp // ZL, dp % ZL
 
     both = jnp.stack([out_grad, tokens])
-    both = gather(both, "tensor", ZH_GROUPS)
-    both = gather(both, "tensor", Y_GROUPS)
-    both = gather(both, "tensor", C_GROUPS)
-    both = both.transpose(3, 1, 2, 0, 4, 5).reshape(2, n, feats)
+    both = pair(both, "tensor", ZH_SWAP, tensor // C % ZH, 0)
+
+    down_all = gather(down_weight, "dp", X_GROUPS)
+
+    both = lax.all_gather(both, "tensor", axis_index_groups=Y_GROUPS)
+    both = both.transpose(2, 0, 1, 3, 4).reshape(2, Y * ZH, rows, feats)
+    both = pair(both, "tensor", C_SWAP, tensor % C, 2)
+    both = both.reshape(2, n, feats)
     grads_all, tokens_all = both[0], both[1]
 
     saved = jnp.stack([gate_pre, up_pre])
-    saved = gather(saved, "dp", Z_GROUPS)
-    saved = gather(saved, "dp", X_GROUPS)
-    gate_all = saved[:, :, 0].reshape(n, hid)
-    up_all = saved[:, :, 1].reshape(n, hid)
+    for dim, reach in enumerate((4, 2, 1)):
+        swap = [(d, d ^ reach) for d in range(X * ZL)]
+        saved = pair(saved, "dp", swap, z // reach % 2, dim)
+    saved = saved.reshape(ZL, 2, toks, hid)
 
-    partial = jnp.einsum(
-        "nd,fd->nf", grads_all, down_weight, preferred_element_type=jnp.float32
+    ahead, down_all, saved = lax.optimization_barrier((grads_all, down_all, saved))
+    grads_x = exchange(ahead.reshape(X, n // X, feats), "dp", X_GROUPS)
+    partial = sum(
+        jnp.einsum("nd,fd->nf", grads_x[k], down_all[k], preferred_element_type=jnp.float32)
+        for k in range(X)
     ).astype(jnp.bfloat16)
-    hidden = add_up(partial.reshape(X, ZL * toks, hid), "dp", X_GROUPS).astype(jnp.bfloat16)
-    hidden = add_up(hidden.reshape(ZL, toks, hid), "dp", Z_GROUPS).astype(jnp.bfloat16)
+
+    from_down = lax.ppermute(saved, "dp", X_UP)
+    from_up = lax.ppermute(saved, "dp", X_DOWN)
+
+    hidden = add_up(partial.reshape(ZL, toks, hid), "dp", Z_GROUPS).astype(jnp.bfloat16)
+
+    far_low = lax.ppermute(from_down[: ZL // 2], "dp", X_UP)
+    far_high = lax.ppermute(from_up[ZL // 2 :], "dp", X_DOWN)
+
     hidden = gather(hidden, "dp", Z_GROUPS)
     hidden = gather(hidden, "dp", X_GROUPS).reshape(n, hid).astype(jnp.float32)
+
+    full = jnp.zeros((X,) + saved.shape, saved.dtype)
+    for block, start, half in (
+        (saved, x, 0),
+        (from_down, (x + X - 1) % X, 0),
+        (from_up, (x + 1) % X, 0),
+        (far_low, (x + 2) % X, 0),
+        (far_high, (x + 2) % X, ZL // 2),
+    ):
+        full = lax.dynamic_update_slice(full, block[None], (start, half, 0, 0, 0))
+    gate_all = full[:, :, 0].reshape(n, hid)
+    up_all = full[:, :, 1].reshape(n, hid)
 
     gate_float = gate_all.astype(jnp.float32)
     up_float = up_all.astype(jnp.float32)

time: 297 us -> 218 us (0.73)
  blocking collectives: 127 us -> 32.3 us
  starting transfers between devices: 25.2 us -> 72.1 us
  waiting for transfers between devices: 115 us -> 68.5 us
  local copies, waits for them, and re-layouts: 4.99 us -> 12.9 us
  other arithmetic: 16.1 us -> 21.7 us
    all_to_all x6 -> x2, blocking collectives: 127 us -> 20.1 us  [exchange(): lax.all_to_all(blocks, axis, 0, 0, axis_index_groups=groups, tiled=True)]
    all_to_all x5, waiting for transfers between devices: 115 us -> 50.1 us  [exchange(): lax.all_to_all(blocks, axis, 0, 0, axis_index_groups=groups, tiled=True)]
    ppermute x0 -> x9, starting transfers between devices: none -> 42.6 us  [the longest x5 29.6 us: pair(): other = lax.ppermute(block, axis, perm)]
    ppermute x0 -> x9, waiting for transfers between devices: none -> 18.5 us  [the longest x5 13.8 us: pair(): other = lax.ppermute(block, axis, perm)]
    all_gather x0 -> x1, blocking collectives: none -> 12.1 us  [on_device(): both = lax.all_gather(both, 'tensor', axis_index_groups=Y_GROUPS)]
    dynamic_update_slice x0 -> x5, local copies, waits for them, and re-layouts: none -> 4.7 us  [on_device(): full = lax.dynamic_update_slice(full, block[None], (start, half, 0, 0, 0))]
    all_to_all x5, starting transfers between devices: 25.2 us -> 29.6 us  [exchange(): lax.all_to_all(blocks, axis, 0, 0, axis_index_groups=groups, tiled=True)]
    convert_element_type x2 -> x1, other arithmetic: 7.13 us -> 3.49 us  [on_device(): up_grad = (hidden * gate_float * gate_sigmoid).astype(jnp.bfloat16)]
  transfers between devices with their start and end apart: 5 -> 14, of which waited for: 5 -> 7; matrix products, arithmetic and copies ran while one was open for 5% -> 15% of each run, Pallas kernels for 0% -> 0%
where the time goes in v2:
time: 218 us; the launch traced here: 217 us
  starting transfers between devices  72.1 us (33%)
  waiting for transfers between devices  68.5 us (31%)
  blocking collectives  32.3 us (15%)
  other arithmetic  21.7 us (10%)
  local copies, waits for them, and re-layouts  12.9 us (6%)
  matrix products  8.51 us (4%)
    all_to_all x5, waiting for transfers between devices, exchange(): lax.all_to_all(blocks, axis, 0, 0, axis_index_groups=groups, tiled=True)  50.1 us
    ppermute x5, starting transfers between devices, pair(): other = lax.ppermute(block, axis, perm)  29.6 us
    all_to_all x5, starting transfers between devices, exchange(): lax.all_to_all(blocks, axis, 0, 0, axis_index_groups=groups, tiled=True)  29.6 us
    all_to_all x2, blocking collectives, exchange(): lax.all_to_all(blocks, axis, 0, 0, axis_index_groups=groups, tiled=True)  20.1 us
    ppermute x5, waiting for transfers between devices, pair(): other = lax.ppermute(block, axis, perm)  13.8 us
    all_gather x1, blocking collectives, on_device(): both = lax.all_gather(both, 'tensor', axis_index_groups=Y_GROUPS)  12.1 us
    broadcast_in_dim x3, local copies, waits for them, and re-layouts, gather(): copies = jnp.broadcast_to(block[None], (len(groups[0]),) + block.shape)  5.69 us
    dynamic_update_slice x5, local copies, waits for them, and re-layouts, on_device(): full = lax.dynamic_update_slice(full, block[None], (start, half, 0, 0, 0))  4.7 us
  transfers between devices with their start and end apart: 14, of which 7 were waited for; matrix products, arithmetic and copies ran while one was open for 15% of the time, Pallas kernels for 0%

profile of v2, /device:TPU:33, one launch (start us, length us, event | category | flops | bytes accessed | tf_op | source)
XLA Modules:
  0.0 217.2 jit_solution(2069717296043990600)
XLA Ops:
  1.5 14.5 %collective-permute-start = (bf16[2,64,256]{2,1,0:T(8,128)(2,1)S(1)}, bf16[2,64,256]{2,1,0:T(8,128)(2,1)S(1)}, u32[]{:S(2)}, u32[]{:S(2)}) collective-permute-start(bf16[2,64,256]{2,1,0:T(8,128)(2,1)S(1)} %pad_maximum_fusion.6), channel_id=1, source_target_pairs={{0,2},{1,3},{2,0},{3,1},{4,6},{5,7},{6,4},{7,5},{8,10},{9,11},{10,... | collective-permute-start | bytes 196616 | tf_op jit(solution)/shard_map/ppermute | solution.py:32
  16.9 4.0 %collective-permute-start.2 = (bf16[2,32,896]{2,1,0:T(8,128)(2,1)S(1)}, bf16[2,32,896]{2,1,0:T(8,128)(2,1)S(1)}, u32[]{:S(2)}, u32[]{:S(2)}) collective-permute-start(bf16[2,32,896]{2,1,0:T(8,128)(2,1)S(1)} %pad_maximum_fusion.5), channel_id=1, source_target_pairs={{0,64},{16,80},{32,96},{48,112},{64,0},{80,16},{96,32},{112,48},{1... | collective-permute-start | bytes 344072 | tf_op jit(solution)/shard_map/ppermute | solution.py:32
  23.3 4.0 %all-to-all-start = ((bf16[4,896,256]{2,1,0:T(8,128)(2,1)}), bf16[4,896,256]{2,1,0:T(8,128)(2,1)S(1)}, u32[]{:S(2)}, u32[]{:S(2)}) async-start(bf16[4,896,256]{2,1,0:T(8,128)(2,1)} %broadcast_in_dim.36), calls=%async_computation | async-start | bytes 3670016 | tf_op jit(solution)/shard_map/all_to_all | solution.py:19
  27.4 4.8 %collective-permute-done.2 = bf16[2,32,896]{2,1,0:T(8,128)(2,1)S(1)} collective-permute-done((bf16[2,32,896]{2,1,0:T(8,128)(2,1)S(1)}, bf16[2,32,896]{2,1,0:T(8,128)(2,1)S(1)}, u32[]{:S(2)}, u32[]{:S(2)}) %collective-permute-start.2) | collective-permute-done | bytes 114720 | tf_op jit(solution)/shard_map/ppermute | solution.py:32
  34.8 12.1 %all-gather = bf16[8,2,64,256]{3,2,1,0:T(8,128)(2,1)S(1)} all-gather(bf16[2,2,64,256]{3,2,1,0:T(8,128)(2,1)S(1)} %pad_maximum_fusion.4), channel_id=2, replica_groups={{0,4,8,12},{1,5,9,13},{2,6,10,14},{3,7,11,15},{16,20,24,28},{17,21,25,2..., dimensions={0}, use_global_device_ids=true | all-gather | bytes 655360 | tf_op jit(solution)/shard_map/all_gather | solution.py:50
  47.0 4.1 %collective-permute-start.1 = (bf16[2,8,64,256]{3,2,1,0:T(8,128)(2,1)S(1)}, bf16[2,8,64,256]{3,2,1,0:T(8,128)(2,1)}, u32[]{:S(2)}, u32[]{:S(2)}) collective-permute-start(bf16[2,8,64,256]{3,2,1,0:T(8,128)(2,1)S(1)} %bitcast.162), channel_id=1, source_target_pairs={{0,1},{1,0},{2,3},{3,2},{4,5},{5,4},{6,7},{7,6},{8,9},{9,8},{10,11... | collective-permute-start | bytes 1572872 | tf_op jit(solution)/shard_map/ppermute | solution.py:32
  51.2 4.5 %collective-permute-start.4 = (bf16[2,2,2,32,896]{4,3,2,1,0:T(8,128)(2,1)S(1)}, bf16[2,2,2,32,896]{4,3,2,1,0:T(8,128)(2,1)}, u32[]{:S(2)}, u32[]{:S(2)}) collective-permute-start(bf16[2,2,2,32,896]{4,3,2,1,0:T(8,128)(2,1)S(1)} %pad_maximum_fusion.2), channel_id=1, source_target_pairs={{0,16},{16,0},{32,48},{48,32},{64,80},{80,64},{96,112},{112,96},{1... | collective-permute-start | bytes 1376264 | tf_op jit(solution)/shard_map/ppermute | solution.py:32
  57.8 8.9 %collective-permute-done.4 = bf16[2,2,2,32,896]{4,3,2,1,0:T(8,128)(2,1)} collective-permute-done((bf16[2,2,2,32,896]{4,3,2,1,0:T(8,128)(2,1)S(1)}, bf16[2,2,2,32,896]{4,3,2,1,0:T(8,128)(2,1)}, u32[]{:S(2)}, u32[]{:S(2)}) %collective-permute-start.4) | collective-permute-done | bytes 458784 | tf_op jit(solution)/shard_map/ppermute | solution.py:32
  67.9 12.6 %all_to_all.35 = bf16[4,256,256]{2,1,0:T(8,128)(2,1)S(1)} all-to-all(bf16[4,256,256]{2,1,0:T(8,128)(2,1)} %bitcast.165), channel_id=1, replica_groups={{0,128,256,384},{16,144,272,400},{32,160,288,416},{48,176,304,432},{64,..., dimensions={0} | all-to-all | bytes 1048576 | tf_op jit(solution)/shard_map/all_to_all | solution.py:19
  82.7 7.1 %all-to-all-start.2 = ((bf16[8,32,896]{2,1,0:T(8,128)(2,1)}), bf16[8,32,896]{2,1,0:T(8,128)(2,1)}, u32[]{:S(2)}, u32[]{:S(2)}) async-start(bf16[8,32,896]{2,1,0:T(8,128)(2,1)} %bitcast.167), calls=%async_computation.2 | async-start | bytes 917504 | tf_op jit(solution)/shard_map/all_to_all | solution.py:19
  91.9 4.3 %collective-permute-start.6 = (bf16[8,2,32,896]{3,2,1,0:T(8,128)(2,1)S(1)}, bf16[8,2,32,896]{3,2,1,0:T(8,128)(2,1)S(1)}, u32[]{:S(2)}, u32[]{:S(2)}) collective-permute-start(bf16[8,2,32,896]{3,2,1,0:T(8,128)(2,1)S(1)} %bitcast.160), channel_id=1, source_target_pairs={{0,384},{16,400},{32,416},{48,432},{64,448},{80,464},{96,480},{112... | collective-permute-start | bytes 2752520 | tf_op jit(solution)/shard_map/ppermute | solution.py:70
  96.2 16.7 %all-to-all-done.2 = bf16[8,32,896]{2,1,0:T(8,128)(2,1)} async-done(((bf16[8,32,896]{2,1,0:T(8,128)(2,1)}), bf16[8,32,896]{2,1,0:T(8,128)(2,1)}, u32[]{:S(2)}, u32[]{:S(2)}) %all-to-all-start.2) | async-done | bytes 458784 | tf_op jit(solution)/shard_map/all_to_all | solution.py:19
  114.8 6.4 %all-to-all-start.3 = ((bf16[8,32,896]{2,1,0:T(8,128)(2,1)}), bf16[8,32,896]{2,1,0:T(8,128)(2,1)}, u32[]{:S(2)}, u32[]{:S(2)}) async-start(bf16[8,32,896]{2,1,0:T(8,128)(2,1)} %broadcast_in_dim.37), calls=%async_computation.3 | async-start | bytes 917504 | tf_op jit(solution)/shard_map/all_to_all | solution.py:19
  126.8 4.3 %collective-permute-start.8 = (bf16[4,2,32,896]{3,2,1,0:T(8,128)(2,1)S(1)}, bf16[4,2,32,896]{3,2,1,0:T(8,128)(2,1)S(1)}, u32[]{:S(2)}, u32[]{:S(2)}) collective-permute-start(bf16[4,2,32,896]{3,2,1,0:T(8,128)(2,1)S(1)} %slice.65), channel_id=1, source_target_pairs={{0,384},{16,400},{32,416},{48,432},{64,448},{80,464},{96,480},{112... | collective-permute-start | bytes 1376264 | tf_op jit(solution)/shard_map/ppermute | solution.py:75
  133.2 4.7 %collective-permute-done.7 = bf16[4,2,32,896]{3,2,1,0:T(8,128)(2,1)S(1)} collective-permute-done((bf16[4,2,32,896]{3,2,1,0:T(8,128)(2,1)S(1)}, bf16[4,2,32,896]{3,2,1,0:T(8,128)(2,1)S(1)}, u32[]{:S(2)}, u32[]{:S(2)}) %collective-permute-start.7) | collective-permute-done | bytes 458784 | tf_op jit(solution)/shard_map/ppermute | solution.py:74
  138.7 5.7 %all-to-all-done.3 = bf16[8,32,896]{2,1,0:T(8,128)(2,1)} async-done(((bf16[8,32,896]{2,1,0:T(8,128)(2,1)}), bf16[8,32,896]{2,1,0:T(8,128)(2,1)}, u32[]{:S(2)}, u32[]{:S(2)}) %all-to-all-start.3) | async-done | bytes 458784 | tf_op jit(solution)/shard_map/all_to_all | solution.py:19
  146.9 3.6 %all-to-all-start.4 = ((bf16[4,8,32,896]{3,2,1,0:T(8,128)(2,1)}), bf16[4,8,32,896]{3,2,1,0:T(8,128)(2,1)S(1)}, u32[]{:S(2)}, u32[]{:S(2)}) async-start(bf16[4,8,32,896]{3,2,1,0:T(8,128)(2,1)} %broadcast_in_dim.38), calls=%async_computation.4 | async-start | bytes 3670016 | tf_op jit(solution)/shard_map/all_to_all | solution.py:19
  156.1 3.8 %slice_convert_fusion = f32[4,8,1,32,896]{4,3,2,1,0:T(8,128)} fusion(bf16[4,8,2,32,896]{4,3,2,1,0:T(8,128)(2,1)} %bitcast_dynamic-update-slice_fusion.3), kind=kLoop, calls=%fused_computation.34 | loop fusion | flops 917504 | bytes 5505024 | tf_op jit(solution)/shard_map/convert_element_type | solution.py:93
  159.9 11.7 %all-to-all-done.4 = bf16[4,8,32,896]{3,2,1,0:T(8,128)(2,1)S(1)} async-done(((bf16[4,8,32,896]{3,2,1,0:T(8,128)(2,1)}), bf16[4,8,32,896]{3,2,1,0:T(8,128)(2,1)S(1)}, u32[]{:S(2)}, u32[]{:S(2)}) %all-to-all-start.4) | async-done | bytes 1835040 | tf_op jit(solution)/shard_map/all_to_all | solution.py:19
  171.6 3.6 %fusion.20 = (bf16[1024,896]{1,0:T(8,128)(2,1)S(1)}, bf16[1024,896]{1,0:T(8,128)(2,1)S(1)}) fusion(f32[4,8,1,32,896]{4,3,2,1,0:T(8,128)} %slice_convert_fusion, bf16[4,8,32,896]{3,2,1,0:T(8,128)(2,1)S(1)} %all-to-all-done.4, bf16[4,8,2,32,896]{4,3,2,1,0:T(8,128)(2,1)} %bitcast_dynamic-update-slice_fusion.3), kind=kLoop, calls=%fused_computation.26 | loop fusion | flops 13762560 | bytes 11010048 | tf_op jit(solution)/shard_map/convert_element_type | solution.py:98
  176.8 7.5 %all_to_all.36 = f32[2,8,64,256]{3,2,1,0:T(8,128)S(1)} all-to-all(f32[2,8,64,256]{3,2,1,0:T(8,128)S(1)} %bitcast.157), channel_id=1, replica_groups={{0,1},{2,3},{4,5},{6,7},{8,9},{10,11},{12,13},{14,15},{16,17},{18,19},{..., dimensions={0} | all-to-all | bytes 2097152 | tf_op jit(solution)/shard_map/all_to_all | solution.py:19
  185.1 8.5 %all-to-all-start.6 = ((bf16[8,64,256]{2,1,0:T(8,128)(2,1)}), bf16[8,64,256]{2,1,0:T(8,128)(2,1)S(1)}, u32[]{:S(2)}, u32[]{:S(2)}) async-start(bf16[8,64,256]{2,1,0:T(8,128)(2,1)} %reduce_sum.34), calls=%async_computation.6 | async-start | bytes 524288 | tf_op jit(solution)/shard_map/all_to_all | solution.py:19
  193.6 3.5 %fusion.10 = (bf16[4,8,32,896]{3,2,1,0:T(8,128)(2,1)S(1)}, bf16[4,8,32,896]{3,2,1,0:T(8,128)(2,1)S(1)}) fusion(bf16[4,8,32,896]{3,2,1,0:T(8,128)(2,1)S(1)} %all-to-all-done.4, bf16[4,8,2,32,896]{4,3,2,1,0:T(8,128)(2,1)} %bitcast_dynamic-update-slice_fusion.3), kind=kLoop, calls=%fused_computation.16 | loop fusion | flops 14680064 | bytes 9175040 | tf_op jit(solution)/shard_map/convert_element_type | solution.py:99
  200.5 16.0 %all-to-all-done.6 = bf16[8,64,256]{2,1,0:T(8,128)(2,1)S(1)} async-done(((bf16[8,64,256]{2,1,0:T(8,128)(2,1)}), bf16[8,64,256]{2,1,0:T(8,128)(2,1)S(1)}, u32[]{:S(2)}, u32[]{:S(2)}) %all-to-all-start.6) | async-done | bytes 262176 | tf_op jit(solution)/shard_map/all_to_all | solution.py:19
  (68 shorter events, 39.1 us)
Async XLA Ops:
  0.6 26.7 %copy-start.9 = (bf16[64,256]{1,0:T(8,128)(2,1)S(1)}, bf16[64,256]{1,0:T(8,128)(2,1)}, u32[]{:S(2)}) copy-start(bf16[64,256]{1,0:T(8,128)(2,1)} %param.8) | copy-start | bytes 98308
  0.6 26.7 %copy-start.8 = (bf16[64,256]{1,0:T(8,128)(2,1)S(1)}, bf16[64,256]{1,0:T(8,128)(2,1)}, u32[]{:S(2)}) copy-start(bf16[64,256]{1,0:T(8,128)(2,1)} %param.7) | copy-start | bytes 98308
  0.7 31.6 %copy-start.7 = (bf16[32,896]{1,0:T(8,128)(2,1)S(1)}, bf16[32,896]{1,0:T(8,128)(2,1)}, u32[]{:S(2)}) copy-start(bf16[32,896]{1,0:T(8,128)(2,1)} %param.9) | copy-start | bytes 172036
  0.7 31.6 %copy-start.6 = (bf16[32,896]{1,0:T(8,128)(2,1)S(1)}, bf16[32,896]{1,0:T(8,128)(2,1)}, u32[]{:S(2)}) copy-start(bf16[32,896]{1,0:T(8,128)(2,1)} %param.10) | copy-start | bytes 172036
  1.5 25.8 %collective-permute-start = (bf16[2,64,256]{2,1,0:T(8,128)(2,1)S(1)}, bf16[2,64,256]{2,1,0:T(8,128)(2,1)S(1)}, u32[]{:S(2)}, u32[]{:S(2)}) collective-permute-start(bf16[2,64,256]{2,1,0:T(8,128)(2,1)S(1)} %pad_maximum_fusion.6), channel_id=1, source_target_pairs={{0,2},{1,3},{2,0},{3,1},{4,6},{5,7},{6,4},{7,5},{8,10},{9,11},{10,... | collective-permute-start | bytes 196616 | tf_op jit(solution)/shard_map/ppermute | solution.py:32
  16.9 15.3 %collective-permute-start.2 = (bf16[2,32,896]{2,1,0:T(8,128)(2,1)S(1)}, bf16[2,32,896]{2,1,0:T(8,128)(2,1)S(1)}, u32[]{:S(2)}, u32[]{:S(2)}) collective-permute-start(bf16[2,32,896]{2,1,0:T(8,128)(2,1)S(1)} %pad_maximum_fusion.5), channel_id=1, source_target_pairs={{0,64},{16,80},{32,96},{48,112},{64,0},{80,16},{96,32},{112,48},{1... | collective-permute-start | bytes 344072 | tf_op jit(solution)/shard_map/ppermute | solution.py:32
  23.3 44.6 %all-to-all-start = ((bf16[4,896,256]{2,1,0:T(8,128)(2,1)}), bf16[4,896,256]{2,1,0:T(8,128)(2,1)S(1)}, u32[]{:S(2)}, u32[]{:S(2)}) async-start(bf16[4,896,256]{2,1,0:T(8,128)(2,1)} %broadcast_in_dim.36), calls=%async_computation | async-start | bytes 3670016 | tf_op jit(solution)/shard_map/all_to_all | solution.py:19
  32.3 18.8 %collective-permute-start.3 = (bf16[2,2,32,896]{3,2,1,0:T(8,128)(2,1)S(1)}, bf16[2,2,32,896]{3,2,1,0:T(8,128)(2,1)S(1)}, u32[]{:S(2)}, u32[]{:S(2)}) collective-permute-start(bf16[2,2,32,896]{3,2,1,0:T(8,128)(2,1)S(1)} %pad_maximum_fusion.3), channel_id=1, source_target_pairs={{0,32},{16,48},{32,0},{48,16},{64,96},{80,112},{96,64},{112,80},{1... | collective-permute-start | bytes 688136 | tf_op jit(solution)/shard_map/ppermute | solution.py:32
  47.0 8.8 %collective-permute-start.1 = (bf16[2,8,64,256]{3,2,1,0:T(8,128)(2,1)S(1)}, bf16[2,8,64,256]{3,2,1,0:T(8,128)(2,1)}, u32[]{:S(2)}, u32[]{:S(2)}) collective-permute-start(bf16[2,8,64,256]{3,2,1,0:T(8,128)(2,1)S(1)} %bitcast.162), channel_id=1, source_target_pairs={{0,1},{1,0},{2,3},{3,2},{4,5},{5,4},{6,7},{7,6},{8,9},{9,8},{10,11... | collective-permute-start | bytes 1572872 | tf_op jit(solution)/shard_map/ppermute | solution.py:32
  51.2 15.5 %collective-permute-start.4 = (bf16[2,2,2,32,896]{4,3,2,1,0:T(8,128)(2,1)S(1)}, bf16[2,2,2,32,896]{4,3,2,1,0:T(8,128)(2,1)}, u32[]{:S(2)}, u32[]{:S(2)}) collective-permute-start(bf16[2,2,2,32,896]{4,3,2,1,0:T(8,128)(2,1)S(1)} %pad_maximum_fusion.2), channel_id=1, source_target_pairs={{0,16},{16,0},{32,48},{48,32},{64,80},{80,64},{96,112},{112,96},{1... | collective-permute-start | bytes 1376264 | tf_op jit(solution)/shard_map/ppermute | solution.py:32
  82.7 30.2 %all-to-all-start.2 = ((bf16[8,32,896]{2,1,0:T(8,128)(2,1)}), bf16[8,32,896]{2,1,0:T(8,128)(2,1)}, u32[]{:S(2)}, u32[]{:S(2)}) async-start(bf16[8,32,896]{2,1,0:T(8,128)(2,1)} %bitcast.167), calls=%async_computation.2 | async-start | bytes 917504 | tf_op jit(solution)/shard_map/all_to_all | solution.py:19
  89.7 34.8 %collective-permute-start.5 = (bf16[8,2,32,896]{3,2,1,0:T(8,128)(2,1)S(1)}, bf16[8,2,32,896]{3,2,1,0:T(8,128)(2,1)S(1)}, u32[]{:S(2)}, u32[]{:S(2)}) collective-permute-start(bf16[8,2,32,896]{3,2,1,0:T(8,128)(2,1)S(1)} %bitcast.159), channel_id=1, source_target_pairs={{0,128},{16,144},{32,160},{48,176},{64,192},{80,208},{96,224},{112... | collective-permute-start | bytes 2752520 | tf_op jit(solution)/shard_map/ppermute | solution.py:69
  91.9 34.8 %collective-permute-start.6 = (bf16[8,2,32,896]{3,2,1,0:T(8,128)(2,1)S(1)}, bf16[8,2,32,896]{3,2,1,0:T(8,128)(2,1)S(1)}, u32[]{:S(2)}, u32[]{:S(2)}) collective-permute-start(bf16[8,2,32,896]{3,2,1,0:T(8,128)(2,1)S(1)} %bitcast.160), channel_id=1, source_target_pairs={{0,384},{16,400},{32,416},{48,432},{64,448},{80,464},{96,480},{112... | collective-permute-start | bytes 2752520 | tf_op jit(solution)/shard_map/ppermute | solution.py:70
  114.8 29.6 %all-to-all-start.3 = ((bf16[8,32,896]{2,1,0:T(8,128)(2,1)}), bf16[8,32,896]{2,1,0:T(8,128)(2,1)}, u32[]{:S(2)}, u32[]{:S(2)}) async-start(bf16[8,32,896]{2,1,0:T(8,128)(2,1)} %broadcast_in_dim.37), calls=%async_computation.3 | async-start | bytes 917504 | tf_op jit(solution)/shard_map/all_to_all | solution.py:19
  124.6 13.3 %collective-permute-start.7 = (bf16[4,2,32,896]{3,2,1,0:T(8,128)(2,1)S(1)}, bf16[4,2,32,896]{3,2,1,0:T(8,128)(2,1)S(1)}, u32[]{:S(2)}, u32[]{:S(2)}) collective-permute-start(bf16[4,2,32,896]{3,2,1,0:T(8,128)(2,1)S(1)} %slice.64), channel_id=1, source_target_pairs={{0,128},{16,144},{32,160},{48,176},{64,192},{80,208},{96,224},{112... | collective-permute-start | bytes 1376264 | tf_op jit(solution)/shard_map/ppermute | solution.py:74
  126.8 23.7 %collective-permute-start.8 = (bf16[4,2,32,896]{3,2,1,0:T(8,128)(2,1)S(1)}, bf16[4,2,32,896]{3,2,1,0:T(8,128)(2,1)S(1)}, u32[]{:S(2)}, u32[]{:S(2)}) collective-permute-start(bf16[4,2,32,896]{3,2,1,0:T(8,128)(2,1)S(1)} %slice.65), channel_id=1, source_target_pairs={{0,384},{16,400},{32,416},{48,432},{64,448},{80,464},{96,480},{112... | collective-permute-start | bytes 1376264 | tf_op jit(solution)/shard_map/ppermute | solution.py:75
  146.9 24.7 %all-to-all-start.4 = ((bf16[4,8,32,896]{3,2,1,0:T(8,128)(2,1)}), bf16[4,8,32,896]{3,2,1,0:T(8,128)(2,1)S(1)}, u32[]{:S(2)}, u32[]{:S(2)}) async-start(bf16[4,8,32,896]{3,2,1,0:T(8,128)(2,1)} %broadcast_in_dim.38), calls=%async_computation.4 | async-start | bytes 3670016 | tf_op jit(solution)/shard_map/all_to_all | solution.py:19
  150.5 4.0 %copy-start = (bf16[1,8,2,64,256]{4,3,2,1,0:T(8,128)(2,1)S(1)}, bf16[1,8,2,64,256]{4,3,2,1,0:T(8,128)(2,1)}, u32[]{:S(2)}) copy-start(bf16[1,8,2,64,256]{4,3,2,1,0:T(8,128)(2,1)} %get-tuple-element.14) | copy-start | bytes 1572868
  150.5 4.0 %copy-start.5 = (bf16[896,256]{1,0:T(8,128)(2,1)S(1)}, bf16[896,256]{1,0:T(8,128)(2,1)}, u32[]{:S(2)}) copy-start(bf16[896,256]{1,0:T(8,128)(2,1)} %param.13) | copy-start | bytes 1376260
  159.9 15.3 %copy-start.3 = (bf16[256,896]{1,0:T(8,128)(2,1)S(1)}, bf16[256,896]{1,0:T(8,128)(2,1)}, u32[]{:S(2)}) copy-start(bf16[256,896]{1,0:T(8,128)(2,1)} %param.12) | copy-start | bytes 1376260
  159.9 16.0 %copy-start.1 = (bf16[256,896]{1,0:T(8,128)(2,1)S(1)}, bf16[256,896]{1,0:T(8,128)(2,1)}, u32[]{:S(2)}) copy-start(bf16[256,896]{1,0:T(8,128)(2,1)} %param.11) | copy-start | bytes 1376260
  185.1 31.4 %all-to-all-start.6 = ((bf16[8,64,256]{2,1,0:T(8,128)(2,1)}), bf16[8,64,256]{2,1,0:T(8,128)(2,1)S(1)}, u32[]{:S(2)}, u32[]{:S(2)}) async-start(bf16[8,64,256]{2,1,0:T(8,128)(2,1)} %reduce_sum.34), calls=%async_computation.6 | async-start | bytes 524288 | tf_op jit(solution)/shard_map/all_to_all | solution.py:19
  193.6 3.5 %copy-start.4 = (bf16[256,896]{1,0:T(8,128)(2,1)S(1)}, bf16[256,896]{1,0:T(8,128)(2,1)}, u32[]{:S(2)}) copy-start(bf16[256,896]{1,0:T(8,128)(2,1)} %param.12) | copy-start | bytes 1376260
  197.1 1.7 copy-start.2

commit v3 on v2

--- a/solution.py
+++ b/solution.py
@@ -6,9 +6,12 @@
 X, ZL, Y, ZH, C = 4, 8, 4, 2, 2
 X_GROUPS = [[x * ZL + z for x in range(X)] for z in range(ZL)]
 Z_GROUPS = [[x * ZL + z for z in range(ZL)] for x in range(X)]
+Z_BY_CORE = [
+    [x * ZL + (h * C + c) * 2 + k for c in range(C) for h in range(ZH) for k in range(2)]
+    for x in range(X)
+]
 Y_GROUPS = [[(y * ZH + h) * C + c for y in range(Y)] for h in range(ZH) for c in range(C)]
 C_GROUPS = [[(y * ZH + h) * C + c for c in range(C)] for y in range(Y) for h in range(ZH)]
-YZH_GROUPS = [[(y * ZH + h) * C + c for y in range(Y) for h in range(ZH)] for c in range(C)]
 ZH_SWAP = [(t, t ^ C) for t in range(Y * ZH * C)]
 C_SWAP = [(t, t ^ 1) for t in range(Y * ZH * C)]
 X_UP = [(x * ZL + z, (x + 1) % X * ZL + z) for x in range(X) for z in range(ZL)]
@@ -43,33 +46,45 @@
     x, z = dp // ZL, dp % ZL
 
     both = jnp.stack([out_grad, tokens])
-    both = pair(both, "tensor", ZH_SWAP, tensor // C % ZH, 0)
+    both = pair(both, "tensor", ZH_SWAP, tensor // C % ZH, 1)
+    grads_y = lax.all_gather(both[0], "tensor", axis_index_groups=Y_GROUPS)
 
     down_all = gather(down_weight, "dp", X_GROUPS)
 
-    both = lax.all_gather(both, "tensor", axis_index_groups=Y_GROUPS)
-    both = both.transpose(2, 0, 1, 3, 4).reshape(2, Y * ZH, rows, feats)
+    saved = jnp.stack([gate_pre, up_pre])
+    for dim, reach in enumerate((4, 2, 1)):
+        swap = [(d, d ^ reach) for d in range(X * ZL)]
+        if reach == 2:
+            saved, grads_y = lax.optimization_barrier((saved, grads_y))
+        if reach == 1:
+            saved, down_all, ahead = lax.optimization_barrier((saved, down_all, grads_y))
+        saved = pair(saved, "dp", swap, z // reach % 2, dim)
+    saved = saved.reshape(ZL, 2, toks, hid)
+
+    grads_x = exchange(ahead, "dp", X_GROUPS)
+    grads_x = lax.all_gather(grads_x, "tensor", axis_index_groups=C_GROUPS)
+    grads_x, saved = lax.optimization_barrier((grads_x, saved))
+    partial = sum(
+        jnp.einsum(
+            "nd,fd->nf",
+            grads_x[:, k].reshape(n // X, feats),
+            down_all[k],
+            preferred_element_type=jnp.float32,
+        )
+        for k in range(X)
+    ).astype(jnp.bfloat16)
+
+    inputs, _ = lax.optimization_barrier((both[1], partial))
+    tokens_y = lax.all_gather(inputs, "tensor", axis_index_groups=Y_GROUPS)
+    both = jnp.stack([grads_y, tokens_y]).reshape(2, Y * ZH, rows, feats)
     both = pair(both, "tensor", C_SWAP, tensor % C, 2)
     both = both.reshape(2, n, feats)
     grads_all, tokens_all = both[0], both[1]
 
-    saved = jnp.stack([gate_pre, up_pre])
-    for dim, reach in enumerate((4, 2, 1)):
-        swap = [(d, d ^ reach) for d in range(X * ZL)]
-        saved = pair(saved, "dp", swap, z // reach % 2, dim)
-    saved = saved.reshape(ZL, 2, toks, hid)
-
-    ahead, down_all, saved = lax.optimization_barrier((grads_all, down_all, saved))
-    grads_x = exchange(ahead.reshape(X, n // X, feats), "dp", X_GROUPS)
-    partial = sum(
-        jnp.einsum("nd,fd->nf", grads_x[k], down_all[k], preferred_element_type=jnp.float32)
-        for k in range(X)
-    ).astype(jnp.bfloat16)
-
     from_down = lax.ppermute(saved, "dp", X_UP)
     from_up = lax.ppermute(saved, "dp", X_DOWN)
 
-    hidden = add_up(partial.reshape(ZL, toks, hid), "dp", Z_GROUPS).astype(jnp.bfloat16)
+    hidden = add_up(partial.reshape(ZL, toks, hid), "dp", Z_BY_CORE).astype(jnp.bfloat16)
 
     far_low = lax.ppermute(from_down[: ZL // 2], "dp", X_UP)
     far_high = lax.ppermute(from_up[ZL // 2 :], "dp", X_DOWN)
@@ -103,7 +118,11 @@
     ) + jnp.einsum("nf,df->nd", up_grad, up_weight, preferred_element_type=jnp.float32)
     partial_in = partial_in.reshape(Y * ZH, C, rows, feats).transpose(1, 0, 2, 3)
     partial_in = add_up(partial_in, "tensor", C_GROUPS).astype(jnp.bfloat16)
-    input_grad = add_up(partial_in, "tensor", YZH_GROUPS).astype(jnp.bfloat16)
+    partial_in = add_up(partial_in.reshape(Y, ZH, rows, feats), "tensor", Y_GROUPS)
+    upper = tensor // C % ZH == 1
+    sent = jnp.where(upper, partial_in[0], partial_in[1])
+    kept = jnp.where(upper, partial_in[1], partial_in[0])
+    input_grad = (kept + lax.ppermute(sent, "tensor", ZH_SWAP)).astype(jnp.bfloat16)
 
     down_sum = jnp.einsum("nf,nd->fd", active, grads_all, preferred_element_type=jnp.float32)
     gate_sum = jnp.einsum("nd,nf->df", tokens_all, gate_grad, preferred_element_type=jnp.float32)

time: 218 us -> 205 us (0.940); the launches traced: 217 us -> 201 us
  waiting for transfers between devices: 68.5 us -> 41.5 us
  starting transfers between devices: 72.1 us -> 77.3 us
  local copies, waits for them, and re-layouts: 12.9 us -> 16.3 us
    all_to_all x5 -> x6, waiting for transfers between devices: 50.1 us -> 17.9 us  [exchange(): lax.all_to_all(blocks, axis, 0, 0, axis_index_groups=groups, tiled=True)]
    all_gather x1 -> x3, blocking collectives: 12.1 us -> 27.3 us  [the longest x1 11.3 us: on_device(): grads_y = lax.all_gather(both[0], 'tensor', axis_index_groups=Y_GROUPS)]
    all_to_all x2 -> x1, blocking collectives: 20.1 us -> 6.81 us  [exchange(): lax.all_to_all(blocks, axis, 0, 0, axis_index_groups=groups, tiled=True)]
    ppermute x0 -> x1, waiting for transfers between devices: none -> 9.45 us  [on_device(): lax.ppermute(sent, 'tensor', ZH_SWAP)]
    ppermute x5, waiting for transfers between devices: 13.8 us -> 8.48 us  [pair(): other = lax.ppermute(block, axis, perm)]
    ppermute x1, waiting for transfers between devices: 0.01 us -> 3.24 us  [on_device(): from_down = lax.ppermute(saved, 'dp', X_UP)]
    ppermute x0 -> x1, starting transfers between devices: none -> 2.68 us  [on_device(): lax.ppermute(sent, 'tensor', ZH_SWAP)]
    dynamic_update_slice x5, local copies, waits for them, and re-layouts: 4.7 us -> 7.05 us  [on_device(): full = lax.dynamic_update_slice(full, block[None], (start, half, 0, 0, 0))]
  transfers between devices with their start and end apart: 14 -> 16, of which waited for: 7 -> 6; matrix products, arithmetic and copies ran while one was open for 15% -> 18% of each run, Pallas kernels for 0% -> 0%
where the time goes in v3:
time: 205 us; the launch traced here: 201 us
  starting transfers between devices  77.3 us (38%)
  waiting for transfers between devices  41.5 us (20%)
  blocking collectives  34.1 us (17%)
  other arithmetic  22.1 us (11%)
  local copies, waits for them, and re-layouts  16.3 us (8%)
  matrix products  8.5 us (4%)
    ppermute x5, starting transfers between devices, pair(): other = lax.ppermute(block, axis, perm)  31.3 us
    all_to_all x6, starting transfers between devices, exchange(): lax.all_to_all(blocks, axis, 0, 0, axis_index_groups=groups, tiled=True)  30.4 us
    all_to_all x6, waiting for transfers between devices, exchange(): lax.all_to_all(blocks, axis, 0, 0, axis_index_groups=groups, tiled=True)  17.9 us
    all_gather x1, blocking collectives, on_device(): grads_y = lax.all_gather(both[0], 'tensor', axis_index_groups=Y_GROUPS)  11.3 us
    all_gather x1, blocking collectives, on_device(): tokens_y = lax.all_gather(inputs, 'tensor', axis_index_groups=Y_GROUPS)  10.2 us
    ppermute x1, waiting for transfers between devices, on_device(): lax.ppermute(sent, 'tensor', ZH_SWAP)  9.45 us
    ppermute x5, waiting for transfers between devices, pair(): other = lax.ppermute(block, axis, perm)  8.48 us
    dynamic_update_slice x5, local copies, waits for them, and re-layouts, on_device(): full = lax.dynamic_update_slice(full, block[None], (start, half, 0, 0, 0))  7.05 us
  transfers between devices with their start and end apart: 16, of which 6 were waited for; matrix products, arithmetic and copies ran while one was open for 18% of the time, Pallas kernels for 0%

profile of v3, /device:TPU:33, one launch (start us, length us, event | category | flops | bytes accessed | tf_op | source)
XLA Modules:
  0.0 201.0 jit_solution(14956288456918506189)
XLA Ops:
  1.5 14.5 %collective-permute-start.1 = (bf16[2,64,256]{2,1,0:T(8,128)(2,1)S(1)}, bf16[2,64,256]{2,1,0:T(8,128)(2,1)S(1)}, u32[]{:S(2)}, u32[]{:S(2)}) collective-permute-start(bf16[2,64,256]{2,1,0:T(8,128)(2,1)S(1)} %pad_maximum_fusion.7), channel_id=1, source_target_pairs={{0,2},{1,3},{2,0},{3,1},{4,6},{5,7},{6,4},{7,5},{8,10},{9,11},{10,... | collective-permute-start | bytes 196616 | tf_op jit(solution)/shard_map/ppermute | solution.py:35
  16.9 4.0 %collective-permute-start = (bf16[2,32,896]{2,1,0:T(8,128)(2,1)S(1)}, bf16[2,32,896]{2,1,0:T(8,128)(2,1)S(1)}, u32[]{:S(2)}, u32[]{:S(2)}) collective-permute-start(bf16[2,32,896]{2,1,0:T(8,128)(2,1)S(1)} %pad_maximum_fusion.5), channel_id=1, source_target_pairs={{0,64},{16,80},{32,96},{48,112},{64,0},{80,16},{96,32},{112,48},{1... | collective-permute-start | bytes 344072 | tf_op jit(solution)/shard_map/ppermute | solution.py:35
  23.3 4.0 %all-to-all-start = ((bf16[4,896,256]{2,1,0:T(8,128)(2,1)}), bf16[4,896,256]{2,1,0:T(8,128)(2,1)S(1)}, u32[]{:S(2)}, u32[]{:S(2)}) async-start(bf16[4,896,256]{2,1,0:T(8,128)(2,1)} %broadcast_in_dim.36), calls=%async_computation | async-start | bytes 3670016 | tf_op jit(solution)/shard_map/all_to_all | solution.py:22
  28.0 11.3 %all_gather.15 = bf16[4,2,64,256]{3,2,1,0:T(8,128)(2,1)} all-gather(bf16[1,2,64,256]{3,2,1,0:T(8,128)(2,1)S(1)} %get-tuple-element.38), channel_id=1, replica_groups={{0,4,8,12},{1,5,9,13},{2,6,10,14},{3,7,11,15},{16,20,24,28},{17,21,25,2..., dimensions={0}, use_global_device_ids=true | all-gather | bytes 327680 | tf_op jit(solution)/shard_map/all_gather | solution.py:50
  42.5 8.5 %collective-permute-done.2 = bf16[2,2,32,896]{3,2,1,0:T(8,128)(2,1)S(1)} collective-permute-done((bf16[2,2,32,896]{3,2,1,0:T(8,128)(2,1)S(1)}, bf16[2,2,32,896]{3,2,1,0:T(8,128)(2,1)S(1)}, u32[]{:S(2)}, u32[]{:S(2)}) %collective-permute-start.2) | collective-permute-done | bytes 229408 | tf_op jit(solution)/shard_map/ppermute | solution.py:35
  51.1 4.7 %collective-permute-start.3 = (bf16[2,2,2,32,896]{4,3,2,1,0:T(8,128)(2,1)S(1)}, bf16[2,2,2,32,896]{4,3,2,1,0:T(8,128)(2,1)S(1)}, u32[]{:S(2)}, u32[]{:S(2)}) collective-permute-start(bf16[2,2,2,32,896]{4,3,2,1,0:T(8,128)(2,1)S(1)} %pad_maximum_fusion.3), channel_id=1, source_target_pairs={{0,16},{16,0},{32,48},{48,32},{64,80},{80,64},{96,112},{112,96},{1... | collective-permute-start | bytes 1376264 | tf_op jit(solution)/shard_map/ppermute | solution.py:35
  55.9 3.7 %all-to-all-start.1 = ((bf16[4,2,64,256]{3,2,1,0:T(8,128)(2,1)}), bf16[4,2,64,256]{3,2,1,0:T(8,128)(2,1)S(1)}, u32[]{:S(2)}, u32[]{:S(2)}) async-start(bf16[4,2,64,256]{3,2,1,0:T(8,128)(2,1)} %all_gather.15), calls=%async_computation.1 | async-start | bytes 524288 | tf_op jit(solution)/shard_map/all_to_all | solution.py:22
  59.6 5.5 %all-to-all-done.1 = bf16[4,2,64,256]{3,2,1,0:T(8,128)(2,1)S(1)} async-done(((bf16[4,2,64,256]{3,2,1,0:T(8,128)(2,1)}), bf16[4,2,64,256]{3,2,1,0:T(8,128)(2,1)S(1)}, u32[]{:S(2)}, u32[]{:S(2)}) %all-to-all-start.1) | async-done | bytes 262176 | tf_op jit(solution)/shard_map/all_to_all | solution.py:22
  65.1 5.9 %all-gather = bf16[8,2,64,256]{3,2,1,0:T(8,128)(2,1)S(1)} all-gather(bf16[4,2,64,256]{3,2,1,0:T(8,128)(2,1)S(1)} %all-to-all-done.1), channel_id=2, replica_groups={{0,1},{2,3},{4,5},{6,7},{8,9},{10,11},{12,13},{14,15},{16,17},{18,19},{..., dimensions={0}, use_global_device_ids=true | all-gather | bytes 786432 | tf_op jit(solution)/shard_map/all_gather | solution.py:65
  73.3 6.2 %all-to-all-start.2 = ((bf16[8,32,896]{2,1,0:T(8,128)(2,1)}), bf16[8,32,896]{2,1,0:T(8,128)(2,1)S(1)}, u32[]{:S(2)}, u32[]{:S(2)}) async-start(bf16[8,32,896]{2,1,0:T(8,128)(2,1)} %bitcast.32), calls=%async_computation.2 | async-start | bytes 917504 | tf_op jit(solution)/shard_map/all_to_all | solution.py:22
  79.5 10.2 %all-gather.1 = bf16[8,64,256]{2,1,0:T(8,128)(2,1)S(1)} all-gather(bf16[2,64,256]{2,1,0:T(8,128)(2,1)S(1)} %copy-done.7), channel_id=3, replica_groups={{0,4,8,12},{1,5,9,13},{2,6,10,14},{3,7,11,15},{16,20,24,28},{17,21,25,2..., dimensions={0}, use_global_device_ids=true | all-gather | bytes 327680 | tf_op jit(solution)/shard_map/all_gather | solution.py:78
  90.7 4.9 %collective-permute-start.4 = (bf16[2,8,64,256]{3,2,1,0:T(8,128)(2,1)S(1)}, bf16[2,8,64,256]{3,2,1,0:T(8,128)(2,1)S(1)}, u32[]{:S(2)}, u32[]{:S(2)}) collective-permute-start(bf16[2,8,64,256]{3,2,1,0:T(8,128)(2,1)S(1)} %pad_maximum_fusion.2), channel_id=1, source_target_pairs={{0,1},{1,0},{2,3},{3,2},{4,5},{5,4},{6,7},{7,6},{8,9},{9,8},{10,11... | collective-permute-start | bytes 1572872 | tf_op jit(solution)/shard_map/ppermute | solution.py:35
  97.8 4.3 %collective-permute-start.6 = (bf16[8,2,32,896]{3,2,1,0:T(8,128)(2,1)S(1)}, bf16[8,2,32,896]{3,2,1,0:T(8,128)(2,1)}, u32[]{:S(2)}, u32[]{:S(2)}) collective-permute-start(bf16[8,2,32,896]{3,2,1,0:T(8,128)(2,1)S(1)} %bitcast.165), channel_id=1, source_target_pairs={{0,384},{16,400},{32,416},{48,432},{64,448},{80,464},{96,480},{112... | collective-permute-start | bytes 2752520 | tf_op jit(solution)/shard_map/ppermute | solution.py:85
  103.0 9.3 %all-to-all-start.3 = ((bf16[8,32,896]{2,1,0:T(8,128)(2,1)}), bf16[8,32,896]{2,1,0:T(8,128)(2,1)S(1)}, u32[]{:S(2)}, u32[]{:S(2)}) async-start(bf16[8,32,896]{2,1,0:T(8,128)(2,1)} %broadcast_in_dim.37), calls=%async_computation.3 | async-start | bytes 917504 | tf_op jit(solution)/shard_map/all_to_all | solution.py:22
  117.6 3.2 %collective-permute-done.5 = bf16[8,2,32,896]{3,2,1,0:T(8,128)(2,1)} collective-permute-done((bf16[8,2,32,896]{3,2,1,0:T(8,128)(2,1)S(1)}, bf16[8,2,32,896]{3,2,1,0:T(8,128)(2,1)}, u32[]{:S(2)}, u32[]{:S(2)}) %collective-permute-start.5) | collective-permute-done | bytes 917536 | tf_op jit(solution)/shard_map/ppermute | solution.py:84
  124.9 4.6 %collective-permute-start.8 = (bf16[4,2,32,896]{3,2,1,0:T(8,128)(2,1)S(1)}, bf16[4,2,32,896]{3,2,1,0:T(8,128)(2,1)S(1)}, u32[]{:S(2)}, u32[]{:S(2)}) collective-permute-start(bf16[4,2,32,896]{3,2,1,0:T(8,128)(2,1)S(1)} %slice.81), channel_id=1, source_target_pairs={{0,384},{16,400},{32,416},{48,432},{64,448},{80,464},{96,480},{112... | collective-permute-start | bytes 1376264 | tf_op jit(solution)/shard_map/ppermute | solution.py:90
  138.5 3.6 %all-to-all-start.4 = ((bf16[4,8,32,896]{3,2,1,0:T(8,128)(2,1)}), bf16[4,8,32,896]{3,2,1,0:T(8,128)(2,1)S(1)}, u32[]{:S(2)}, u32[]{:S(2)}) async-start(bf16[4,8,32,896]{3,2,1,0:T(8,128)(2,1)} %broadcast_in_dim.38), calls=%async_computation.4 | async-start | bytes 3670016 | tf_op jit(solution)/shard_map/all_to_all | solution.py:22
  147.8 3.8 %slice_convert_fusion = f32[4,8,1,32,896]{4,3,2,1,0:T(8,128)} fusion(bf16[4,8,2,32,896]{4,3,2,1,0:T(8,128)(2,1)} %bitcast_dynamic-update-slice_fusion.3), kind=kLoop, calls=%fused_computation.34 | loop fusion | flops 917504 | bytes 5505024 | tf_op jit(solution)/shard_map/convert_element_type | solution.py:108
  151.6 12.4 %all-to-all-done.4 = bf16[4,8,32,896]{3,2,1,0:T(8,128)(2,1)S(1)} async-done(((bf16[4,8,32,896]{3,2,1,0:T(8,128)(2,1)}), bf16[4,8,32,896]{3,2,1,0:T(8,128)(2,1)S(1)}, u32[]{:S(2)}, u32[]{:S(2)}) %all-to-all-start.4) | async-done | bytes 1835040 | tf_op jit(solution)/shard_map/all_to_all | solution.py:22
  164.0 3.6 %fusion.20 = (bf16[1024,896]{1,0:T(8,128)(2,1)S(1)}, bf16[1024,896]{1,0:T(8,128)(2,1)S(1)}) fusion(f32[4,8,1,32,896]{4,3,2,1,0:T(8,128)} %slice_convert_fusion, bf16[4,8,32,896]{3,2,1,0:T(8,128)(2,1)S(1)} %all-to-all-done.4, bf16[4,8,2,32,896]{4,3,2,1,0:T(8,128)(2,1)} %bitcast_dynamic-update-slice_fusion.3), kind=kLoop, calls=%fused_computation.26 | loop fusion | flops 13762560 | bytes 11010048 | tf_op jit(solution)/shard_map/convert_element_type | solution.py:113
  169.2 6.8 %all_to_all.35 = f32[2,8,64,256]{3,2,1,0:T(8,128)S(1)} all-to-all(f32[2,8,64,256]{3,2,1,0:T(8,128)S(1)} %bitcast.162), channel_id=1, replica_groups={{0,1},{2,3},{4,5},{6,7},{8,9},{10,11},{12,13},{14,15},{16,17},{18,19},{..., dimensions={0} | all-to-all | bytes 2097152 | tf_op jit(solution)/shard_map/all_to_all | solution.py:22
  176.8 3.5 %all-to-all-start.6 = ((bf16[4,2,64,256]{3,2,1,0:T(8,128)(2,1)}), bf16[4,2,64,256]{3,2,1,0:T(8,128)(2,1)S(1)}, u32[]{:S(2)}, u32[]{:S(2)}) async-start(bf16[4,2,64,256]{3,2,1,0:T(8,128)(2,1)} %bitcast.171), calls=%async_computation.6 | async-start | bytes 524288 | tf_op jit(solution)/shard_map/all_to_all | solution.py:22
  180.4 4.4 %fusion.10 = (bf16[4,8,32,896]{3,2,1,0:T(8,128)(2,1)S(1)}, bf16[4,8,32,896]{3,2,1,0:T(8,128)(2,1)}) fusion(bf16[4,8,32,896]{3,2,1,0:T(8,128)(2,1)S(1)} %all-to-all-done.4, bf16[4,8,2,32,896]{4,3,2,1,0:T(8,128)(2,1)} %bitcast_dynamic-update-slice_fusion.3), kind=kLoop, calls=%fused_computation.16 | loop fusion | flops 14680064 | bytes 9175040 | tf_op jit(solution)/shard_map/convert_element_type | solution.py:114
  190.9 9.5 %collective-permute-done.9 = f32[64,256]{1,0:T(8,128)S(1)} collective-permute-done((f32[64,256]{1,0:T(8,128)S(1)}, f32[64,256]{1,0:T(8,128)S(1)}, u32[]{:S(2)}, u32[]{:S(2)}) %collective-permute-start.9) | collective-permute-done | bytes 65568 | tf_op jit(solution)/shard_map/ppermute | solution.py:125
  (80 shorter events, 47.4 us)
Async XLA Ops:
  0.6 26.7 %copy-start.11 = (bf16[64,256]{1,0:T(8,128)(2,1)S(1)}, bf16[64,256]{1,0:T(8,128)(2,1)}, u32[]{:S(2)}) copy-start(bf16[64,256]{1,0:T(8,128)(2,1)} %param.8) | copy-start | bytes 98308
  0.6 26.7 %copy-start.10 = (bf16[64,256]{1,0:T(8,128)(2,1)S(1)}, bf16[64,256]{1,0:T(8,128)(2,1)}, u32[]{:S(2)}) copy-start(bf16[64,256]{1,0:T(8,128)(2,1)} %param.7) | copy-start | bytes 98308
  0.7 38.7 %copy-start.9 = (bf16[32,896]{1,0:T(8,128)(2,1)S(1)}, bf16[32,896]{1,0:T(8,128)(2,1)}, u32[]{:S(2)}) copy-start(bf16[32,896]{1,0:T(8,128)(2,1)} %param.9) | copy-start | bytes 172036
  0.7 38.6 %copy-start.8 = (bf16[32,896]{1,0:T(8,128)(2,1)S(1)}, bf16[32,896]{1,0:T(8,128)(2,1)}, u32[]{:S(2)}) copy-start(bf16[32,896]{1,0:T(8,128)(2,1)} %param.10) | copy-start | bytes 172036
  1.5 25.8 %collective-permute-start.1 = (bf16[2,64,256]{2,1,0:T(8,128)(2,1)S(1)}, bf16[2,64,256]{2,1,0:T(8,128)(2,1)S(1)}, u32[]{:S(2)}, u32[]{:S(2)}) collective-permute-start(bf16[2,64,256]{2,1,0:T(8,128)(2,1)S(1)} %pad_maximum_fusion.7), channel_id=1, source_target_pairs={{0,2},{1,3},{2,0},{3,1},{4,6},{5,7},{6,4},{7,5},{8,10},{9,11},{10,... | collective-permute-start | bytes 196616 | tf_op jit(solution)/shard_map/ppermute | solution.py:35
  16.9 22.4 %collective-permute-start = (bf16[2,32,896]{2,1,0:T(8,128)(2,1)S(1)}, bf16[2,32,896]{2,1,0:T(8,128)(2,1)S(1)}, u32[]{:S(2)}, u32[]{:S(2)}) collective-permute-start(bf16[2,32,896]{2,1,0:T(8,128)(2,1)S(1)} %pad_maximum_fusion.5), channel_id=1, source_target_pairs={{0,64},{16,80},{32,96},{48,112},{64,0},{80,16},{96,32},{112,48},{1... | collective-permute-start | bytes 344072 | tf_op jit(solution)/shard_map/ppermute | solution.py:35
  23.3 27.8 %all-to-all-start = ((bf16[4,896,256]{2,1,0:T(8,128)(2,1)}), bf16[4,896,256]{2,1,0:T(8,128)(2,1)S(1)}, u32[]{:S(2)}, u32[]{:S(2)}) async-start(bf16[4,896,256]{2,1,0:T(8,128)(2,1)} %broadcast_in_dim.36), calls=%async_computation | async-start | bytes 3670016 | tf_op jit(solution)/shard_map/all_to_all | solution.py:22
  39.4 11.6 %collective-permute-start.2 = (bf16[2,2,32,896]{3,2,1,0:T(8,128)(2,1)S(1)}, bf16[2,2,32,896]{3,2,1,0:T(8,128)(2,1)S(1)}, u32[]{:S(2)}, u32[]{:S(2)}) collective-permute-start(bf16[2,2,32,896]{3,2,1,0:T(8,128)(2,1)S(1)} %pad_maximum_fusion.4), channel_id=1, source_target_pairs={{0,32},{16,48},{32,0},{48,16},{64,96},{80,112},{96,64},{112,80},{1... | collective-permute-start | bytes 688136 | tf_op jit(solution)/shard_map/ppermute | solution.py:35
  51.1 19.8 %collective-permute-start.3 = (bf16[2,2,2,32,896]{4,3,2,1,0:T(8,128)(2,1)S(1)}, bf16[2,2,2,32,896]{4,3,2,1,0:T(8,128)(2,1)S(1)}, u32[]{:S(2)}, u32[]{:S(2)}) collective-permute-start(bf16[2,2,2,32,896]{4,3,2,1,0:T(8,128)(2,1)S(1)} %pad_maximum_fusion.3), channel_id=1, source_target_pairs={{0,16},{16,0},{32,48},{48,32},{64,80},{80,64},{96,112},{112,96},{1... | collective-permute-start | bytes 1376264 | tf_op jit(solution)/shard_map/ppermute | solution.py:35
  55.9 9.2 %all-to-all-start.1 = ((bf16[4,2,64,256]{3,2,1,0:T(8,128)(2,1)}), bf16[4,2,64,256]{3,2,1,0:T(8,128)(2,1)S(1)}, u32[]{:S(2)}, u32[]{:S(2)}) async-start(bf16[4,2,64,256]{3,2,1,0:T(8,128)(2,1)} %all_gather.15), calls=%async_computation.1 | async-start | bytes 524288 | tf_op jit(solution)/shard_map/all_to_all | solution.py:22
  71.6 8.0 %copy-start.7 = (bf16[2,64,256]{2,1,0:T(8,128)(2,1)S(1)}, bf16[2,64,256]{2,1,0:T(8,128)(2,1)}, u32[]{:S(2)}) copy-start(bf16[2,64,256]{2,1,0:T(8,128)(2,1)} %get-tuple-element.18) | copy-start | bytes 196612
  73.3 28.8 %all-to-all-start.2 = ((bf16[8,32,896]{2,1,0:T(8,128)(2,1)}), bf16[8,32,896]{2,1,0:T(8,128)(2,1)S(1)}, u32[]{:S(2)}, u32[]{:S(2)}) async-start(bf16[8,32,896]{2,1,0:T(8,128)(2,1)} %bitcast.32), calls=%async_computation.2 | async-start | bytes 917504 | tf_op jit(solution)/shard_map/all_to_all | solution.py:22
  90.7 25.0 %collective-permute-start.4 = (bf16[2,8,64,256]{3,2,1,0:T(8,128)(2,1)S(1)}, bf16[2,8,64,256]{3,2,1,0:T(8,128)(2,1)S(1)}, u32[]{:S(2)}, u32[]{:S(2)}) collective-permute-start(bf16[2,8,64,256]{3,2,1,0:T(8,128)(2,1)S(1)} %pad_maximum_fusion.2), channel_id=1, source_target_pairs={{0,1},{1,0},{2,3},{3,2},{4,5},{5,4},{6,7},{7,6},{8,9},{9,8},{10,11... | collective-permute-start | bytes 1572872 | tf_op jit(solution)/shard_map/ppermute | solution.py:35
  95.6 25.2 %collective-permute-start.5 = (bf16[8,2,32,896]{3,2,1,0:T(8,128)(2,1)S(1)}, bf16[8,2,32,896]{3,2,1,0:T(8,128)(2,1)}, u32[]{:S(2)}, u32[]{:S(2)}) collective-permute-start(bf16[8,2,32,896]{3,2,1,0:T(8,128)(2,1)S(1)} %bitcast.164), channel_id=1, source_target_pairs={{0,128},{16,144},{32,160},{48,176},{64,192},{80,208},{96,224},{112... | collective-permute-start | bytes 2752520 | tf_op jit(solution)/shard_map/ppermute | solution.py:84
  97.8 26.0 %collective-permute-start.6 = (bf16[8,2,32,896]{3,2,1,0:T(8,128)(2,1)S(1)}, bf16[8,2,32,896]{3,2,1,0:T(8,128)(2,1)}, u32[]{:S(2)}, u32[]{:S(2)}) collective-permute-start(bf16[8,2,32,896]{3,2,1,0:T(8,128)(2,1)S(1)} %bitcast.165), channel_id=1, source_target_pairs={{0,384},{16,400},{32,416},{48,432},{64,448},{80,464},{96,480},{112... | collective-permute-start | bytes 2752520 | tf_op jit(solution)/shard_map/ppermute | solution.py:85
  103.0 34.0 %all-to-all-start.3 = ((bf16[8,32,896]{2,1,0:T(8,128)(2,1)}), bf16[8,32,896]{2,1,0:T(8,128)(2,1)S(1)}, u32[]{:S(2)}, u32[]{:S(2)}) async-start(bf16[8,32,896]{2,1,0:T(8,128)(2,1)} %broadcast_in_dim.37), calls=%async_computation.3 | async-start | bytes 917504 | tf_op jit(solution)/shard_map/all_to_all | solution.py:22
  121.9 14.4 %collective-permute-start.7 = (bf16[4,2,32,896]{3,2,1,0:T(8,128)(2,1)S(1)}, bf16[4,2,32,896]{3,2,1,0:T(8,128)(2,1)S(1)}, u32[]{:S(2)}, u32[]{:S(2)}) collective-permute-start(bf16[4,2,32,896]{3,2,1,0:T(8,128)(2,1)S(1)} %slice.80), channel_id=1, source_target_pairs={{0,128},{16,144},{32,160},{48,176},{64,192},{80,208},{96,224},{112... | collective-permute-start | bytes 1376264 | tf_op jit(solution)/shard_map/ppermute | solution.py:89
  124.9 17.3 %collective-permute-start.8 = (bf16[4,2,32,896]{3,2,1,0:T(8,128)(2,1)S(1)}, bf16[4,2,32,896]{3,2,1,0:T(8,128)(2,1)S(1)}, u32[]{:S(2)}, u32[]{:S(2)}) collective-permute-start(bf16[4,2,32,896]{3,2,1,0:T(8,128)(2,1)S(1)} %slice.81), channel_id=1, source_target_pairs={{0,384},{16,400},{32,416},{48,432},{64,448},{80,464},{96,480},{112... | collective-permute-start | bytes 1376264 | tf_op jit(solution)/shard_map/ppermute | solution.py:90
  138.5 25.4 %all-to-all-start.4 = ((bf16[4,8,32,896]{3,2,1,0:T(8,128)(2,1)}), bf16[4,8,32,896]{3,2,1,0:T(8,128)(2,1)S(1)}, u32[]{:S(2)}, u32[]{:S(2)}) async-start(bf16[4,8,32,896]{3,2,1,0:T(8,128)(2,1)} %broadcast_in_dim.38), calls=%async_computation.4 | async-start | bytes 3670016 | tf_op jit(solution)/shard_map/all_to_all | solution.py:22
  151.6 16.0 %copy-start.3 = (bf16[256,896]{1,0:T(8,128)(2,1)S(1)}, bf16[256,896]{1,0:T(8,128)(2,1)}, u32[]{:S(2)}) copy-start(bf16[256,896]{1,0:T(8,128)(2,1)} %param.12) | copy-start | bytes 1376260
  151.6 16.8 %copy-start.1 = (bf16[256,896]{1,0:T(8,128)(2,1)S(1)}, bf16[256,896]{1,0:T(8,128)(2,1)}, u32[]{:S(2)}) copy-start(bf16[256,896]{1,0:T(8,128)(2,1)} %param.11) | copy-start | bytes 1376260
  176.8 9.6 %all-to-all-start.6 = ((bf16[4,2,64,256]{3,2,1,0:T(8,128)(2,1)}), bf16[4,2,64,256]{3,2,1,0:T(8,128)(2,1)S(1)}, u32[]{:S(2)}, u32[]{:S(2)}) async-start(bf16[4,2,64,256]{3,2,1,0:T(8,128)(2,1)} %bitcast.171), calls=%async_computation.6 | async-start | bytes 524288 | tf_op jit(solution)/shard_map/all_to_all | solution.py:22
  180.4 4.4 %copy-start.4 = (bf16[256,896]{1,0:T(8,128)(2,1)S(1)}, bf16[256,896]{1,0:T(8,128)(2,1)}, u32[]{:S(2)}) copy-start(bf16[256,896]{1,0:T(8,128)(2,1)} %param.12) | copy-start | bytes 1376260
  186.5 13.8 %collective-permute-start.9 = (f32[64,256]{1,0:T(8,128)S(1)}, f32[64,256]{1,0:T(8,128)S(1)}, u32[]{:S(2)}, u32[]{:S(2)}) collective-permute-start(f32[64,256]{1,0:T(8,128)S(1)} %select_bitcast_fusion.8), channel_id=1, source_target_pairs={{0,2},{1,3},{2,0},{3,1},{4,6},{5,7},{6,4},{7,5},{8,10},{9,11},{10,... | collective-permute-start | bytes 196616 | tf_op jit(solution)/shard_map/ppermute | solution.py:125
  (4 other events, 16.9 us)

commit v4 on v3

v4 whole, which is shorter than its diff:
```python
import jax
import jax.numpy as jnp
from jax import lax
from jax.sharding import PartitionSpec as P

X, ZL, Y, ZH, C = 4, 8, 4, 2, 2
X_GROUPS = [[x * ZL + z for x in range(X)] for z in range(ZL)]
Z_GROUPS = [[x * ZL + z for z in range(ZL)] for x in range(X)]
Z_BY_CORE = [
    [x * ZL + (h * C + c) * 2 + k for c in range(C) for h in range(ZH) for k in range(2)]
    for x in range(X)
]
YC_GROUPS = [[(y * ZH + h) * C + c for y in range(Y) for c in range(C)] for h in range(ZH)]
Y_GROUPS = [[(y * ZH + h) * C + c for y in range(Y)] for h in range(ZH) for c in range(C)]
C_GROUPS = [[(y * ZH + h) * C + c for c in range(C)] for y in range(Y) for h in range(ZH)]
ZH_SWAP = [(t, t ^ C) for t in range(Y * ZH * C)]
C_SWAP = [(t, t ^ 1) for t in range(Y * ZH * C)]
X_UP = [(x * ZL + z, (x + 1) % X * ZL + z) for x in range(X) for z in range(ZL)]
X_DOWN = [(x * ZL + z, (x - 1) % X * ZL + z) for x in range(X) for z in range(ZL)]


def exchange(blocks, axis, groups):
    return lax.all_to_all(blocks, axis, 0, 0, axis_index_groups=groups, tiled=True)


def gather(block, axis, groups):
    copies = jnp.broadcast_to(block[None], (len(groups[0]),) + block.shape)
    return exchange(copies, axis, groups)


def add_up(blocks, axis, groups):
    return jnp.sum(exchange(blocks, axis, groups).astype(jnp.float32), axis=0)


def pair(block, axis, perm, bit, dim):
    other = lax.ppermute(block, axis, perm)
    first = jnp.where(bit == 0, block, other)
    second = jnp.where(bit == 0, other, block)
    return jnp.stack([first, second], axis=dim)


def around(block, held):
    half = block.shape[0] // 2
    before = lax.ppermute(block, "dp", X_UP)
    after = lax.ppermute(block, "dp", X_DOWN)
    before, after, held = lax.optimization_barrier((before, after, held))
    far_low = lax.ppermute(before[:half], "dp", X_UP)
    far_high = lax.ppermute(after[half:], "dp", X_DOWN)
    return [block, after, jnp.concatenate([far_low, far_high]), before], held


def on_device(tokens, out_grad, gate_pre, up_pre, gate_weight, up_weight, down_weight):
    rows, feats = out_grad.shape
    toks, hid = gate_pre.shape
    part = rows * ZH * C
    dp, tensor = lax.axis_index("dp"), lax.axis_index("tensor")
    x, z = dp // ZL, dp % ZL

    both = jnp.stack([out_grad, tokens])
    both = pair(both, "tensor", ZH_SWAP, tensor // C % ZH, 1)

    down_ring, both = around(down_weight, both)
    grads_y = gather(both[0], "tensor", Y_GROUPS)

    saved = jnp.stack([gate_pre, up_pre])
    for dim, reach in enumerate((4, 2)):
        swap = [(d, d ^ reach) for d in range(X * ZL)]
        if reach == 2:
            saved, grads_y = lax.optimization_barrier((saved, grads_y))
        saved = pair(saved, "dp", swap, z // reach % 2, dim)

    grads_x = exchange(grads_y, "dp", X_GROUPS)
    grads_x = lax.all_gather(grads_x, "tensor", axis_index_groups=C_GROUPS)
    grads_x, saved = lax.optimization_barrier((grads_x, saved))
    partial = sum(
        jnp.einsum(
            "nd,fd->nf",
            lax.dynamic_index_in_dim(grads_x, (x + k) % X, 1, False).reshape(part, feats),
            down_ring[k],
            preferred_element_type=jnp.float32,
        )
        for k in range(X)
    ).astype(jnp.bfloat16)

    saved = pair(saved, "dp", [(d, d ^ 1) for d in range(X * ZL)], z % 2, 2)
    saved_ring, _ = around(saved.reshape(ZL, 2, toks, hid), ())

    inputs, _ = lax.optimization_barrier((both[1], partial))
    tokens_y = lax.all_gather(inputs, "tensor", axis_index_groups=Y_GROUPS)
    both = jnp.stack([grads_y, tokens_y])
    both = lax.dynamic_slice_in_dim(jnp.concatenate([both, both], axis=1), x, Y, 1)
    both = pair(both, "tensor", C_SWAP, tensor % C, 3)
    both = both.reshape(2, Y, part, feats)
    grads_ring, tokens_ring = both[0], both[1]

    hidden = add_up(partial.reshape(ZL, toks, hid), "dp", Z_BY_CORE).astype(jnp.bfloat16)
    hidden = gather(hidden, "dp", Z_GROUPS)
    hidden_ring, own = around(hidden, hidden)
    hidden_ring[0] = own

    down_sum = gate_sum = up_sum = 0.0
    partial_in = jnp.zeros((Y, C, ZH, rows, feats), jnp.bfloat16)
    for k in (0, 1, 3, 2):
        gate_float = saved_ring[k][:, 0].reshape(part, hid).astype(jnp.float32)
        up_float = saved_ring[k][:, 1].reshape(part, hid).astype(jnp.float32)
        hidden = hidden_ring[k].reshape(part, hid).astype(jnp.float32)
        gate_sigmoid = 1.0 / (1.0 + jnp.exp(-gate_float))
        active = (gate_float * gate_sigmoid * up_float).astype(jnp.bfloat16)
        gate_grad = (
            hidden * up_float * gate_sigmoid * (1.0 + gate_float * (1.0 - gate_sigmoid))
        ).astype(jnp.bfloat16)
        up_grad = (hidden * gate_float * gate_sigmoid).astype(jnp.bfloat16)
        gate_grad, up_grad = lax.optimization_barrier((gate_grad, up_grad))
        block = jnp.einsum(
            "nf,df->nd", gate_grad, gate_weight, preferred_element_type=jnp.float32
        ) + jnp.einsum("nf,df->nd", up_grad, up_weight, preferred_element_type=jnp.float32)
        block = block.astype(jnp.bfloat16).reshape(1, ZH, C, rows, feats).swapaxes(1, 2)
        partial_in = lax.dynamic_update_slice_in_dim(partial_in, block, (x + k) % X, 0)
        down_sum += jnp.einsum(
            "nf,nd->fd", active, grads_ring[k], preferred_element_type=jnp.float32
        )
        gate_sum += jnp.einsum(
            "nd,nf->df", tokens_ring[k], gate_grad, preferred_element_type=jnp.float32
        )
        up_sum += jnp.einsum(
            "nd,nf->df", tokens_ring[k], up_grad, preferred_element_type=jnp.float32
        )

    partial_in = partial_in.reshape(Y * C, ZH, rows, feats)
    partial_in = add_up(partial_in, "tensor", YC_GROUPS)
    upper = tensor // C % ZH == 1
    sent = jnp.where(upper, partial_in[0], partial_in[1])
    kept = jnp.where(upper, partial_in[1], partial_in[0])
    input_grad = (kept + lax.ppermute(sent, "tensor", ZH_SWAP)).astype(jnp.bfloat16)

    gate_score = jnp.abs(gate_weight.astype(jnp.float32) * gate_sum)
    up_score = jnp.abs(up_weight.astype(jnp.float32) * up_sum)
    down_score = jnp.abs(down_weight.astype(jnp.float32) * down_sum)
    return (gate_score, up_score, down_score, input_grad)


def solution(mesh):
    return jax.shard_map(
        on_device,
        mesh=mesh,
        in_specs=(
            P("tensor", "dp"),
            P("tensor", "dp"),
            P("dp", "tensor"),
            P("dp", "tensor"),
            P("dp", "tensor"),
            P("dp", "tensor"),
            P("tensor", "dp"),
        ),
        out_specs=(P("dp", "tensor"), P("dp", "tensor"), P("tensor", "dp"), P("tensor", "dp")),
        check_vma=False,
    )
```

time: 205 us -> 221 us (1.078); the launches traced: 201 us -> 220 us
  starting transfers between devices: 77.3 us -> 115 us
  blocking collectives: 34.1 us -> 15.3 us
  waiting for transfers between devices: 41.5 us -> 51.3 us
  local copies, waits for them, and re-layouts: 16.3 us -> 7.02 us
  other arithmetic: 22.1 us -> 14.6 us
  matrix products: 8.5 us -> 15.2 us
    ppermute x4 -> x12, starting transfers between devices: 13 us -> 39.6 us  [the longest x3 10.6 us: around(): far_high = lax.ppermute(after[half:], 'dp', X_DOWN)]
    ppermute x4 -> x12, waiting for transfers between devices: 5.62 us -> 28 us  [the longest x3 18.8 us: around(): before = lax.ppermute(block, 'dp', X_UP)]
    all_gather x1 -> x0, blocking collectives: 11.3 us -> none  [on_device(): grads_y = lax.all_gather(both[0], 'tensor', axis_index_groups=Y_GROUPS)]
    ppermute x1, starting transfers between devices: 2.68 us -> 10.4 us  [on_device(): lax.ppermute(sent, 'tensor', ZH_SWAP)]
    dynamic_update_slice x5 -> x4, local copies, waits for them, and re-layouts: 7.05 us -> 0.06 us  [on_device(): lax.dynamic_update_slice_in_dim(partial_in, block, (x + k) % X, 0)]
    all_to_all x1 -> x0, blocking collectives: 6.81 us -> none  [exchange(): lax.all_to_all(blocks, axis, 0, 0, axis_index_groups=groups, tiled=True)]
    dot_general x7 -> x16, matrix products: 7.02 us -> 12.6 us  [the longest x4 4.06 us: on_device(): jnp.einsum('nd,nf->df', tokens_ring[k], gate_grad, preferred_element_type...]
    ppermute x1, waiting for transfers between devices: 9.45 us -> 4.33 us  [on_device(): lax.ppermute(sent, 'tensor', ZH_SWAP)]
  transfers between devices with their start and end apart: 16 -> 23, of which waited for: 6 -> 11; matrix products, arithmetic and copies ran while one was open for 18% -> 13% of each run, Pallas kernels for 0% -> 0%
where the time goes in v4:
time: 221 us; the launch traced here: 220 us
  starting transfers between devices  115 us (52%)
  waiting for transfers between devices  51.3 us (23%)
  blocking collectives  15.3 us (7%)
  matrix products  15.2 us (7%)
  other arithmetic  14.6 us (7%)
  local copies, waits for them, and re-layouts  7.02 us (3%)
    ppermute x5, starting transfers between devices, pair(): other = lax.ppermute(block, axis, perm)  34.6 us
    all_to_all x5, starting transfers between devices, exchange(): lax.all_to_all(blocks, axis, 0, 0, axis_index_groups=groups, tiled=True)  29.9 us
    ppermute x3, waiting for transfers between devices, around(): before = lax.ppermute(block, 'dp', X_UP)  18.8 us
    all_to_all x5, waiting for transfers between devices, exchange(): lax.all_to_all(blocks, axis, 0, 0, axis_index_groups=groups, tiled=True)  13.4 us
    ppermute x3, starting transfers between devices, around(): far_high = lax.ppermute(after[half:], 'dp', X_DOWN)  10.6 us
    ppermute x1, starting transfers between devices, on_device(): lax.ppermute(sent, 'tensor', ZH_SWAP)  10.4 us
    all_gather x1, blocking collectives, on_device(): tokens_y = lax.all_gather(inputs, 'tensor', axis_index_groups=Y_GROUPS)  9.91 us
    ppermute x3, starting transfers between devices, around(): after = lax.ppermute(block, 'dp', X_DOWN)  9.91 us
  transfers between devices with their start and end apart: 23, of which 11 were waited for; matrix products, arithmetic and copies ran while one was open for 13% of the time, Pallas kernels for 0%

profile of v4, /device:TPU:33, one launch (start us, length us, event | category | flops | bytes accessed | tf_op | source)
XLA Modules:
  0.0 219.6 jit_solution(14265779593269789831)
XLA Ops:
  3.8 3.4 %collective-permute-start.2 = (bf16[896,256]{1,0:T(8,128)(2,1)}, bf16[896,256]{1,0:T(8,128)(2,1)S(1)}, u32[]{:S(2)}, u32[]{:S(2)}) collective-permute-start(bf16[896,256]{1,0:T(8,128)(2,1)} %param.13), channel_id=1, source_target_pairs={{0,384},{16,400},{32,416},{48,432},{64,448},{80,464},{96,480},{112... | collective-permute-start | bytes 1376264 | tf_op jit(solution)/shard_map/ppermute | solution.py:45
  8.0 14.5 %collective-permute-start.3 = (bf16[2,64,256]{2,1,0:T(8,128)(2,1)S(1)}, bf16[2,64,256]{2,1,0:T(8,128)(2,1)S(1)}, u32[]{:S(2)}, u32[]{:S(2)}) collective-permute-start(bf16[2,64,256]{2,1,0:T(8,128)(2,1)S(1)} %pad_maximum_fusion.7), channel_id=1, source_target_pairs={{0,2},{1,3},{2,0},{3,1},{4,6},{5,7},{6,4},{7,5},{8,10},{9,11},{10,... | collective-permute-start | bytes 196616 | tf_op jit(solution)/shard_map/ppermute | solution.py:36
  22.6 4.0 %collective-permute-start = (bf16[2,32,896]{2,1,0:T(8,128)(2,1)S(1)}, bf16[2,32,896]{2,1,0:T(8,128)(2,1)S(1)}, u32[]{:S(2)}, u32[]{:S(2)}) collective-permute-start(bf16[2,32,896]{2,1,0:T(8,128)(2,1)S(1)} %pad_maximum_fusion.6), channel_id=1, source_target_pairs={{0,64},{16,80},{32,96},{48,112},{64,0},{80,16},{96,32},{112,48},{1... | collective-permute-start | bytes 344072 | tf_op jit(solution)/shard_map/ppermute | solution.py:36
  28.2 4.2 %all-to-all-start = ((bf16[4,2,64,256]{3,2,1,0:T(8,128)(2,1)}), bf16[4,2,64,256]{3,2,1,0:T(8,128)(2,1)}, u32[]{:S(2)}, u32[]{:S(2)}) async-start(bf16[4,2,64,256]{3,2,1,0:T(8,128)(2,1)} %broadcast_in_dim.17), calls=%async_computation | async-start | bytes 524288 | tf_op jit(solution)/shard_map/all_to_all | solution.py:23
  32.4 5.5 %collective-permute-done = bf16[2,32,896]{2,1,0:T(8,128)(2,1)S(1)} collective-permute-done((bf16[2,32,896]{2,1,0:T(8,128)(2,1)S(1)}, bf16[2,32,896]{2,1,0:T(8,128)(2,1)S(1)}, u32[]{:S(2)}, u32[]{:S(2)}) %collective-permute-start) | collective-permute-done | bytes 114720 | tf_op jit(solution)/shard_map/ppermute | solution.py:36
  38.2 3.4 %all-to-all-start.1 = ((bf16[4,2,64,256]{3,2,1,0:T(8,128)(2,1)}), bf16[4,2,64,256]{3,2,1,0:T(8,128)(2,1)S(1)}, u32[]{:S(2)}, u32[]{:S(2)}) async-start(bf16[4,2,64,256]{3,2,1,0:T(8,128)(2,1)} %all-to-all-done), calls=%async_computation.1 | async-start | bytes 524288 | tf_op jit(solution)/shard_map/all_to_all | solution.py:23
  41.6 3.4 %collective-permute-start.4 = (bf16[2,2,32,896]{3,2,1,0:T(8,128)(2,1)S(1)}, bf16[2,2,32,896]{3,2,1,0:T(8,128)(2,1)S(1)}, u32[]{:S(2)}, u32[]{:S(2)}) collective-permute-start(bf16[2,2,32,896]{3,2,1,0:T(8,128)(2,1)S(1)} %pad_maximum_fusion.3), channel_id=1, source_target_pairs={{0,32},{16,48},{32,0},{48,16},{64,96},{80,112},{96,64},{112,80},{1... | collective-permute-start | bytes 688136 | tf_op jit(solution)/shard_map/ppermute | solution.py:36
  51.8 5.4 %all-gather = bf16[8,2,64,256]{3,2,1,0:T(8,128)(2,1)S(1)} all-gather(bf16[4,2,64,256]{3,2,1,0:T(8,128)(2,1)S(1)} %all-to-all-done.1), channel_id=2, replica_groups={{0,1},{2,3},{4,5},{6,7},{8,9},{10,11},{12,13},{14,15},{16,17},{18,19},{..., dimensions={0}, use_global_device_ids=true | all-gather | bytes 786432 | tf_op jit(solution)/shard_map/all_gather | solution.py:73
  57.3 6.8 %collective-permute-start.10 = (bf16[2,2,2,32,896]{4,3,2,1,0:T(8,128)(2,1)S(1)}, bf16[2,2,2,32,896]{4,3,2,1,0:T(8,128)(2,1)S(1)}, u32[]{:S(2)}, u32[]{:S(2)}) collective-permute-start(bf16[2,2,2,32,896]{4,3,2,1,0:T(8,128)(2,1)S(1)} %pad_maximum_fusion.1), channel_id=1, source_target_pairs={{0,16},{16,0},{32,48},{48,32},{64,80},{80,64},{96,112},{112,96},{1... | collective-permute-start | bytes 1376264 | tf_op jit(solution)/shard_map/ppermute | solution.py:36
  66.3 4.9 %all-to-all-start.2 = ((bf16[8,32,896]{2,1,0:T(8,128)(2,1)}), bf16[8,32,896]{2,1,0:T(8,128)(2,1)S(1)}, u32[]{:S(2)}, u32[]{:S(2)}) async-start(bf16[8,32,896]{2,1,0:T(8,128)(2,1)} %bitcast.25), calls=%async_computation.2 | async-start | bytes 917504 | tf_op jit(solution)/shard_map/all_to_all | solution.py:23
  71.2 9.9 %all-gather.1 = bf16[8,64,256]{2,1,0:T(8,128)(2,1)S(1)} all-gather(bf16[2,64,256]{2,1,0:T(8,128)(2,1)S(1)} %get-tuple-element.31), channel_id=3, replica_groups={{0,4,8,12},{1,5,9,13},{2,6,10,14},{3,7,11,15},{16,20,24,28},{17,21,25,2..., dimensions={0}, use_global_device_ids=true | all-gather | bytes 327680 | tf_op jit(solution)/shard_map/all_gather | solution.py:89
  82.3 5.8 %collective-permute-start.7 = (bf16[2,4,2,64,256]{4,3,2,1,0:T(8,128)(2,1)S(1)}, bf16[2,4,2,64,256]{4,3,2,1,0:T(8,128)(2,1)S(1)}, u32[]{:S(2)}, u32[]{:S(2)}) collective-permute-start(bf16[2,4,2,64,256]{4,3,2,1,0:T(8,128)(2,1)S(1)} %fusion.69), channel_id=1, source_target_pairs={{0,1},{1,0},{2,3},{3,2},{4,5},{5,4},{6,7},{7,6},{8,9},{9,8},{10,11... | collective-permute-start | bytes 1572872 | tf_op jit(solution)/shard_map/ppermute | solution.py:36
  88.4 3.4 %collective-permute-start.11 = (bf16[8,2,32,896]{3,2,1,0:T(8,128)(2,1)S(1)}, bf16[8,2,32,896]{3,2,1,0:T(8,128)(2,1)S(1)}, u32[]{:S(2)}, u32[]{:S(2)}) collective-permute-start(bf16[8,2,32,896]{3,2,1,0:T(8,128)(2,1)S(1)} %bitcast.219), channel_id=1, source_target_pairs={{0,128},{16,144},{32,160},{48,176},{64,192},{80,208},{96,224},{112... | collective-permute-start | bytes 2752520 | tf_op jit(solution)/shard_map/ppermute | solution.py:44
  99.7 14.0 %collective-permute-done.11 = bf16[8,2,32,896]{3,2,1,0:T(8,128)(2,1)S(1)} collective-permute-done((bf16[8,2,32,896]{3,2,1,0:T(8,128)(2,1)S(1)}, bf16[8,2,32,896]{3,2,1,0:T(8,128)(2,1)S(1)}, u32[]{:S(2)}, u32[]{:S(2)}) %collective-permute-start.11) | collective-permute-done | bytes 917536 | tf_op jit(solution)/shard_map/ppermute | solution.py:44
  116.4 9.2 %all-to-all-start.3 = ((bf16[8,32,896]{2,1,0:T(8,128)(2,1)}), bf16[8,32,896]{2,1,0:T(8,128)(2,1)}, u32[]{:S(2)}, u32[]{:S(2)}) async-start(bf16[8,32,896]{2,1,0:T(8,128)(2,1)} %broadcast_in_dim.18), calls=%async_computation.3 | async-start | bytes 917504 | tf_op jit(solution)/shard_map/all_to_all | solution.py:23
  129.6 3.4 %collective-permute-start.16 = (bf16[4,2,32,896]{3,2,1,0:T(8,128)(2,1)S(1)}, bf16[4,2,32,896]{3,2,1,0:T(8,128)(2,1)S(1)}, u32[]{:S(2)}, u32[]{:S(2)}) collective-permute-start(bf16[4,2,32,896]{3,2,1,0:T(8,128)(2,1)S(1)} %slice.121), channel_id=1, source_target_pairs={{0,384},{16,400},{32,416},{48,432},{64,448},{80,464},{96,480},{112... | collective-permute-start | bytes 1376264 | tf_op jit(solution)/shard_map/ppermute | solution.py:48
  135.7 4.3 %collective-permute-done.15 = bf16[4,2,32,896]{3,2,1,0:T(8,128)(2,1)S(1)} collective-permute-done((bf16[4,2,32,896]{3,2,1,0:T(8,128)(2,1)S(1)}, bf16[4,2,32,896]{3,2,1,0:T(8,128)(2,1)S(1)}, u32[]{:S(2)}, u32[]{:S(2)}) %collective-permute-start.15) | collective-permute-done | bytes 458784 | tf_op jit(solution)/shard_map/ppermute | solution.py:47
  142.7 6.1 %all-to-all-done.3 = bf16[8,32,896]{2,1,0:T(8,128)(2,1)} async-done(((bf16[8,32,896]{2,1,0:T(8,128)(2,1)}), bf16[8,32,896]{2,1,0:T(8,128)(2,1)}, u32[]{:S(2)}, u32[]{:S(2)}) %all-to-all-start.3) | async-done | bytes 458784 | tf_op jit(solution)/shard_map/all_to_all | solution.py:23
  157.0 4.8 %collective-permute-done.8 = bf16[8,32,896]{2,1,0:T(8,128)(2,1)S(1)} collective-permute-done((bf16[8,32,896]{2,1,0:T(8,128)(2,1)}, bf16[8,32,896]{2,1,0:T(8,128)(2,1)S(1)}, u32[]{:S(2)}, u32[]{:S(2)}) %collective-permute-start.8) | collective-permute-done | bytes 458784 | tf_op jit(solution)/shard_map/ppermute | solution.py:44
  166.4 4.0 %collective-permute-start.14 = (bf16[4,32,896]{2,1,0:T(8,128)(2,1)S(1)}, bf16[4,32,896]{2,1,0:T(8,128)(2,1)S(1)}, u32[]{:S(2)}, u32[]{:S(2)}) collective-permute-start(bf16[4,32,896]{2,1,0:T(8,128)(2,1)S(1)} %slice.119), channel_id=1, source_target_pairs={{0,384},{16,400},{32,416},{48,432},{64,448},{80,464},{96,480},{112... | collective-permute-start | bytes 688136 | tf_op jit(solution)/shard_map/ppermute | solution.py:48
  184.1 8.2 %all-to-all-start.4 = ((bf16[8,2,64,256]{3,2,1,0:T(8,128)(2,1)}), bf16[8,2,64,256]{3,2,1,0:T(8,128)(2,1)}, u32[]{:S(2)}, u32[]{:S(2)}) async-start(bf16[8,2,64,256]{3,2,1,0:T(8,128)(2,1)} %bitcast.227), calls=%async_computation.4 | async-start | bytes 1048576 | tf_op jit(solution)/shard_map/all_to_all | solution.py:23
  194.8 7.1 %all-to-all-done.4 = bf16[8,2,64,256]{3,2,1,0:T(8,128)(2,1)} async-done(((bf16[8,2,64,256]{3,2,1,0:T(8,128)(2,1)}), bf16[8,2,64,256]{3,2,1,0:T(8,128)(2,1)}, u32[]{:S(2)}, u32[]{:S(2)}) %all-to-all-start.4) | async-done | bytes 524320 | tf_op jit(solution)/shard_map/all_to_all | solution.py:23
  203.0 10.4 %collective-permute-start.17 = (f32[64,256]{1,0:T(8,128)S(1)}, f32[64,256]{1,0:T(8,128)S(1)}, u32[]{:S(2)}, u32[]{:S(2)}) collective-permute-start(f32[64,256]{1,0:T(8,128)S(1)} %select_bitcast_fusion.8), channel_id=1, source_target_pairs={{0,2},{1,3},{2,0},{3,1},{4,6},{5,7},{6,4},{7,5},{8,10},{9,11},{10,... | collective-permute-start | bytes 196616 | tf_op jit(solution)/shard_map/ppermute | solution.py:134
  214.7 4.3 %collective-permute-done.17 = f32[64,256]{1,0:T(8,128)S(1)} collective-permute-done((f32[64,256]{1,0:T(8,128)S(1)}, f32[64,256]{1,0:T(8,128)S(1)}, u32[]{:S(2)}, u32[]{:S(2)}) %collective-permute-start.17) | collective-permute-done | bytes 65568 | tf_op jit(solution)/shard_map/ppermute | solution.py:134
  (145 shorter events, 67.5 us)
Async XLA Ops:
  0.6 26.8 %collective-permute-start.1 = (bf16[896,256]{1,0:T(8,128)(2,1)}, bf16[896,256]{1,0:T(8,128)(2,1)S(1)}, u32[]{:S(2)}, u32[]{:S(2)}) collective-permute-start(bf16[896,256]{1,0:T(8,128)(2,1)} %param.13), channel_id=1, source_target_pairs={{0,128},{16,144},{32,160},{48,176},{64,192},{80,208},{96,224},{112... | collective-permute-start | bytes 1376264 | tf_op jit(solution)/shard_map/ppermute | solution.py:44
  3.8 23.7 %collective-permute-start.2 = (bf16[896,256]{1,0:T(8,128)(2,1)}, bf16[896,256]{1,0:T(8,128)(2,1)S(1)}, u32[]{:S(2)}, u32[]{:S(2)}) collective-permute-start(bf16[896,256]{1,0:T(8,128)(2,1)} %param.13), channel_id=1, source_target_pairs={{0,384},{16,400},{32,416},{48,432},{64,448},{80,464},{96,480},{112... | collective-permute-start | bytes 1376264 | tf_op jit(solution)/shard_map/ppermute | solution.py:45
  8.0 18.7 %collective-permute-start.3 = (bf16[2,64,256]{2,1,0:T(8,128)(2,1)S(1)}, bf16[2,64,256]{2,1,0:T(8,128)(2,1)S(1)}, u32[]{:S(2)}, u32[]{:S(2)}) collective-permute-start(bf16[2,64,256]{2,1,0:T(8,128)(2,1)S(1)} %pad_maximum_fusion.7), channel_id=1, source_target_pairs={{0,2},{1,3},{2,0},{3,1},{4,6},{5,7},{6,4},{7,5},{8,10},{9,11},{10,... | collective-permute-start | bytes 196616 | tf_op jit(solution)/shard_map/ppermute | solution.py:36
  22.6 15.3 %collective-permute-start = (bf16[2,32,896]{2,1,0:T(8,128)(2,1)S(1)}, bf16[2,32,896]{2,1,0:T(8,128)(2,1)S(1)}, u32[]{:S(2)}, u32[]{:S(2)}) collective-permute-start(bf16[2,32,896]{2,1,0:T(8,128)(2,1)S(1)} %pad_maximum_fusion.6), channel_id=1, source_target_pairs={{0,64},{16,80},{32,96},{48,112},{64,0},{80,16},{96,32},{112,48},{1... | collective-permute-start | bytes 344072 | tf_op jit(solution)/shard_map/ppermute | solution.py:36
  28.2 10.0 %all-to-all-start = ((bf16[4,2,64,256]{3,2,1,0:T(8,128)(2,1)}), bf16[4,2,64,256]{3,2,1,0:T(8,128)(2,1)}, u32[]{:S(2)}, u32[]{:S(2)}) async-start(bf16[4,2,64,256]{3,2,1,0:T(8,128)(2,1)} %broadcast_in_dim.17), calls=%async_computation | async-start | bytes 524288 | tf_op jit(solution)/shard_map/all_to_all | solution.py:23
  38.2 13.6 %all-to-all-start.1 = ((bf16[4,2,64,256]{3,2,1,0:T(8,128)(2,1)}), bf16[4,2,64,256]{3,2,1,0:T(8,128)(2,1)S(1)}, u32[]{:S(2)}, u32[]{:S(2)}) async-start(bf16[4,2,64,256]{3,2,1,0:T(8,128)(2,1)} %all-to-all-done), calls=%async_computation.1 | async-start | bytes 524288 | tf_op jit(solution)/shard_map/all_to_all | solution.py:23
  41.6 15.5 %collective-permute-start.4 = (bf16[2,2,32,896]{3,2,1,0:T(8,128)(2,1)S(1)}, bf16[2,2,32,896]{3,2,1,0:T(8,128)(2,1)S(1)}, u32[]{:S(2)}, u32[]{:S(2)}) collective-permute-start(bf16[2,2,32,896]{3,2,1,0:T(8,128)(2,1)S(1)} %pad_maximum_fusion.3), channel_id=1, source_target_pairs={{0,32},{16,48},{32,0},{48,16},{64,96},{80,112},{96,64},{112,80},{1... | collective-permute-start | bytes 688136 | tf_op jit(solution)/shard_map/ppermute | solution.py:36
  45.2 19.9 %collective-permute-start.5 = (bf16[448,256]{1,0:T(8,128)(2,1)S(1)}, bf16[448,256]{1,0:T(8,128)(2,1)S(1)}, u32[]{:S(2)}, u32[]{:S(2)}) collective-permute-start(bf16[448,256]{1,0:T(8,128)(2,1)S(1)} %slice.106), channel_id=1, source_target_pairs={{0,128},{16,144},{32,160},{48,176},{64,192},{80,208},{96,224},{112... | collective-permute-start | bytes 688136 | tf_op jit(solution)/shard_map/ppermute | solution.py:47
  48.6 16.5 %collective-permute-start.6 = (bf16[448,256]{1,0:T(8,128)(2,1)S(1)}, bf16[448,256]{1,0:T(8,128)(2,1)S(1)}, u32[]{:S(2)}, u32[]{:S(2)}) collective-permute-start(bf16[448,256]{1,0:T(8,128)(2,1)S(1)} %slice.107), channel_id=1, source_target_pairs={{0,384},{16,400},{32,416},{48,432},{64,448},{80,464},{96,480},{112... | collective-permute-start | bytes 688136 | tf_op jit(solution)/shard_map/ppermute | solution.py:48
  57.3 30.9 %collective-permute-start.10 = (bf16[2,2,2,32,896]{4,3,2,1,0:T(8,128)(2,1)S(1)}, bf16[2,2,2,32,896]{4,3,2,1,0:T(8,128)(2,1)S(1)}, u32[]{:S(2)}, u32[]{:S(2)}) collective-permute-start(bf16[2,2,2,32,896]{4,3,2,1,0:T(8,128)(2,1)S(1)} %pad_maximum_fusion.1), channel_id=1, source_target_pairs={{0,16},{16,0},{32,48},{48,32},{64,80},{80,64},{96,112},{112,96},{1... | collective-permute-start | bytes 1376264 | tf_op jit(solution)/shard_map/ppermute | solution.py:36
  66.3 49.1 %all-to-all-start.2 = ((bf16[8,32,896]{2,1,0:T(8,128)(2,1)}), bf16[8,32,896]{2,1,0:T(8,128)(2,1)S(1)}, u32[]{:S(2)}, u32[]{:S(2)}) async-start(bf16[8,32,896]{2,1,0:T(8,128)(2,1)} %bitcast.25), calls=%async_computation.2 | async-start | bytes 917504 | tf_op jit(solution)/shard_map/all_to_all | solution.py:23
  82.3 13.9 %collective-permute-start.7 = (bf16[2,4,2,64,256]{4,3,2,1,0:T(8,128)(2,1)S(1)}, bf16[2,4,2,64,256]{4,3,2,1,0:T(8,128)(2,1)S(1)}, u32[]{:S(2)}, u32[]{:S(2)}) collective-permute-start(bf16[2,4,2,64,256]{4,3,2,1,0:T(8,128)(2,1)S(1)} %fusion.69), channel_id=1, source_target_pairs={{0,1},{1,0},{2,3},{3,2},{4,5},{5,4},{6,7},{7,6},{8,9},{9,8},{10,11... | collective-permute-start | bytes 1572872 | tf_op jit(solution)/shard_map/ppermute | solution.py:36
  88.4 25.3 %collective-permute-start.11 = (bf16[8,2,32,896]{3,2,1,0:T(8,128)(2,1)S(1)}, bf16[8,2,32,896]{3,2,1,0:T(8,128)(2,1)S(1)}, u32[]{:S(2)}, u32[]{:S(2)}) collective-permute-start(bf16[8,2,32,896]{3,2,1,0:T(8,128)(2,1)S(1)} %bitcast.219), channel_id=1, source_target_pairs={{0,128},{16,144},{32,160},{48,176},{64,192},{80,208},{96,224},{112... | collective-permute-start | bytes 2752520 | tf_op jit(solution)/shard_map/ppermute | solution.py:44
  91.8 23.5 %collective-permute-start.12 = (bf16[8,2,32,896]{3,2,1,0:T(8,128)(2,1)S(1)}, bf16[8,2,32,896]{3,2,1,0:T(8,128)(2,1)S(1)}, u32[]{:S(2)}, u32[]{:S(2)}) collective-permute-start(bf16[8,2,32,896]{3,2,1,0:T(8,128)(2,1)S(1)} %bitcast.220), channel_id=1, source_target_pairs={{0,384},{16,400},{32,416},{48,432},{64,448},{80,464},{96,480},{112... | collective-permute-start | bytes 2752520 | tf_op jit(solution)/shard_map/ppermute | solution.py:45
  116.4 32.4 %all-to-all-start.3 = ((bf16[8,32,896]{2,1,0:T(8,128)(2,1)}), bf16[8,32,896]{2,1,0:T(8,128)(2,1)}, u32[]{:S(2)}, u32[]{:S(2)}) async-start(bf16[8,32,896]{2,1,0:T(8,128)(2,1)} %broadcast_in_dim.18), calls=%async_computation.3 | async-start | bytes 917504 | tf_op jit(solution)/shard_map/all_to_all | solution.py:23
  126.3 13.7 %collective-permute-start.15 = (bf16[4,2,32,896]{3,2,1,0:T(8,128)(2,1)S(1)}, bf16[4,2,32,896]{3,2,1,0:T(8,128)(2,1)S(1)}, u32[]{:S(2)}, u32[]{:S(2)}) collective-permute-start(bf16[4,2,32,896]{3,2,1,0:T(8,128)(2,1)S(1)} %slice.120), channel_id=1, source_target_pairs={{0,128},{16,144},{32,160},{48,176},{64,192},{80,208},{96,224},{112... | collective-permute-start | bytes 1376264 | tf_op jit(solution)/shard_map/ppermute | solution.py:47
  129.6 12.1 %collective-permute-start.16 = (bf16[4,2,32,896]{3,2,1,0:T(8,128)(2,1)S(1)}, bf16[4,2,32,896]{3,2,1,0:T(8,128)(2,1)S(1)}, u32[]{:S(2)}, u32[]{:S(2)}) collective-permute-start(bf16[4,2,32,896]{3,2,1,0:T(8,128)(2,1)S(1)} %slice.121), channel_id=1, source_target_pairs={{0,384},{16,400},{32,416},{48,432},{64,448},{80,464},{96,480},{112... | collective-permute-start | bytes 1376264 | tf_op jit(solution)/shard_map/ppermute | solution.py:48
  148.8 13.1 %collective-permute-start.8 = (bf16[8,32,896]{2,1,0:T(8,128)(2,1)}, bf16[8,32,896]{2,1,0:T(8,128)(2,1)S(1)}, u32[]{:S(2)}, u32[]{:S(2)}) collective-permute-start(bf16[8,32,896]{2,1,0:T(8,128)(2,1)} %all-to-all-done.3), channel_id=1, source_target_pairs={{0,128},{16,144},{32,160},{48,176},{64,192},{80,208},{96,224},{112... | collective-permute-start | bytes 1376264 | tf_op jit(solution)/shard_map/ppermute | solution.py:44
  152.0 11.5 %collective-permute-start.9 = (bf16[8,32,896]{2,1,0:T(8,128)(2,1)}, bf16[8,32,896]{2,1,0:T(8,128)(2,1)S(1)}, u32[]{:S(2)}, u32[]{:S(2)}) collective-permute-start(bf16[8,32,896]{2,1,0:T(8,128)(2,1)} %all-to-all-done.3), channel_id=1, source_target_pairs={{0,384},{16,400},{32,416},{48,432},{64,448},{80,464},{96,480},{112... | collective-permute-start | bytes 1376264 | tf_op jit(solution)/shard_map/ppermute | solution.py:45
  163.5 17.4 %collective-permute-start.13 = (bf16[4,32,896]{2,1,0:T(8,128)(2,1)S(1)}, bf16[4,32,896]{2,1,0:T(8,128)(2,1)S(1)}, u32[]{:S(2)}, u32[]{:S(2)}) collective-permute-start(bf16[4,32,896]{2,1,0:T(8,128)(2,1)S(1)} %slice.118), channel_id=1, source_target_pairs={{0,128},{16,144},{32,160},{48,176},{64,192},{80,208},{96,224},{112... | collective-permute-start | bytes 688136 | tf_op jit(solution)/shard_map/ppermute | solution.py:47
  166.4 14.6 %collective-permute-start.14 = (bf16[4,32,896]{2,1,0:T(8,128)(2,1)S(1)}, bf16[4,32,896]{2,1,0:T(8,128)(2,1)S(1)}, u32[]{:S(2)}, u32[]{:S(2)}) collective-permute-start(bf16[4,32,896]{2,1,0:T(8,128)(2,1)S(1)} %slice.119), channel_id=1, source_target_pairs={{0,384},{16,400},{32,416},{48,432},{64,448},{80,464},{96,480},{112... | collective-permute-start | bytes 688136 | tf_op jit(solution)/shard_map/ppermute | solution.py:48
  184.1 17.8 %all-to-all-start.4 = ((bf16[8,2,64,256]{3,2,1,0:T(8,128)(2,1)}), bf16[8,2,64,256]{3,2,1,0:T(8,128)(2,1)}, u32[]{:S(2)}, u32[]{:S(2)}) async-start(bf16[8,2,64,256]{3,2,1,0:T(8,128)(2,1)} %bitcast.227), calls=%async_computation.4 | async-start | bytes 1048576 | tf_op jit(solution)/shard_map/all_to_all | solution.py:23
  193.5 19.9 %copy-start.9 = (f32[256,896]{1,0:T(8,128)S(1)}, f32[256,896]{1,0:T(8,128)}, u32[]{:S(2)}) copy-start(f32[256,896]{1,0:T(8,128)} %convolution_add_fusion.7) | copy-start | bytes 2752516
  203.0 16.0 %collective-permute-start.17 = (f32[64,256]{1,0:T(8,128)S(1)}, f32[64,256]{1,0:T(8,128)S(1)}, u32[]{:S(2)}, u32[]{:S(2)}) collective-permute-start(f32[64,256]{1,0:T(8,128)S(1)} %select_bitcast_fusion.8), channel_id=1, source_target_pairs={{0,2},{1,3},{2,0},{3,1},{4,6},{5,7},{6,4},{7,5},{8,10},{9,11},{10,... | collective-permute-start | bytes 196616 | tf_op jit(solution)/shard_map/ppermute | solution.py:134
  (25 other events, 193.6 us)

commit v5 on v3

--- a/solution.py
+++ b/solution.py
@@ -10,6 +10,7 @@
     [x * ZL + (h * C + c) * 2 + k for c in range(C) for h in range(ZH) for k in range(2)]
     for x in range(X)
 ]
+YC_GROUPS = [[(y * ZH + h) * C + c for y in range(Y) for c in range(C)] for h in range(ZH)]
 Y_GROUPS = [[(y * ZH + h) * C + c for y in range(Y)] for h in range(ZH) for c in range(C)]
 C_GROUPS = [[(y * ZH + h) * C + c for c in range(C)] for y in range(Y) for h in range(ZH)]
 ZH_SWAP = [(t, t ^ C) for t in range(Y * ZH * C)]
@@ -45,25 +46,27 @@
     dp, tensor = lax.axis_index("dp"), lax.axis_index("tensor")
     x, z = dp // ZL, dp % ZL
 
+    copies = jnp.broadcast_to(down_weight[None], (X,) + down_weight.shape)
+    copies, out_grad, tokens, gate_pre, up_pre = lax.optimization_barrier(
+        (copies, out_grad, tokens, gate_pre, up_pre)
+    )
+    down_all = exchange(copies, "dp", X_GROUPS)
+
     both = jnp.stack([out_grad, tokens])
     both = pair(both, "tensor", ZH_SWAP, tensor // C % ZH, 1)
     grads_y = lax.all_gather(both[0], "tensor", axis_index_groups=Y_GROUPS)
 
-    down_all = gather(down_weight, "dp", X_GROUPS)
+    saved = jnp.stack([gate_pre, up_pre])
+    saved = pair(saved, "dp", [(d, d ^ 4) for d in range(X * ZL)], z // 4, 0)
+    saved, grads_y = lax.optimization_barrier((saved, grads_y))
+    saved = pair(saved, "dp", [(d, d ^ 2) for d in range(X * ZL)], z // 2 % 2, 1)
 
-    saved = jnp.stack([gate_pre, up_pre])
-    for dim, reach in enumerate((4, 2, 1)):
-        swap = [(d, d ^ reach) for d in range(X * ZL)]
-        if reach == 2:
-            saved, grads_y = lax.optimization_barrier((saved, grads_y))
-        if reach == 1:
-            saved, down_all, ahead = lax.optimization_barrier((saved, down_all, grads_y))
-        saved = pair(saved, "dp", swap, z // reach % 2, dim)
-    saved = saved.reshape(ZL, 2, toks, hid)
-
+    down_all, ahead = lax.optimization_barrier((down_all, grads_y))
     grads_x = exchange(ahead, "dp", X_GROUPS)
     grads_x = lax.all_gather(grads_x, "tensor", axis_index_groups=C_GROUPS)
     grads_x, saved = lax.optimization_barrier((grads_x, saved))
+    saved = pair(saved, "dp", [(d, d ^ 1) for d in range(X * ZL)], z % 2, 2)
+    saved = saved.reshape(ZL, 2, toks, hid)
     partial = sum(
         jnp.einsum(
             "nd,fd->nf",
@@ -92,9 +95,8 @@
     hidden = gather(hidden, "dp", Z_GROUPS)
     hidden = gather(hidden, "dp", X_GROUPS).reshape(n, hid).astype(jnp.float32)
 
-    full = jnp.zeros((X,) + saved.shape, saved.dtype)
+    full = jnp.broadcast_to(saved[None], (X,) + saved.shape)
     for block, start, half in (
-        (saved, x, 0),
         (from_down, (x + X - 1) % X, 0),
         (from_up, (x + 1) % X, 0),
         (far_low, (x + 2) % X, 0),
@@ -116,9 +118,9 @@
     partial_in = jnp.einsum(
         "nf,df->nd", gate_grad, gate_weight, preferred_element_type=jnp.float32
     ) + jnp.einsum("nf,df->nd", up_grad, up_weight, preferred_element_type=jnp.float32)
-    partial_in = partial_in.reshape(Y * ZH, C, rows, feats).transpose(1, 0, 2, 3)
-    partial_in = add_up(partial_in, "tensor", C_GROUPS).astype(jnp.bfloat16)
-    partial_in = add_up(partial_in.reshape(Y, ZH, rows, feats), "tensor", Y_GROUPS)
+    partial_in = partial_in.reshape(Y, ZH, C, rows, feats).astype(jnp.bfloat16)
+    partial_in = partial_in.swapaxes(1, 2).reshape(Y * C, ZH, rows, feats)
+    partial_in = add_up(partial_in, "tensor", YC_GROUPS)
     upper = tensor // C % ZH == 1
     sent = jnp.where(upper, partial_in[0], partial_in[1])
     kept = jnp.where(upper, partial_in[1], partial_in[0])

time: 205 us -> 205 us (level)
  the two profiles are of different devices: /device:TPU:33 before, /device:TPU:416 now
where the time goes in v5:
time: 205 us; the launch traced here: 204 us
  starting transfers between devices  69.6 us (34%)
  waiting for transfers between devices  61.3 us (30%)
  blocking collectives  27.9 us (14%)
  other arithmetic  19 us (9%)
  local copies, waits for them, and re-layouts  15.6 us (8%)
  matrix products  9.54 us (5%)
    all_to_all x6, starting transfers between devices, exchange(): lax.all_to_all(blocks, axis, 0, 0, axis_index_groups=groups, tiled=True)  39.2 us
    ppermute x5, waiting for transfers between devices, pair(): other = lax.ppermute(block, axis, perm)  22 us
    all_to_all x6, waiting for transfers between devices, exchange(): lax.all_to_all(blocks, axis, 0, 0, axis_index_groups=groups, tiled=True)  20.6 us
    ppermute x5, starting transfers between devices, pair(): other = lax.ppermute(block, axis, perm)  14.3 us
    all_gather x1, blocking collectives, on_device(): grads_y = lax.all_gather(both[0], 'tensor', axis_index_groups=Y_GROUPS)  13.5 us
    all_gather x1, blocking collectives, on_device(): tokens_y = lax.all_gather(inputs, 'tensor', axis_index_groups=Y_GROUPS)  12.3 us
    ppermute x1, waiting for transfers between devices, on_device(): lax.ppermute(sent, 'tensor', ZH_SWAP)  10.4 us
    ppermute x1, waiting for transfers between devices, on_device(): from_down = lax.ppermute(saved, 'dp', X_UP)  7.96 us
  transfers between devices with their start and end apart: 16, of which 9 were waited for; matrix products, arithmetic and copies ran while one was open for 16% of the time, Pallas kernels for 0%

profile of v5, /device:TPU:416, one launch (start us, length us, event | category | flops | bytes accessed | tf_op | source)
XLA Modules:
  0.0 204.1 jit_solution(6240858953339739532)
XLA Ops:
  3.1 4.3 %all-to-all-start = ((bf16[4,896,256]{2,1,0:T(8,128)(2,1)}), bf16[4,896,256]{2,1,0:T(8,128)(2,1)S(1)}, u32[]{:S(2)}, u32[]{:S(2)}) async-start(bf16[4,896,256]{2,1,0:T(8,128)(2,1)} %broadcast_in_dim.18), calls=%async_computation | async-start | bytes 3670016 | tf_op jit(solution)/shard_map/all_to_all | solution.py:23
  7.4 4.5 %collective-permute-start.1 = (bf16[2,64,256]{2,1,0:T(8,128)(2,1)S(1)}, bf16[2,64,256]{2,1,0:T(8,128)(2,1)S(1)}, u32[]{:S(2)}, u32[]{:S(2)}) collective-permute-start(bf16[2,64,256]{2,1,0:T(8,128)(2,1)S(1)} %pad_maximum_fusion.7), channel_id=1, source_target_pairs={{0,2},{1,3},{2,0},{3,1},{4,6},{5,7},{6,4},{7,5},{8,10},{9,11},{10,... | collective-permute-start | bytes 196616 | tf_op jit(solution)/shard_map/ppermute | solution.py:36
  12.0 2.8 %collective-permute-start = (bf16[2,32,896]{2,1,0:T(8,128)(2,1)S(1)}, bf16[2,32,896]{2,1,0:T(8,128)(2,1)S(1)}, u32[]{:S(2)}, u32[]{:S(2)}) collective-permute-start(bf16[2,32,896]{2,1,0:T(8,128)(2,1)S(1)} %pad_maximum_fusion.5), channel_id=1, source_target_pairs={{0,64},{16,80},{32,96},{48,112},{64,0},{80,16},{96,32},{112,48},{1... | collective-permute-start | bytes 344072 | tf_op jit(solution)/shard_map/ppermute | solution.py:36
  14.9 9.0 %collective-permute-done.1 = bf16[2,64,256]{2,1,0:T(8,128)(2,1)S(1)} collective-permute-done((bf16[2,64,256]{2,1,0:T(8,128)(2,1)S(1)}, bf16[2,64,256]{2,1,0:T(8,128)(2,1)S(1)}, u32[]{:S(2)}, u32[]{:S(2)}) %collective-permute-start.1) | collective-permute-done | bytes 65568 | tf_op jit(solution)/shard_map/ppermute | solution.py:36
  23.9 13.5 %all_gather.15 = bf16[4,2,64,256]{3,2,1,0:T(8,128)(2,1)} all-gather(bf16[1,2,64,256]{3,2,1,0:T(8,128)(2,1)S(1)} %get-tuple-element.46), channel_id=1, replica_groups={{0,4,8,12},{1,5,9,13},{2,6,10,14},{3,7,11,15},{16,20,24,28},{17,21,25,2..., dimensions={0}, use_global_device_ids=true | all-gather | bytes 327680 | tf_op jit(solution)/shard_map/all_gather | solution.py:57
  40.2 4.3 %all-to-all-start.1 = ((bf16[4,2,64,256]{3,2,1,0:T(8,128)(2,1)}), bf16[4,2,64,256]{3,2,1,0:T(8,128)(2,1)S(1)}, u32[]{:S(2)}, u32[]{:S(2)}) async-start(bf16[4,2,64,256]{3,2,1,0:T(8,128)(2,1)} %all_gather.15), calls=%async_computation.1 | async-start | bytes 524288 | tf_op jit(solution)/shard_map/all_to_all | solution.py:23
  46.6 4.6 %all-to-all-done.1 = bf16[4,2,64,256]{3,2,1,0:T(8,128)(2,1)S(1)} async-done(((bf16[4,2,64,256]{3,2,1,0:T(8,128)(2,1)}), bf16[4,2,64,256]{3,2,1,0:T(8,128)(2,1)S(1)}, u32[]{:S(2)}, u32[]{:S(2)}) %all-to-all-start.1) | async-done | bytes 262176 | tf_op jit(solution)/shard_map/all_to_all | solution.py:23
  55.5 14.9 %all-to-all-start.2 = ((bf16[8,32,896]{2,1,0:T(8,128)(2,1)}), bf16[8,32,896]{2,1,0:T(8,128)(2,1)S(1)}, u32[]{:S(2)}, u32[]{:S(2)}) async-start(bf16[8,32,896]{2,1,0:T(8,128)(2,1)} %bitcast.28), calls=%async_computation.2 | async-start | bytes 917504 | tf_op jit(solution)/shard_map/all_to_all | solution.py:23
  72.9 12.3 %all-gather.1 = bf16[8,64,256]{2,1,0:T(8,128)(2,1)S(1)} all-gather(bf16[2,64,256]{2,1,0:T(8,128)(2,1)S(1)} %get-tuple-element.26), channel_id=3, replica_groups={{0,4,8,12},{1,5,9,13},{2,6,10,14},{3,7,11,15},{16,20,24,28},{17,21,25,2..., dimensions={0}, use_global_device_ids=true | all-gather | bytes 327680 | tf_op jit(solution)/shard_map/all_gather | solution.py:81
  88.8 11.1 %collective-permute-done.4 = bf16[2,2,2,32,896]{4,3,2,1,0:T(8,128)(2,1)S(1)} collective-permute-done((bf16[2,2,2,32,896]{4,3,2,1,0:T(8,128)(2,1)S(1)}, bf16[2,2,2,32,896]{4,3,2,1,0:T(8,128)(2,1)S(1)}, u32[]{:S(2)}, u32[]{:S(2)}) %collective-permute-start.4) | collective-permute-done | bytes 458784 | tf_op jit(solution)/shard_map/ppermute | solution.py:36
  102.6 4.6 %collective-permute-start.6 = (bf16[8,2,32,896]{3,2,1,0:T(8,128)(2,1)S(1)}, bf16[8,2,32,896]{3,2,1,0:T(8,128)(2,1)}, u32[]{:S(2)}, u32[]{:S(2)}) collective-permute-start(bf16[8,2,32,896]{3,2,1,0:T(8,128)(2,1)S(1)} %bitcast.160), channel_id=1, source_target_pairs={{0,384},{16,400},{32,416},{48,432},{64,448},{80,464},{96,480},{112... | collective-permute-start | bytes 2752520 | tf_op jit(solution)/shard_map/ppermute | solution.py:88
  108.1 8.3 %all-to-all-start.3 = ((bf16[8,32,896]{2,1,0:T(8,128)(2,1)}), bf16[8,32,896]{2,1,0:T(8,128)(2,1)S(1)}, u32[]{:S(2)}, u32[]{:S(2)}) async-start(bf16[8,32,896]{2,1,0:T(8,128)(2,1)} %broadcast_in_dim.38), calls=%async_computation.3 | async-start | bytes 917504 | tf_op jit(solution)/shard_map/all_to_all | solution.py:23
  117.5 8.0 %collective-permute-done.5 = bf16[8,2,32,896]{3,2,1,0:T(8,128)(2,1)S(1)} collective-permute-done((bf16[8,2,32,896]{3,2,1,0:T(8,128)(2,1)S(1)}, bf16[8,2,32,896]{3,2,1,0:T(8,128)(2,1)S(1)}, u32[]{:S(2)}, u32[]{:S(2)}) %collective-permute-start.5) | collective-permute-done | bytes 917536 | tf_op jit(solution)/shard_map/ppermute | solution.py:87
  129.3 5.1 %collective-permute-start.8 = (bf16[4,2,32,896]{3,2,1,0:T(8,128)(2,1)}, bf16[4,2,32,896]{3,2,1,0:T(8,128)(2,1)}, u32[]{:S(2)}, u32[]{:S(2)}) collective-permute-start(bf16[4,2,32,896]{3,2,1,0:T(8,128)(2,1)} %slice.81), channel_id=1, source_target_pairs={{0,384},{16,400},{32,416},{48,432},{64,448},{80,464},{96,480},{112... | collective-permute-start | bytes 1376264 | tf_op jit(solution)/shard_map/ppermute | solution.py:93
  142.5 3.6 %all-to-all-start.4 = ((bf16[4,8,32,896]{3,2,1,0:T(8,128)(2,1)}), bf16[4,8,32,896]{3,2,1,0:T(8,128)(2,1)S(1)}, u32[]{:S(2)}, u32[]{:S(2)}) async-start(bf16[4,8,32,896]{3,2,1,0:T(8,128)(2,1)} %broadcast_in_dim.39), calls=%async_computation.4 | async-start | bytes 3670016 | tf_op jit(solution)/shard_map/all_to_all | solution.py:23
  148.0 3.2 %fusion.25 = bf16[4,8,1,32,896]{4,3,2,1,0:T(8,128)(2,1)S(1)} fusion(bf16[4,8,2,32,896]{4,3,2,1,0:T(8,128)(2,1)} %bitcast_dynamic-update-slice_fusion.2), kind=kLoop, calls=%fused_computation.33 | loop fusion | flops 7340032 | bytes 5505024 | tf_op jit(solution)/shard_map/convert_element_type | solution.py:112
  152.8 3.8 %slice_convert_fusion = f32[4,8,1,32,896]{4,3,2,1,0:T(8,128)} fusion(bf16[4,8,2,32,896]{4,3,2,1,0:T(8,128)(2,1)} %bitcast_dynamic-update-slice_fusion.2), kind=kLoop, calls=%fused_computation.34 | loop fusion | flops 917504 | bytes 5505024 | tf_op jit(solution)/shard_map/convert_element_type | solution.py:110
  156.6 11.7 %all-to-all-done.4 = bf16[4,8,32,896]{3,2,1,0:T(8,128)(2,1)S(1)} async-done(((bf16[4,8,32,896]{3,2,1,0:T(8,128)(2,1)}), bf16[4,8,32,896]{3,2,1,0:T(8,128)(2,1)S(1)}, u32[]{:S(2)}, u32[]{:S(2)}) %all-to-all-start.4) | async-done | bytes 1835040 | tf_op jit(solution)/shard_map/all_to_all | solution.py:23
  168.3 3.6 %fusion.20 = (bf16[1024,896]{1,0:T(8,128)(2,1)S(1)}, bf16[1024,896]{1,0:T(8,128)(2,1)S(1)}) fusion(f32[4,8,1,32,896]{4,3,2,1,0:T(8,128)} %slice_convert_fusion, bf16[4,8,32,896]{3,2,1,0:T(8,128)(2,1)S(1)} %all-to-all-done.4, bf16[4,8,2,32,896]{4,3,2,1,0:T(8,128)(2,1)} %bitcast_dynamic-update-slice_fusion.2), kind=kLoop, calls=%fused_computation.26 | loop fusion | flops 13762560 | bytes 11010048 | tf_op jit(solution)/shard_map/convert_element_type | solution.py:115
  174.3 3.8 %all-to-all-start.5 = ((bf16[8,2,64,256]{3,2,1,0:T(8,128)(2,1)}), bf16[8,2,64,256]{3,2,1,0:T(8,128)(2,1)S(1)}, u32[]{:S(2)}, u32[]{:S(2)}) async-start(bf16[8,2,64,256]{3,2,1,0:T(8,128)(2,1)} %bitcast.48), calls=%async_computation.5 | async-start | bytes 1048576 | tf_op jit(solution)/shard_map/all_to_all | solution.py:23
  178.0 4.4 %fusion.10 = (bf16[4,8,32,896]{3,2,1,0:T(8,128)(2,1)S(1)}, bf16[4,8,32,896]{3,2,1,0:T(8,128)(2,1)}) fusion(bf16[4,8,32,896]{3,2,1,0:T(8,128)(2,1)S(1)} %all-to-all-done.4, bf16[4,8,2,32,896]{4,3,2,1,0:T(8,128)(2,1)} %bitcast_dynamic-update-slice_fusion.2), kind=kLoop, calls=%fused_computation.16 | loop fusion | flops 14680064 | bytes 9175040 | tf_op jit(solution)/shard_map/convert_element_type | solution.py:116
  184.1 4.3 %all-to-all-done.5 = bf16[8,2,64,256]{3,2,1,0:T(8,128)(2,1)S(1)} async-done(((bf16[8,2,64,256]{3,2,1,0:T(8,128)(2,1)}), bf16[8,2,64,256]{3,2,1,0:T(8,128)(2,1)S(1)}, u32[]{:S(2)}, u32[]{:S(2)}) %all-to-all-start.5) | async-done | bytes 524320 | tf_op jit(solution)/shard_map/all_to_all | solution.py:23
  190.4 2.7 %fusion.28 = f32[256,896]{1,0:T(8,128)} fusion(bf16[1024,256]{1,0:T(8,128)(2,1)S(1)} %bitcast.158, bf16[1024,896]{1,0:T(8,128)(2,1)S(1)} %bitcast.155, bf16[256,896]{1,0:T(8,128)(2,1)} %param.11), kind=kOutput, calls=%fused_computation.41 | convolution fusion | flops 470450176 | bytes 3735552 | tf_op jit(solution)/shard_map/nd,nf->df/dot_general | solution.py:130
  193.1 10.4 %collective-permute-done.9 = f32[64,256]{1,0:T(8,128)S(1)} collective-permute-done((f32[64,256]{1,0:T(8,128)S(1)}, f32[64,256]{1,0:T(8,128)S(1)}, u32[]{:S(2)}, u32[]{:S(2)}) %collective-permute-start.9) | collective-permute-done | bytes 65568 | tf_op jit(solution)/shard_map/ppermute | solution.py:127
  (69 shorter events, 44.3 us)
Async XLA Ops:
  0.6 11.3 %copy-start.4 = (bf16[32,896]{1,0:T(8,128)(2,1)S(1)}, bf16[32,896]{1,0:T(8,128)(2,1)}, u32[]{:S(2)}) copy-start(bf16[32,896]{1,0:T(8,128)(2,1)} %param.10) | copy-start | bytes 172036
  0.6 6.7 %copy-start.6 = (bf16[64,256]{1,0:T(8,128)(2,1)S(1)}, bf16[64,256]{1,0:T(8,128)(2,1)}, u32[]{:S(2)}) copy-start(bf16[64,256]{1,0:T(8,128)(2,1)} %param.7) | copy-start | bytes 98308
  0.7 6.7 %copy-start.7 = (bf16[64,256]{1,0:T(8,128)(2,1)S(1)}, bf16[64,256]{1,0:T(8,128)(2,1)}, u32[]{:S(2)}) copy-start(bf16[64,256]{1,0:T(8,128)(2,1)} %param.8) | copy-start | bytes 98308
  0.7 11.3 %copy-start.5 = (bf16[32,896]{1,0:T(8,128)(2,1)S(1)}, bf16[32,896]{1,0:T(8,128)(2,1)}, u32[]{:S(2)}) copy-start(bf16[32,896]{1,0:T(8,128)(2,1)} %param.9) | copy-start | bytes 172036
  3.1 37.1 %all-to-all-start = ((bf16[4,896,256]{2,1,0:T(8,128)(2,1)}), bf16[4,896,256]{2,1,0:T(8,128)(2,1)S(1)}, u32[]{:S(2)}, u32[]{:S(2)}) async-start(bf16[4,896,256]{2,1,0:T(8,128)(2,1)} %broadcast_in_dim.18), calls=%async_computation | async-start | bytes 3670016 | tf_op jit(solution)/shard_map/all_to_all | solution.py:23
  7.4 16.5 %collective-permute-start.1 = (bf16[2,64,256]{2,1,0:T(8,128)(2,1)S(1)}, bf16[2,64,256]{2,1,0:T(8,128)(2,1)S(1)}, u32[]{:S(2)}, u32[]{:S(2)}) collective-permute-start(bf16[2,64,256]{2,1,0:T(8,128)(2,1)S(1)} %pad_maximum_fusion.7), channel_id=1, source_target_pairs={{0,2},{1,3},{2,0},{3,1},{4,6},{5,7},{6,4},{7,5},{8,10},{9,11},{10,... | collective-permute-start | bytes 196616 | tf_op jit(solution)/shard_map/ppermute | solution.py:36
  12.0 25.5 %collective-permute-start = (bf16[2,32,896]{2,1,0:T(8,128)(2,1)S(1)}, bf16[2,32,896]{2,1,0:T(8,128)(2,1)S(1)}, u32[]{:S(2)}, u32[]{:S(2)}) collective-permute-start(bf16[2,32,896]{2,1,0:T(8,128)(2,1)S(1)} %pad_maximum_fusion.5), channel_id=1, source_target_pairs={{0,64},{16,80},{32,96},{48,112},{64,0},{80,16},{96,32},{112,48},{1... | collective-permute-start | bytes 344072 | tf_op jit(solution)/shard_map/ppermute | solution.py:36
  37.5 8.9 %collective-permute-start.2 = (bf16[2,2,32,896]{3,2,1,0:T(8,128)(2,1)S(1)}, bf16[2,2,32,896]{3,2,1,0:T(8,128)(2,1)S(1)}, u32[]{:S(2)}, u32[]{:S(2)}) collective-permute-start(bf16[2,2,32,896]{3,2,1,0:T(8,128)(2,1)S(1)} %pad_maximum_fusion.4), channel_id=1, source_target_pairs={{0,32},{16,48},{32,0},{48,16},{64,96},{80,112},{96,64},{112,80},{1... | collective-permute-start | bytes 688136 | tf_op jit(solution)/shard_map/ppermute | solution.py:36
  40.2 11.0 %all-to-all-start.1 = ((bf16[4,2,64,256]{3,2,1,0:T(8,128)(2,1)}), bf16[4,2,64,256]{3,2,1,0:T(8,128)(2,1)S(1)}, u32[]{:S(2)}, u32[]{:S(2)}) async-start(bf16[4,2,64,256]{3,2,1,0:T(8,128)(2,1)} %all_gather.15), calls=%async_computation.1 | async-start | bytes 524288 | tf_op jit(solution)/shard_map/all_to_all | solution.py:23
  55.5 51.7 %all-to-all-start.2 = ((bf16[8,32,896]{2,1,0:T(8,128)(2,1)}), bf16[8,32,896]{2,1,0:T(8,128)(2,1)S(1)}, u32[]{:S(2)}, u32[]{:S(2)}) async-start(bf16[8,32,896]{2,1,0:T(8,128)(2,1)} %bitcast.28), calls=%async_computation.2 | async-start | bytes 917504 | tf_op jit(solution)/shard_map/all_to_all | solution.py:23
  70.4 29.5 %collective-permute-start.4 = (bf16[2,2,2,32,896]{4,3,2,1,0:T(8,128)(2,1)S(1)}, bf16[2,2,2,32,896]{4,3,2,1,0:T(8,128)(2,1)S(1)}, u32[]{:S(2)}, u32[]{:S(2)}) collective-permute-start(bf16[2,2,2,32,896]{4,3,2,1,0:T(8,128)(2,1)S(1)} %pad_maximum_fusion.3), channel_id=1, source_target_pairs={{0,16},{16,0},{32,48},{48,32},{64,80},{80,64},{96,112},{112,96},{1... | collective-permute-start | bytes 1376264 | tf_op jit(solution)/shard_map/ppermute | solution.py:36
  86.9 29.5 %collective-permute-start.3 = (bf16[2,8,64,256]{3,2,1,0:T(8,128)(2,1)}, bf16[2,8,64,256]{3,2,1,0:T(8,128)(2,1)S(1)}, u32[]{:S(2)}, u32[]{:S(2)}) collective-permute-start(bf16[2,8,64,256]{3,2,1,0:T(8,128)(2,1)} %pad_maximum_fusion.2), channel_id=1, source_target_pairs={{0,1},{1,0},{2,3},{3,2},{4,5},{5,4},{6,7},{7,6},{8,9},{9,8},{10,11... | collective-permute-start | bytes 1572872 | tf_op jit(solution)/shard_map/ppermute | solution.py:36
  100.1 25.4 %collective-permute-start.5 = (bf16[8,2,32,896]{3,2,1,0:T(8,128)(2,1)S(1)}, bf16[8,2,32,896]{3,2,1,0:T(8,128)(2,1)S(1)}, u32[]{:S(2)}, u32[]{:S(2)}) collective-permute-start(bf16[8,2,32,896]{3,2,1,0:T(8,128)(2,1)S(1)} %bitcast.159), channel_id=1, source_target_pairs={{0,128},{16,144},{32,160},{48,176},{64,192},{80,208},{96,224},{112... | collective-permute-start | bytes 2752520 | tf_op jit(solution)/shard_map/ppermute | solution.py:87
  102.6 24.9 %collective-permute-start.6 = (bf16[8,2,32,896]{3,2,1,0:T(8,128)(2,1)S(1)}, bf16[8,2,32,896]{3,2,1,0:T(8,128)(2,1)}, u32[]{:S(2)}, u32[]{:S(2)}) collective-permute-start(bf16[8,2,32,896]{3,2,1,0:T(8,128)(2,1)S(1)} %bitcast.160), channel_id=1, source_target_pairs={{0,384},{16,400},{32,416},{48,432},{64,448},{80,464},{96,480},{112... | collective-permute-start | bytes 2752520 | tf_op jit(solution)/shard_map/ppermute | solution.py:88
  108.1 33.0 %all-to-all-start.3 = ((bf16[8,32,896]{2,1,0:T(8,128)(2,1)}), bf16[8,32,896]{2,1,0:T(8,128)(2,1)S(1)}, u32[]{:S(2)}, u32[]{:S(2)}) async-start(bf16[8,32,896]{2,1,0:T(8,128)(2,1)} %broadcast_in_dim.38), calls=%async_computation.3 | async-start | bytes 917504 | tf_op jit(solution)/shard_map/all_to_all | solution.py:23
  125.5 14.7 %collective-permute-start.7 = (bf16[4,2,32,896]{3,2,1,0:T(8,128)(2,1)S(1)}, bf16[4,2,32,896]{3,2,1,0:T(8,128)(2,1)S(1)}, u32[]{:S(2)}, u32[]{:S(2)}) collective-permute-start(bf16[4,2,32,896]{3,2,1,0:T(8,128)(2,1)S(1)} %slice.80), channel_id=1, source_target_pairs={{0,128},{16,144},{32,160},{48,176},{64,192},{80,208},{96,224},{112... | collective-permute-start | bytes 1376264 | tf_op jit(solution)/shard_map/ppermute | solution.py:92
  129.3 16.8 %collective-permute-start.8 = (bf16[4,2,32,896]{3,2,1,0:T(8,128)(2,1)}, bf16[4,2,32,896]{3,2,1,0:T(8,128)(2,1)}, u32[]{:S(2)}, u32[]{:S(2)}) collective-permute-start(bf16[4,2,32,896]{3,2,1,0:T(8,128)(2,1)} %slice.81), channel_id=1, source_target_pairs={{0,384},{16,400},{32,416},{48,432},{64,448},{80,464},{96,480},{112... | collective-permute-start | bytes 1376264 | tf_op jit(solution)/shard_map/ppermute | solution.py:93
  142.5 25.8 %all-to-all-start.4 = ((bf16[4,8,32,896]{3,2,1,0:T(8,128)(2,1)}), bf16[4,8,32,896]{3,2,1,0:T(8,128)(2,1)S(1)}, u32[]{:S(2)}, u32[]{:S(2)}) async-start(bf16[4,8,32,896]{3,2,1,0:T(8,128)(2,1)} %broadcast_in_dim.39), calls=%async_computation.4 | async-start | bytes 3670016 | tf_op jit(solution)/shard_map/all_to_all | solution.py:23
  146.1 5.1 %copy-start.3 = (bf16[896,256]{1,0:T(8,128)(2,1)S(1)}, bf16[896,256]{1,0:T(8,128)(2,1)}, u32[]{:S(2)}) copy-start(bf16[896,256]{1,0:T(8,128)(2,1)} %param.13) | copy-start | bytes 1376260
  156.6 15.3 %copy-start.1 = (bf16[256,896]{1,0:T(8,128)(2,1)S(1)}, bf16[256,896]{1,0:T(8,128)(2,1)}, u32[]{:S(2)}) copy-start(bf16[256,896]{1,0:T(8,128)(2,1)} %param.12) | copy-start | bytes 1376260
  156.6 16.1 %copy-start.2 = (bf16[256,896]{1,0:T(8,128)(2,1)S(1)}, bf16[256,896]{1,0:T(8,128)(2,1)}, u32[]{:S(2)}) copy-start(bf16[256,896]{1,0:T(8,128)(2,1)} %param.11) | copy-start | bytes 1376260
  174.3 14.1 %all-to-all-start.5 = ((bf16[8,2,64,256]{3,2,1,0:T(8,128)(2,1)}), bf16[8,2,64,256]{3,2,1,0:T(8,128)(2,1)S(1)}, u32[]{:S(2)}, u32[]{:S(2)}) async-start(bf16[8,2,64,256]{3,2,1,0:T(8,128)(2,1)} %bitcast.48), calls=%async_computation.5 | async-start | bytes 1048576 | tf_op jit(solution)/shard_map/all_to_all | solution.py:23
  182.4 8.0 %copy-start = (bf16[4,8,32,896]{3,2,1,0:T(8,128)(2,1)S(1)}, bf16[4,8,32,896]{3,2,1,0:T(8,128)(2,1)}, u32[]{:S(2)}) copy-start(bf16[4,8,32,896]{3,2,1,0:T(8,128)(2,1)} %get-tuple-element.31) | copy-start | bytes 5505028
  188.5 15.0 %collective-permute-start.9 = (f32[64,256]{1,0:T(8,128)S(1)}, f32[64,256]{1,0:T(8,128)S(1)}, u32[]{:S(2)}, u32[]{:S(2)}) collective-permute-start(f32[64,256]{1,0:T(8,128)S(1)} %select_bitcast_fusion.8), channel_id=1, source_target_pairs={{0,2},{1,3},{2,0},{3,1},{4,6},{5,7},{6,4},{7,5},{8,10},{9,11},{10,... | collective-permute-start | bytes 196616 | tf_op jit(solution)/shard_map/ppermute | solution.py:127

commit v6 on v5

--- a/solution.py
+++ b/solution.py
@@ -10,6 +10,7 @@
     [x * ZL + (h * C + c) * 2 + k for c in range(C) for h in range(ZH) for k in range(2)]
     for x in range(X)
 ]
+ZH_GROUPS = [[(y * ZH + h) * C + c for h in range(ZH)] for y in range(Y) for c in range(C)]
 YC_GROUPS = [[(y * ZH + h) * C + c for y in range(Y) for c in range(C)] for h in range(ZH)]
 Y_GROUPS = [[(y * ZH + h) * C + c for y in range(Y)] for h in range(ZH) for c in range(C)]
 C_GROUPS = [[(y * ZH + h) * C + c for c in range(C)] for y in range(Y) for h in range(ZH)]
@@ -52,21 +53,21 @@
     )
     down_all = exchange(copies, "dp", X_GROUPS)
 
-    both = jnp.stack([out_grad, tokens])
-    both = pair(both, "tensor", ZH_SWAP, tensor // C % ZH, 1)
-    grads_y = lax.all_gather(both[0], "tensor", axis_index_groups=Y_GROUPS)
-
     saved = jnp.stack([gate_pre, up_pre])
     saved = pair(saved, "dp", [(d, d ^ 4) for d in range(X * ZL)], z // 4, 0)
-    saved, grads_y = lax.optimization_barrier((saved, grads_y))
+
+    both = jnp.stack([out_grad, tokens])
+    both = lax.all_gather(both, "tensor", axis_index_groups=ZH_GROUPS, axis=1)
+    saved, both = lax.optimization_barrier((saved, both))
     saved = pair(saved, "dp", [(d, d ^ 2) for d in range(X * ZL)], z // 2 % 2, 1)
+    grads_y = lax.all_gather(both[0], "tensor", axis_index_groups=Y_GROUPS)
+    down_all, grads_y, saved = lax.optimization_barrier((down_all, grads_y, saved))
+    saved = pair(saved, "dp", [(d, d ^ 1) for d in range(X * ZL)], z % 2, 2)
+    saved = saved.reshape(ZL, 2, toks, hid)
 
-    down_all, ahead = lax.optimization_barrier((down_all, grads_y))
-    grads_x = exchange(ahead, "dp", X_GROUPS)
+    grads_x = exchange(grads_y, "dp", X_GROUPS)
     grads_x = lax.all_gather(grads_x, "tensor", axis_index_groups=C_GROUPS)
     grads_x, saved = lax.optimization_barrier((grads_x, saved))
-    saved = pair(saved, "dp", [(d, d ^ 1) for d in range(X * ZL)], z % 2, 2)
-    saved = saved.reshape(ZL, 2, toks, hid)
     partial = sum(
         jnp.einsum(
             "nd,fd->nf",

time: 205 us -> 207 us (level)
  the two profiles are of different devices: /device:TPU:416 before, /device:TPU:160 now
where the time goes in v6:
time: 207 us; the launch traced here: 206 us
  starting transfers between devices  68.2 us (33%)
  blocking collectives  52.4 us (25%)
  waiting for transfers between devices  37.3 us (18%)
  other arithmetic  19 us (9%)
  local copies, waits for them, and re-layouts  18.5 us (9%)
  matrix products  9.51 us (5%)
    all_to_all x6, starting transfers between devices, exchange(): lax.all_to_all(blocks, axis, 0, 0, axis_index_groups=groups, tiled=True)  37.6 us
    all_gather x1, blocking collectives, on_device(): both = lax.all_gather(both, 'tensor', axis_index_groups=ZH_GROUPS, axis=1)  24.5 us
    all_to_all x6, waiting for transfers between devices, exchange(): lax.all_to_all(blocks, axis, 0, 0, axis_index_groups=groups, tiled=True)  23.5 us
    all_gather x1, blocking collectives, on_device(): grads_y = lax.all_gather(both[0], 'tensor', axis_index_groups=Y_GROUPS)  13.5 us
    all_gather x1, blocking collectives, on_device(): tokens_y = lax.all_gather(inputs, 'tensor', axis_index_groups=Y_GROUPS)  12.2 us
    ppermute x1, starting transfers between devices, on_device(): lax.ppermute(sent, 'tensor', ZH_SWAP)  8.83 us
    ppermute x4, starting transfers between devices, pair(): other = lax.ppermute(block, axis, perm)  7.68 us
    ppermute x1, waiting for transfers between devices, on_device(): lax.ppermute(sent, 'tensor', ZH_SWAP)  7.56 us
  transfers between devices with their start and end apart: 15, of which 5 were waited for; matrix products, arithmetic and copies ran while one was open for 17% of the time, Pallas kernels for 0%

profile of v6, /device:TPU:160, one launch (start us, length us, event | category | flops | bytes accessed | tf_op | source)
XLA Modules:
  0.0 205.9 jit_solution(15936686612545374434)
XLA Ops:
  0.7 2.4 %broadcast_in_dim.16 = bf16[4,896,256]{2,1,0:T(8,128)(2,1)} broadcast(bf16[896,256]{1,0:T(8,128)(2,1)} %param.13), dimensions={1,2} | broadcast | bytes 2293760 | tf_op jit(solution)/shard_map/broadcast_in_dim | solution.py:50
  3.1 4.3 %all-to-all-start = ((bf16[4,896,256]{2,1,0:T(8,128)(2,1)}), bf16[4,896,256]{2,1,0:T(8,128)(2,1)S(1)}, u32[]{:S(2)}, u32[]{:S(2)}) async-start(bf16[4,896,256]{2,1,0:T(8,128)(2,1)} %broadcast_in_dim.16), calls=%async_computation | async-start | bytes 3670016 | tf_op jit(solution)/shard_map/all_to_all | solution.py:24
  9.4 24.5 %all-gather = bf16[2,128,256]{2,1,0:T(8,128)(2,1)S(1)} all-gather(bf16[2,64,256]{2,1,0:T(8,128)(2,1)S(1)} %pad_maximum_fusion.6), channel_id=2, replica_groups={{0,2},{1,3},{4,6},{5,7},{8,10},{9,11},{12,14},{13,15},{16,18},{17,19},{..., dimensions={1}, use_global_device_ids=true | all-gather | bytes 196608 | tf_op jit(solution)/shard_map/all_gather | solution.py:60
  36.6 13.5 %all_gather.23 = bf16[4,2,64,256]{3,2,1,0:T(8,128)(2,1)} all-gather(bf16[1,2,64,256]{3,2,1,0:T(8,128)(2,1)S(1)} %get-tuple-element.48), channel_id=1, replica_groups={{0,4,8,12},{1,5,9,13},{2,6,10,14},{3,7,11,15},{16,20,24,28},{17,21,25,2..., dimensions={0}, use_global_device_ids=true | all-gather | bytes 327680 | tf_op jit(solution)/shard_map/all_gather | solution.py:63
  52.2 4.5 %all-to-all-start.1 = ((bf16[4,2,64,256]{3,2,1,0:T(8,128)(2,1)}), bf16[4,2,64,256]{3,2,1,0:T(8,128)(2,1)S(1)}, u32[]{:S(2)}, u32[]{:S(2)}) async-start(bf16[4,2,64,256]{3,2,1,0:T(8,128)(2,1)} %all_gather.23), calls=%async_computation.1 | async-start | bytes 524288 | tf_op jit(solution)/shard_map/all_to_all | solution.py:24
  56.7 6.7 %all-to-all-done.1 = bf16[4,2,64,256]{3,2,1,0:T(8,128)(2,1)S(1)} async-done(((bf16[4,2,64,256]{3,2,1,0:T(8,128)(2,1)}), bf16[4,2,64,256]{3,2,1,0:T(8,128)(2,1)S(1)}, u32[]{:S(2)}, u32[]{:S(2)}) %all-to-all-start.1) | async-done | bytes 262176 | tf_op jit(solution)/shard_map/all_to_all | solution.py:24
  67.9 11.0 %all-to-all-start.2 = ((bf16[8,32,896]{2,1,0:T(8,128)(2,1)}), bf16[8,32,896]{2,1,0:T(8,128)(2,1)S(1)}, u32[]{:S(2)}, u32[]{:S(2)}) async-start(bf16[8,32,896]{2,1,0:T(8,128)(2,1)} %bitcast.30), calls=%async_computation.2 | async-start | bytes 917504 | tf_op jit(solution)/shard_map/all_to_all | solution.py:24
  78.9 12.2 %all-gather.2 = bf16[8,64,256]{2,1,0:T(8,128)(2,1)S(1)} all-gather(bf16[2,64,256]{2,1,0:T(8,128)(2,1)S(1)} %copy-done.5), channel_id=4, replica_groups={{0,4,8,12},{1,5,9,13},{2,6,10,14},{3,7,11,15},{16,20,24,28},{17,21,25,2..., dimensions={0}, use_global_device_ids=true | all-gather | bytes 327680 | tf_op jit(solution)/shard_map/all_gather | solution.py:82
  94.1 2.5 %collective-permute-start.4 = (bf16[8,2,32,896]{3,2,1,0:T(8,128)(2,1)S(1)}, bf16[8,2,32,896]{3,2,1,0:T(8,128)(2,1)}, u32[]{:S(2)}, u32[]{:S(2)}) collective-permute-start(bf16[8,2,32,896]{3,2,1,0:T(8,128)(2,1)S(1)} %bitcast.154), channel_id=1, source_target_pairs={{0,128},{16,144},{32,160},{48,176},{64,192},{80,208},{96,224},{112... | collective-permute-start | bytes 2752520 | tf_op jit(solution)/shard_map/ppermute | solution.py:88
  96.6 4.6 %collective-permute-start.5 = (bf16[8,2,32,896]{3,2,1,0:T(8,128)(2,1)S(1)}, bf16[8,2,32,896]{3,2,1,0:T(8,128)(2,1)}, u32[]{:S(2)}, u32[]{:S(2)}) collective-permute-start(bf16[8,2,32,896]{3,2,1,0:T(8,128)(2,1)S(1)} %bitcast.155), channel_id=1, source_target_pairs={{0,384},{16,400},{32,416},{48,432},{64,448},{80,464},{96,480},{112... | collective-permute-start | bytes 2752520 | tf_op jit(solution)/shard_map/ppermute | solution.py:89
  102.1 9.9 %all-to-all-start.3 = ((bf16[8,32,896]{2,1,0:T(8,128)(2,1)}), bf16[8,32,896]{2,1,0:T(8,128)(2,1)S(1)}, u32[]{:S(2)}, u32[]{:S(2)}) async-start(bf16[8,32,896]{2,1,0:T(8,128)(2,1)} %broadcast_in_dim.17), calls=%async_computation.3 | async-start | bytes 917504 | tf_op jit(solution)/shard_map/all_to_all | solution.py:24
  113.9 6.2 %collective-permute-done.4 = bf16[8,2,32,896]{3,2,1,0:T(8,128)(2,1)} collective-permute-done((bf16[8,2,32,896]{3,2,1,0:T(8,128)(2,1)S(1)}, bf16[8,2,32,896]{3,2,1,0:T(8,128)(2,1)}, u32[]{:S(2)}, u32[]{:S(2)}) %collective-permute-start.4) | collective-permute-done | bytes 917536 | tf_op jit(solution)/shard_map/ppermute | solution.py:88
  124.9 5.1 %collective-permute-start.7 = (bf16[4,2,32,896]{3,2,1,0:T(8,128)(2,1)}, bf16[4,2,32,896]{3,2,1,0:T(8,128)(2,1)}, u32[]{:S(2)}, u32[]{:S(2)}) collective-permute-start(bf16[4,2,32,896]{3,2,1,0:T(8,128)(2,1)} %slice.79), channel_id=1, source_target_pairs={{0,384},{16,400},{32,416},{48,432},{64,448},{80,464},{96,480},{112... | collective-permute-start | bytes 1376264 | tf_op jit(solution)/shard_map/ppermute | solution.py:94
  138.9 3.6 %all-to-all-start.4 = ((bf16[4,8,32,896]{3,2,1,0:T(8,128)(2,1)}), bf16[4,8,32,896]{3,2,1,0:T(8,128)(2,1)S(1)}, u32[]{:S(2)}, u32[]{:S(2)}) async-start(bf16[4,8,32,896]{3,2,1,0:T(8,128)(2,1)} %broadcast_in_dim.18), calls=%async_computation.4 | async-start | bytes 3670016 | tf_op jit(solution)/shard_map/all_to_all | solution.py:24
  144.5 3.2 %fusion.25 = bf16[4,8,1,32,896]{4,3,2,1,0:T(8,128)(2,1)S(1)} fusion(bf16[4,8,2,32,896]{4,3,2,1,0:T(8,128)(2,1)} %bitcast_dynamic-update-slice_fusion.2), kind=kLoop, calls=%fused_computation.33 | loop fusion | flops 7340032 | bytes 5505024 | tf_op jit(solution)/shard_map/convert_element_type | solution.py:113
  149.3 3.8 %slice_convert_fusion = f32[4,8,1,32,896]{4,3,2,1,0:T(8,128)} fusion(bf16[4,8,2,32,896]{4,3,2,1,0:T(8,128)(2,1)} %bitcast_dynamic-update-slice_fusion.2), kind=kLoop, calls=%fused_computation.34 | loop fusion | flops 917504 | bytes 5505024 | tf_op jit(solution)/shard_map/convert_element_type | solution.py:111
  153.1 12.5 %all-to-all-done.4 = bf16[4,8,32,896]{3,2,1,0:T(8,128)(2,1)S(1)} async-done(((bf16[4,8,32,896]{3,2,1,0:T(8,128)(2,1)}), bf16[4,8,32,896]{3,2,1,0:T(8,128)(2,1)S(1)}, u32[]{:S(2)}, u32[]{:S(2)}) %all-to-all-start.4) | async-done | bytes 1835040 | tf_op jit(solution)/shard_map/all_to_all | solution.py:24
  165.6 3.6 %fusion.20 = (bf16[1024,896]{1,0:T(8,128)(2,1)S(1)}, bf16[1024,896]{1,0:T(8,128)(2,1)S(1)}) fusion(f32[4,8,1,32,896]{4,3,2,1,0:T(8,128)} %slice_convert_fusion, bf16[4,8,32,896]{3,2,1,0:T(8,128)(2,1)S(1)} %all-to-all-done.4, bf16[4,8,2,32,896]{4,3,2,1,0:T(8,128)(2,1)} %bitcast_dynamic-update-slice_fusion.2), kind=kLoop, calls=%fused_computation.26 | loop fusion | flops 13762560 | bytes 11010048 | tf_op jit(solution)/shard_map/convert_element_type | solution.py:116
  171.6 4.2 %all-to-all-start.5 = ((bf16[8,2,64,256]{3,2,1,0:T(8,128)(2,1)}), bf16[8,2,64,256]{3,2,1,0:T(8,128)(2,1)S(1)}, u32[]{:S(2)}, u32[]{:S(2)}) async-start(bf16[8,2,64,256]{3,2,1,0:T(8,128)(2,1)} %bitcast.46), calls=%async_computation.5 | async-start | bytes 1048576 | tf_op jit(solution)/shard_map/all_to_all | solution.py:24
  175.8 4.4 %fusion.10 = (bf16[4,8,32,896]{3,2,1,0:T(8,128)(2,1)S(1)}, bf16[4,8,32,896]{3,2,1,0:T(8,128)(2,1)}) fusion(bf16[4,8,32,896]{3,2,1,0:T(8,128)(2,1)S(1)} %all-to-all-done.4, bf16[4,8,2,32,896]{4,3,2,1,0:T(8,128)(2,1)} %bitcast_dynamic-update-slice_fusion.2), kind=kLoop, calls=%fused_computation.16 | loop fusion | flops 14680064 | bytes 9175040 | tf_op jit(solution)/shard_map/convert_element_type | solution.py:117
  181.8 4.3 %all-to-all-done.5 = bf16[8,2,64,256]{3,2,1,0:T(8,128)(2,1)S(1)} async-done(((bf16[8,2,64,256]{3,2,1,0:T(8,128)(2,1)}), bf16[8,2,64,256]{3,2,1,0:T(8,128)(2,1)S(1)}, u32[]{:S(2)}, u32[]{:S(2)}) %all-to-all-start.5) | async-done | bytes 524320 | tf_op jit(solution)/shard_map/all_to_all | solution.py:24
  186.2 8.8 %collective-permute-start.8 = (f32[64,256]{1,0:T(8,128)S(1)}, f32[64,256]{1,0:T(8,128)S(1)}, u32[]{:S(2)}, u32[]{:S(2)}) collective-permute-start(f32[64,256]{1,0:T(8,128)S(1)} %select_bitcast_fusion.8), channel_id=1, source_target_pairs={{0,2},{1,3},{2,0},{3,1},{4,6},{5,7},{6,4},{7,5},{8,10},{9,11},{10,... | collective-permute-start | bytes 196616 | tf_op jit(solution)/shard_map/ppermute | solution.py:128
  195.1 2.7 %fusion.28 = f32[256,896]{1,0:T(8,128)} fusion(bf16[1024,256]{1,0:T(8,128)(2,1)S(1)} %bitcast.153, bf16[1024,896]{1,0:T(8,128)(2,1)S(1)} %bitcast.150, bf16[256,896]{1,0:T(8,128)(2,1)} %param.11), kind=kOutput, calls=%fused_computation.41 | convolution fusion | flops 470450176 | bytes 3735552 | tf_op jit(solution)/shard_map/nd,nf->df/dot_general | solution.py:131
  197.7 7.6 %collective-permute-done.8 = f32[64,256]{1,0:T(8,128)S(1)} collective-permute-done((f32[64,256]{1,0:T(8,128)S(1)}, f32[64,256]{1,0:T(8,128)S(1)}, u32[]{:S(2)}, u32[]{:S(2)}) %collective-permute-start.8) | collective-permute-done | bytes 65568 | tf_op jit(solution)/shard_map/ppermute | solution.py:128
  (71 shorter events, 38.8 us)
Async XLA Ops:
  0.6 6.8 %copy-start.6 = (bf16[32,896]{1,0:T(8,128)(2,1)S(1)}, bf16[32,896]{1,0:T(8,128)(2,1)}, u32[]{:S(2)}) copy-start(bf16[32,896]{1,0:T(8,128)(2,1)} %param.10) | copy-start | bytes 172036
  0.6 8.8 %copy-start.8 = (bf16[64,256]{1,0:T(8,128)(2,1)S(1)}, bf16[64,256]{1,0:T(8,128)(2,1)}, u32[]{:S(2)}) copy-start(bf16[64,256]{1,0:T(8,128)(2,1)} %param.7) | copy-start | bytes 98308
  0.7 8.8 %copy-start.9 = (bf16[64,256]{1,0:T(8,128)(2,1)S(1)}, bf16[64,256]{1,0:T(8,128)(2,1)}, u32[]{:S(2)}) copy-start(bf16[64,256]{1,0:T(8,128)(2,1)} %param.8) | copy-start | bytes 98308
  0.7 6.7 %copy-start.7 = (bf16[32,896]{1,0:T(8,128)(2,1)S(1)}, bf16[32,896]{1,0:T(8,128)(2,1)}, u32[]{:S(2)}) copy-start(bf16[32,896]{1,0:T(8,128)(2,1)} %param.9) | copy-start | bytes 172036
  3.1 47.1 %all-to-all-start = ((bf16[4,896,256]{2,1,0:T(8,128)(2,1)}), bf16[4,896,256]{2,1,0:T(8,128)(2,1)S(1)}, u32[]{:S(2)}, u32[]{:S(2)}) async-start(bf16[4,896,256]{2,1,0:T(8,128)(2,1)} %broadcast_in_dim.16), calls=%async_computation | async-start | bytes 3670016 | tf_op jit(solution)/shard_map/all_to_all | solution.py:24
  7.4 26.5 %collective-permute-start = (bf16[2,32,896]{2,1,0:T(8,128)(2,1)S(1)}, bf16[2,32,896]{2,1,0:T(8,128)(2,1)S(1)}, u32[]{:S(2)}, u32[]{:S(2)}) collective-permute-start(bf16[2,32,896]{2,1,0:T(8,128)(2,1)S(1)} %pad_maximum_fusion.5), channel_id=1, source_target_pairs={{0,64},{16,80},{32,96},{48,112},{64,0},{80,16},{96,32},{112,48},{1... | collective-permute-start | bytes 344072 | tf_op jit(solution)/shard_map/ppermute | solution.py:37
  34.0 16.1 %collective-permute-start.1 = (bf16[2,2,32,896]{3,2,1,0:T(8,128)(2,1)S(1)}, bf16[2,2,32,896]{3,2,1,0:T(8,128)(2,1)S(1)}, u32[]{:S(2)}, u32[]{:S(2)}) collective-permute-start(bf16[2,2,32,896]{3,2,1,0:T(8,128)(2,1)S(1)} %pad_maximum_fusion.4), channel_id=1, source_target_pairs={{0,32},{16,48},{32,0},{48,16},{64,96},{80,112},{96,64},{112,80},{1... | collective-permute-start | bytes 688136 | tf_op jit(solution)/shard_map/ppermute | solution.py:37
  50.2 15.3 %collective-permute-start.2 = (bf16[2,2,2,32,896]{4,3,2,1,0:T(8,128)(2,1)S(1)}, bf16[2,2,2,32,896]{4,3,2,1,0:T(8,128)(2,1)S(1)}, u32[]{:S(2)}, u32[]{:S(2)}) collective-permute-start(bf16[2,2,2,32,896]{4,3,2,1,0:T(8,128)(2,1)S(1)} %pad_maximum_fusion.3), channel_id=1, source_target_pairs={{0,16},{16,0},{32,48},{48,32},{64,80},{80,64},{96,112},{112,96},{1... | collective-permute-start | bytes 1376264 | tf_op jit(solution)/shard_map/ppermute | solution.py:37
  52.2 11.2 %all-to-all-start.1 = ((bf16[4,2,64,256]{3,2,1,0:T(8,128)(2,1)}), bf16[4,2,64,256]{3,2,1,0:T(8,128)(2,1)S(1)}, u32[]{:S(2)}, u32[]{:S(2)}) async-start(bf16[4,2,64,256]{3,2,1,0:T(8,128)(2,1)} %all_gather.23), calls=%async_computation.1 | async-start | bytes 524288 | tf_op jit(solution)/shard_map/all_to_all | solution.py:24
  66.1 12.8 %copy-start.5 = (bf16[2,64,256]{2,1,0:T(8,128)(2,1)S(1)}, bf16[2,64,256]{2,1,0:T(8,128)(2,1)}, u32[]{:S(2)}) copy-start(bf16[2,64,256]{2,1,0:T(8,128)(2,1)} %get-tuple-element.28) | copy-start | bytes 196612
  67.9 33.3 %all-to-all-start.2 = ((bf16[8,32,896]{2,1,0:T(8,128)(2,1)}), bf16[8,32,896]{2,1,0:T(8,128)(2,1)S(1)}, u32[]{:S(2)}, u32[]{:S(2)}) async-start(bf16[8,32,896]{2,1,0:T(8,128)(2,1)} %bitcast.30), calls=%async_computation.2 | async-start | bytes 917504 | tf_op jit(solution)/shard_map/all_to_all | solution.py:24
  92.2 19.8 %collective-permute-start.3 = (bf16[2,8,64,256]{3,2,1,0:T(8,128)(2,1)S(1)}, bf16[2,8,64,256]{3,2,1,0:T(8,128)(2,1)S(1)}, u32[]{:S(2)}, u32[]{:S(2)}) collective-permute-start(bf16[2,8,64,256]{3,2,1,0:T(8,128)(2,1)S(1)} %pad_maximum_fusion.2), channel_id=1, source_target_pairs={{0,1},{1,0},{2,3},{3,2},{4,5},{5,4},{6,7},{7,6},{8,9},{9,8},{10,11... | collective-permute-start | bytes 1572872 | tf_op jit(solution)/shard_map/ppermute | solution.py:37
  94.1 26.0 %collective-permute-start.4 = (bf16[8,2,32,896]{3,2,1,0:T(8,128)(2,1)S(1)}, bf16[8,2,32,896]{3,2,1,0:T(8,128)(2,1)}, u32[]{:S(2)}, u32[]{:S(2)}) collective-permute-start(bf16[8,2,32,896]{3,2,1,0:T(8,128)(2,1)S(1)} %bitcast.154), channel_id=1, source_target_pairs={{0,128},{16,144},{32,160},{48,176},{64,192},{80,208},{96,224},{112... | collective-permute-start | bytes 2752520 | tf_op jit(solution)/shard_map/ppermute | solution.py:88
  96.6 26.5 %collective-permute-start.5 = (bf16[8,2,32,896]{3,2,1,0:T(8,128)(2,1)S(1)}, bf16[8,2,32,896]{3,2,1,0:T(8,128)(2,1)}, u32[]{:S(2)}, u32[]{:S(2)}) collective-permute-start(bf16[8,2,32,896]{3,2,1,0:T(8,128)(2,1)S(1)} %bitcast.155), channel_id=1, source_target_pairs={{0,384},{16,400},{32,416},{48,432},{64,448},{80,464},{96,480},{112... | collective-permute-start | bytes 2752520 | tf_op jit(solution)/shard_map/ppermute | solution.py:89
  102.1 35.4 %all-to-all-start.3 = ((bf16[8,32,896]{2,1,0:T(8,128)(2,1)}), bf16[8,32,896]{2,1,0:T(8,128)(2,1)S(1)}, u32[]{:S(2)}, u32[]{:S(2)}) async-start(bf16[8,32,896]{2,1,0:T(8,128)(2,1)} %broadcast_in_dim.17), calls=%async_computation.3 | async-start | bytes 917504 | tf_op jit(solution)/shard_map/all_to_all | solution.py:24
  121.1 15.5 %collective-permute-start.6 = (bf16[4,2,32,896]{3,2,1,0:T(8,128)(2,1)S(1)}, bf16[4,2,32,896]{3,2,1,0:T(8,128)(2,1)S(1)}, u32[]{:S(2)}, u32[]{:S(2)}) collective-permute-start(bf16[4,2,32,896]{3,2,1,0:T(8,128)(2,1)S(1)} %slice.78), channel_id=1, source_target_pairs={{0,128},{16,144},{32,160},{48,176},{64,192},{80,208},{96,224},{112... | collective-permute-start | bytes 1376264 | tf_op jit(solution)/shard_map/ppermute | solution.py:93
  124.9 17.7 %collective-permute-start.7 = (bf16[4,2,32,896]{3,2,1,0:T(8,128)(2,1)}, bf16[4,2,32,896]{3,2,1,0:T(8,128)(2,1)}, u32[]{:S(2)}, u32[]{:S(2)}) collective-permute-start(bf16[4,2,32,896]{3,2,1,0:T(8,128)(2,1)} %slice.79), channel_id=1, source_target_pairs={{0,384},{16,400},{32,416},{48,432},{64,448},{80,464},{96,480},{112... | collective-permute-start | bytes 1376264 | tf_op jit(solution)/shard_map/ppermute | solution.py:94
  138.9 26.7 %all-to-all-start.4 = ((bf16[4,8,32,896]{3,2,1,0:T(8,128)(2,1)}), bf16[4,8,32,896]{3,2,1,0:T(8,128)(2,1)S(1)}, u32[]{:S(2)}, u32[]{:S(2)}) async-start(bf16[4,8,32,896]{3,2,1,0:T(8,128)(2,1)} %broadcast_in_dim.18), calls=%async_computation.4 | async-start | bytes 3670016 | tf_op jit(solution)/shard_map/all_to_all | solution.py:24
  142.5 5.1 %copy-start.3 = (bf16[1,8,2,64,256]{4,3,2,1,0:T(8,128)(2,1)S(1)}, bf16[1,8,2,64,256]{4,3,2,1,0:T(8,128)(2,1)}, u32[]{:S(2)}) copy-start(bf16[1,8,2,64,256]{4,3,2,1,0:T(8,128)(2,1)} %get-tuple-element.34) | copy-start | bytes 1572868
  153.1 16.1 %copy-start.1 = (bf16[256,896]{1,0:T(8,128)(2,1)S(1)}, bf16[256,896]{1,0:T(8,128)(2,1)}, u32[]{:S(2)}) copy-start(bf16[256,896]{1,0:T(8,128)(2,1)} %param.12) | copy-start | bytes 1376260
  153.1 16.9 %copy-start.2 = (bf16[256,896]{1,0:T(8,128)(2,1)S(1)}, bf16[256,896]{1,0:T(8,128)(2,1)}, u32[]{:S(2)}) copy-start(bf16[256,896]{1,0:T(8,128)(2,1)} %param.11) | copy-start | bytes 1376260
  171.6 14.6 %all-to-all-start.5 = ((bf16[8,2,64,256]{3,2,1,0:T(8,128)(2,1)}), bf16[8,2,64,256]{3,2,1,0:T(8,128)(2,1)S(1)}, u32[]{:S(2)}, u32[]{:S(2)}) async-start(bf16[8,2,64,256]{3,2,1,0:T(8,128)(2,1)} %bitcast.46), calls=%async_computation.5 | async-start | bytes 1048576 | tf_op jit(solution)/shard_map/all_to_all | solution.py:24
  180.1 14.9 %copy-start = (bf16[4,8,32,896]{3,2,1,0:T(8,128)(2,1)S(1)}, bf16[4,8,32,896]{3,2,1,0:T(8,128)(2,1)}, u32[]{:S(2)}) copy-start(bf16[4,8,32,896]{3,2,1,0:T(8,128)(2,1)} %get-tuple-element.33) | copy-start | bytes 5505028
  186.2 19.1 %collective-permute-start.8 = (f32[64,256]{1,0:T(8,128)S(1)}, f32[64,256]{1,0:T(8,128)S(1)}, u32[]{:S(2)}, u32[]{:S(2)}) collective-permute-start(f32[64,256]{1,0:T(8,128)S(1)} %select_bitcast_fusion.8), channel_id=1, source_target_pairs={{0,2},{1,3},{2,0},{3,1},{4,6},{5,7},{6,4},{7,5},{8,10},{9,11},{10,... | collective-permute-start | bytes 196616 | tf_op jit(solution)/shard_map/ppermute | solution.py:128
  (1 other events, 5.1 us)

commit v7 on v5

--- a/solution.py
+++ b/solution.py
@@ -6,10 +6,6 @@
 X, ZL, Y, ZH, C = 4, 8, 4, 2, 2
 X_GROUPS = [[x * ZL + z for x in range(X)] for z in range(ZL)]
 Z_GROUPS = [[x * ZL + z for z in range(ZL)] for x in range(X)]
-Z_BY_CORE = [
-    [x * ZL + (h * C + c) * 2 + k for c in range(C) for h in range(ZH) for k in range(2)]
-    for x in range(X)
-]
 YC_GROUPS = [[(y * ZH + h) * C + c for y in range(Y) for c in range(C)] for h in range(ZH)]
 Y_GROUPS = [[(y * ZH + h) * C + c for y in range(Y)] for h in range(ZH) for c in range(C)]
 C_GROUPS = [[(y * ZH + h) * C + c for c in range(C)] for y in range(Y) for h in range(ZH)]
@@ -46,48 +42,33 @@
     dp, tensor = lax.axis_index("dp"), lax.axis_index("tensor")
     x, z = dp // ZL, dp % ZL
 
-    copies = jnp.broadcast_to(down_weight[None], (X,) + down_weight.shape)
-    copies, out_grad, tokens, gate_pre, up_pre = lax.optimization_barrier(
-        (copies, out_grad, tokens, gate_pre, up_pre)
-    )
-    down_all = exchange(copies, "dp", X_GROUPS)
-
     both = jnp.stack([out_grad, tokens])
     both = pair(both, "tensor", ZH_SWAP, tensor // C % ZH, 1)
-    grads_y = lax.all_gather(both[0], "tensor", axis_index_groups=Y_GROUPS)
+    both = gather(both, "tensor", Y_GROUPS)
 
     saved = jnp.stack([gate_pre, up_pre])
     saved = pair(saved, "dp", [(d, d ^ 4) for d in range(X * ZL)], z // 4, 0)
-    saved, grads_y = lax.optimization_barrier((saved, grads_y))
+    saved, both = lax.optimization_barrier((saved, both))
     saved = pair(saved, "dp", [(d, d ^ 2) for d in range(X * ZL)], z // 2 % 2, 1)
-
-    down_all, ahead = lax.optimization_barrier((down_all, grads_y))
-    grads_x = exchange(ahead, "dp", X_GROUPS)
-    grads_x = lax.all_gather(grads_x, "tensor", axis_index_groups=C_GROUPS)
-    grads_x, saved = lax.optimization_barrier((grads_x, saved))
     saved = pair(saved, "dp", [(d, d ^ 1) for d in range(X * ZL)], z % 2, 2)
     saved = saved.reshape(ZL, 2, toks, hid)
-    partial = sum(
-        jnp.einsum(
-            "nd,fd->nf",
-            grads_x[:, k].reshape(n // X, feats),
-            down_all[k],
-            preferred_element_type=jnp.float32,
-        )
-        for k in range(X)
+
+    grads_all = lax.all_gather(both[:, 0], "tensor", axis_index_groups=C_GROUPS)
+    grads_all = grads_all.transpose(1, 2, 0, 3, 4).reshape(n, feats)
+
+    partial = jnp.einsum(
+        "nd,fd->nf", grads_all, down_weight, preferred_element_type=jnp.float32
     ).astype(jnp.bfloat16)
-
-    inputs, _ = lax.optimization_barrier((both[1], partial))
-    tokens_y = lax.all_gather(inputs, "tensor", axis_index_groups=Y_GROUPS)
-    both = jnp.stack([grads_y, tokens_y]).reshape(2, Y * ZH, rows, feats)
-    both = pair(both, "tensor", C_SWAP, tensor % C, 2)
-    both = both.reshape(2, n, feats)
-    grads_all, tokens_all = both[0], both[1]
+    inputs, _ = lax.optimization_barrier((both[:, 1], partial))
+    tokens_all = lax.all_gather(inputs, "tensor", axis_index_groups=C_GROUPS)
+    tokens_all = tokens_all.transpose(1, 2, 0, 3, 4).reshape(n, feats)
+    partial = add_up(partial.reshape(X, ZL * toks, hid), "dp", X_GROUPS).astype(jnp.bfloat16)
+    partial, saved = lax.optimization_barrier((partial, saved))
 
     from_down = lax.ppermute(saved, "dp", X_UP)
     from_up = lax.ppermute(saved, "dp", X_DOWN)
 
-    hidden = add_up(partial.reshape(ZL, toks, hid), "dp", Z_BY_CORE).astype(jnp.bfloat16)
+    hidden = add_up(partial.reshape(ZL, toks, hid), "dp", Z_GROUPS).astype(jnp.bfloat16)
 
     far_low = lax.ppermute(from_down[: ZL // 2], "dp", X_UP)
     far_high = lax.ppermute(from_up[ZL // 2 :], "dp", X_DOWN)

time: 205 us -> 203 us (level)
  the two profiles are of different devices: /device:TPU:416 before, /device:TPU:160 now
where the time goes in v7:
time: 203 us; the launch traced here: 202 us
  starting transfers between devices  83.8 us (41%)
  waiting for transfers between devices  68.9 us (34%)
  other arithmetic  20.6 us (10%)
  local copies, waits for them, and re-layouts  13.8 us (7%)
  matrix products  9.44 us (5%)
  blocking collectives  4.35 us (2%)
    all_to_all x6, waiting for transfers between devices, exchange(): lax.all_to_all(blocks, axis, 0, 0, axis_index_groups=groups, tiled=True)  42 us
    all_to_all x6, starting transfers between devices, exchange(): lax.all_to_all(blocks, axis, 0, 0, axis_index_groups=groups, tiled=True)  38.2 us
    ppermute x4, starting transfers between devices, pair(): other = lax.ppermute(block, axis, perm)  24.7 us
    ppermute x4, waiting for transfers between devices, pair(): other = lax.ppermute(block, axis, perm)  11.9 us
    ppermute x1, starting transfers between devices, on_device(): lax.ppermute(sent, 'tensor', ZH_SWAP)  9.16 us
    ppermute x1, waiting for transfers between devices, on_device(): far_low = lax.ppermute(from_down[:ZL // 2], 'dp', X_UP)  8.29 us
    ppermute x1, waiting for transfers between devices, on_device(): lax.ppermute(sent, 'tensor', ZH_SWAP)  6.67 us
    dynamic_update_slice x4, local copies, waits for them, and re-layouts, on_device(): full = lax.dynamic_update_slice(full, block[None], (start, half, 0, 0, 0))  4.79 us
  transfers between devices with their start and end apart: 15, of which 9 were waited for; matrix products, arithmetic and copies ran while one was open for 17% of the time, Pallas kernels for 0%

profile of v7, /device:TPU:160, one launch (start us, length us, event | category | flops | bytes accessed | tf_op | source)
XLA Modules:
  0.0 201.9 jit_solution(12507845978583877678)
XLA Ops:
  1.5 10.0 %collective-permute-start.1 = (bf16[2,64,256]{2,1,0:T(8,128)(2,1)S(1)}, bf16[2,64,256]{2,1,0:T(8,128)(2,1)S(1)}, u32[]{:S(2)}, u32[]{:S(2)}) collective-permute-start(bf16[2,64,256]{2,1,0:T(8,128)(2,1)S(1)} %pad_maximum_fusion.5), channel_id=1, source_target_pairs={{0,2},{1,3},{2,0},{3,1},{4,6},{5,7},{6,4},{7,5},{8,10},{9,11},{10,... | collective-permute-start | bytes 196616 | tf_op jit(solution)/shard_map/ppermute | solution.py:32
  12.4 5.5 %collective-permute-start = (bf16[2,32,896]{2,1,0:T(8,128)(2,1)S(1)}, bf16[2,32,896]{2,1,0:T(8,128)(2,1)S(1)}, u32[]{:S(2)}, u32[]{:S(2)}) collective-permute-start(bf16[2,32,896]{2,1,0:T(8,128)(2,1)S(1)} %pad_maximum_fusion.4), channel_id=1, source_target_pairs={{0,64},{16,80},{32,96},{48,112},{64,0},{80,16},{96,32},{112,48},{1... | collective-permute-start | bytes 344072 | tf_op jit(solution)/shard_map/ppermute | solution.py:32
  19.5 4.5 %all-to-all-start = ((bf16[4,2,2,64,256]{4,3,2,1,0:T(8,128)(2,1)}), bf16[4,2,2,64,256]{4,3,2,1,0:T(8,128)(2,1)S(1)}, u32[]{:S(2)}, u32[]{:S(2)}) async-start(bf16[4,2,2,64,256]{4,3,2,1,0:T(8,128)(2,1)} %broadcast_in_dim.16), calls=%async_computation | async-start | bytes 1048576 | tf_op jit(solution)/shard_map/all_to_all | solution.py:19
  26.3 6.6 %all-to-all-done = bf16[4,2,2,64,256]{4,3,2,1,0:T(8,128)(2,1)S(1)} async-done(((bf16[4,2,2,64,256]{4,3,2,1,0:T(8,128)(2,1)}), bf16[4,2,2,64,256]{4,3,2,1,0:T(8,128)(2,1)S(1)}, u32[]{:S(2)}, u32[]{:S(2)}) %all-to-all-start) | async-done | bytes 524320 | tf_op jit(solution)/shard_map/all_to_all | solution.py:19
  33.0 3.4 %collective-permute-start.2 = (bf16[2,2,32,896]{3,2,1,0:T(8,128)(2,1)S(1)}, bf16[2,2,32,896]{3,2,1,0:T(8,128)(2,1)S(1)}, u32[]{:S(2)}, u32[]{:S(2)}) collective-permute-start(bf16[2,2,32,896]{3,2,1,0:T(8,128)(2,1)S(1)} %pad_maximum_fusion.2), channel_id=1, source_target_pairs={{0,32},{16,48},{32,0},{48,16},{64,96},{80,112},{96,64},{112,80},{1... | collective-permute-start | bytes 688136 | tf_op jit(solution)/shard_map/ppermute | solution.py:32
  41.4 4.3 %all-to-all-start.1 = ((bf16[4,256,896]{2,1,0:T(8,128)(2,1)}), bf16[4,256,896]{2,1,0:T(8,128)(2,1)S(1)}, u32[]{:S(2)}, u32[]{:S(2)}) async-start(bf16[4,256,896]{2,1,0:T(8,128)(2,1)} %bitcast.133), calls=%async_computation.1 | async-start | bytes 3670016 | tf_op jit(solution)/shard_map/all_to_all | solution.py:19
  45.8 5.9 %collective-permute-start.3 = (bf16[2,2,2,32,896]{4,3,2,1,0:T(8,128)(2,1)S(1)}, bf16[2,2,2,32,896]{4,3,2,1,0:T(8,128)(2,1)S(1)}, u32[]{:S(2)}, u32[]{:S(2)}) collective-permute-start(bf16[2,2,2,32,896]{4,3,2,1,0:T(8,128)(2,1)S(1)} %pad_maximum_fusion.1), channel_id=1, source_target_pairs={{0,16},{16,0},{32,48},{48,32},{64,80},{80,64},{96,112},{112,96},{1... | collective-permute-start | bytes 1376264 | tf_op jit(solution)/shard_map/ppermute | solution.py:32
  51.7 10.5 %collective-permute-done.3 = bf16[2,2,2,32,896]{4,3,2,1,0:T(8,128)(2,1)S(1)} collective-permute-done((bf16[2,2,2,32,896]{4,3,2,1,0:T(8,128)(2,1)S(1)}, bf16[2,2,2,32,896]{4,3,2,1,0:T(8,128)(2,1)S(1)}, u32[]{:S(2)}, u32[]{:S(2)}) %collective-permute-start.3) | collective-permute-done | bytes 458784 | tf_op jit(solution)/shard_map/ppermute | solution.py:32
  62.4 7.1 %all-to-all-done.1 = bf16[4,256,896]{2,1,0:T(8,128)(2,1)S(1)} async-done(((bf16[4,256,896]{2,1,0:T(8,128)(2,1)}), bf16[4,256,896]{2,1,0:T(8,128)(2,1)S(1)}, u32[]{:S(2)}, u32[]{:S(2)}) %all-to-all-start.1) | async-done | bytes 1835040 | tf_op jit(solution)/shard_map/all_to_all | solution.py:19
  70.7 10.6 %all-to-all-start.2 = ((bf16[8,32,896]{2,1,0:T(8,128)(2,1)}), bf16[8,32,896]{2,1,0:T(8,128)(2,1)S(1)}, u32[]{:S(2)}, u32[]{:S(2)}) async-start(bf16[8,32,896]{2,1,0:T(8,128)(2,1)} %bitcast.23), calls=%async_computation.2 | async-start | bytes 917504 | tf_op jit(solution)/shard_map/all_to_all | solution.py:19
  87.1 11.8 %all-to-all-done.2 = bf16[8,32,896]{2,1,0:T(8,128)(2,1)S(1)} async-done(((bf16[8,32,896]{2,1,0:T(8,128)(2,1)}), bf16[8,32,896]{2,1,0:T(8,128)(2,1)S(1)}, u32[]{:S(2)}, u32[]{:S(2)}) %all-to-all-start.2) | async-done | bytes 458784 | tf_op jit(solution)/shard_map/all_to_all | solution.py:19
  99.8 11.7 %all-to-all-start.3 = ((bf16[8,32,896]{2,1,0:T(8,128)(2,1)}), bf16[8,32,896]{2,1,0:T(8,128)(2,1)}, u32[]{:S(2)}, u32[]{:S(2)}) async-start(bf16[8,32,896]{2,1,0:T(8,128)(2,1)} %broadcast_in_dim.17), calls=%async_computation.3 | async-start | bytes 917504 | tf_op jit(solution)/shard_map/all_to_all | solution.py:19
  114.5 3.1 %collective-permute-start.7 = (bf16[4,2,32,896]{3,2,1,0:T(8,128)(2,1)}, bf16[4,2,32,896]{3,2,1,0:T(8,128)(2,1)}, u32[]{:S(2)}, u32[]{:S(2)}) collective-permute-start(bf16[4,2,32,896]{3,2,1,0:T(8,128)(2,1)} %slice.35), channel_id=1, source_target_pairs={{0,384},{16,400},{32,416},{48,432},{64,448},{80,464},{96,480},{112... | collective-permute-start | bytes 1376264 | tf_op jit(solution)/shard_map/ppermute | solution.py:74
  124.8 8.3 %collective-permute-done.6 = bf16[4,2,32,896]{3,2,1,0:T(8,128)(2,1)S(1)} collective-permute-done((bf16[4,2,32,896]{3,2,1,0:T(8,128)(2,1)S(1)}, bf16[4,2,32,896]{3,2,1,0:T(8,128)(2,1)S(1)}, u32[]{:S(2)}, u32[]{:S(2)}) %collective-permute-start.6) | collective-permute-done | bytes 458784 | tf_op jit(solution)/shard_map/ppermute | solution.py:73
  136.4 3.6 %all-to-all-start.4 = ((bf16[4,8,32,896]{3,2,1,0:T(8,128)(2,1)}), bf16[4,8,32,896]{3,2,1,0:T(8,128)(2,1)S(1)}, u32[]{:S(2)}, u32[]{:S(2)}) async-start(bf16[4,8,32,896]{3,2,1,0:T(8,128)(2,1)} %broadcast_in_dim.18), calls=%async_computation.4 | async-start | bytes 3670016 | tf_op jit(solution)/shard_map/all_to_all | solution.py:19
  141.9 3.2 %fusion.25 = bf16[4,8,1,32,896]{4,3,2,1,0:T(8,128)(2,1)S(1)} fusion(bf16[4,8,2,32,896]{4,3,2,1,0:T(8,128)(2,1)} %bitcast_dynamic-update-slice_fusion.2), kind=kLoop, calls=%fused_computation.33 | loop fusion | flops 7340032 | bytes 5505024 | tf_op jit(solution)/shard_map/convert_element_type | solution.py:93
  146.7 3.8 %slice_convert_fusion = f32[4,8,1,32,896]{4,3,2,1,0:T(8,128)} fusion(bf16[4,8,2,32,896]{4,3,2,1,0:T(8,128)(2,1)} %bitcast_dynamic-update-slice_fusion.2), kind=kLoop, calls=%fused_computation.34 | loop fusion | flops 917504 | bytes 5505024 | tf_op jit(solution)/shard_map/convert_element_type | solution.py:91
  150.5 12.4 %all-to-all-done.4 = bf16[4,8,32,896]{3,2,1,0:T(8,128)(2,1)S(1)} async-done(((bf16[4,8,32,896]{3,2,1,0:T(8,128)(2,1)}), bf16[4,8,32,896]{3,2,1,0:T(8,128)(2,1)S(1)}, u32[]{:S(2)}, u32[]{:S(2)}) %all-to-all-start.4) | async-done | bytes 1835040 | tf_op jit(solution)/shard_map/all_to_all | solution.py:19
  162.9 3.6 %fusion.20 = (bf16[1024,896]{1,0:T(8,128)(2,1)S(1)}, bf16[1024,896]{1,0:T(8,128)(2,1)S(1)}) fusion(f32[4,8,1,32,896]{4,3,2,1,0:T(8,128)} %slice_convert_fusion, bf16[4,8,32,896]{3,2,1,0:T(8,128)(2,1)S(1)} %all-to-all-done.4, bf16[4,8,2,32,896]{4,3,2,1,0:T(8,128)(2,1)} %bitcast_dynamic-update-slice_fusion.2), kind=kLoop, calls=%fused_computation.26 | loop fusion | flops 13762560 | bytes 11010048 | tf_op jit(solution)/shard_map/convert_element_type | solution.py:96
  168.8 3.5 %all-to-all-start.5 = ((bf16[8,2,64,256]{3,2,1,0:T(8,128)(2,1)}), bf16[8,2,64,256]{3,2,1,0:T(8,128)(2,1)S(1)}, u32[]{:S(2)}, u32[]{:S(2)}) async-start(bf16[8,2,64,256]{3,2,1,0:T(8,128)(2,1)} %bitcast.38), calls=%async_computation.5 | async-start | bytes 1048576 | tf_op jit(solution)/shard_map/all_to_all | solution.py:19
  172.3 4.4 %fusion.10 = (bf16[4,8,32,896]{3,2,1,0:T(8,128)(2,1)S(1)}, bf16[4,8,32,896]{3,2,1,0:T(8,128)(2,1)}) fusion(bf16[4,8,32,896]{3,2,1,0:T(8,128)(2,1)S(1)} %all-to-all-done.4, bf16[4,8,2,32,896]{4,3,2,1,0:T(8,128)(2,1)} %bitcast_dynamic-update-slice_fusion.2), kind=kLoop, calls=%fused_computation.16 | loop fusion | flops 14680064 | bytes 9175040 | tf_op jit(solution)/shard_map/convert_element_type | solution.py:97
  178.4 4.2 %all-to-all-done.5 = bf16[8,2,64,256]{3,2,1,0:T(8,128)(2,1)S(1)} async-done(((bf16[8,2,64,256]{3,2,1,0:T(8,128)(2,1)}), bf16[8,2,64,256]{3,2,1,0:T(8,128)(2,1)S(1)}, u32[]{:S(2)}, u32[]{:S(2)}) %all-to-all-start.5) | async-done | bytes 524320 | tf_op jit(solution)/shard_map/all_to_all | solution.py:19
  182.7 9.2 %collective-permute-start.8 = (f32[64,256]{1,0:T(8,128)S(1)}, f32[64,256]{1,0:T(8,128)S(1)}, u32[]{:S(2)}, u32[]{:S(2)}) collective-permute-start(f32[64,256]{1,0:T(8,128)S(1)} %select_bitcast_fusion.6), channel_id=1, source_target_pairs={{0,2},{1,3},{2,0},{3,1},{4,6},{5,7},{6,4},{7,5},{8,10},{9,11},{10,... | collective-permute-start | bytes 196616 | tf_op jit(solution)/shard_map/ppermute | solution.py:108
  194.6 6.7 %collective-permute-done.8 = f32[64,256]{1,0:T(8,128)S(1)} collective-permute-done((f32[64,256]{1,0:T(8,128)S(1)}, f32[64,256]{1,0:T(8,128)S(1)}, u32[]{:S(2)}, u32[]{:S(2)}) %collective-permute-start.8) | collective-permute-done | bytes 65568 | tf_op jit(solution)/shard_map/ppermute | solution.py:108
  (62 shorter events, 43.3 us)
Async XLA Ops:
  0.6 38.8 %copy-start.5 = (bf16[896,256]{1,0:T(8,128)(2,1)S(1)}, bf16[896,256]{1,0:T(8,128)(2,1)}, u32[]{:S(2)}) copy-start(bf16[896,256]{1,0:T(8,128)(2,1)} %param.13) | copy-start | bytes 1376260
  1.5 16.4 %collective-permute-start.1 = (bf16[2,64,256]{2,1,0:T(8,128)(2,1)S(1)}, bf16[2,64,256]{2,1,0:T(8,128)(2,1)S(1)}, u32[]{:S(2)}, u32[]{:S(2)}) collective-permute-start(bf16[2,64,256]{2,1,0:T(8,128)(2,1)S(1)} %pad_maximum_fusion.5), channel_id=1, source_target_pairs={{0,2},{1,3},{2,0},{3,1},{4,6},{5,7},{6,4},{7,5},{8,10},{9,11},{10,... | collective-permute-start | bytes 196616 | tf_op jit(solution)/shard_map/ppermute | solution.py:32
  12.4 13.1 %collective-permute-start = (bf16[2,32,896]{2,1,0:T(8,128)(2,1)S(1)}, bf16[2,32,896]{2,1,0:T(8,128)(2,1)S(1)}, u32[]{:S(2)}, u32[]{:S(2)}) collective-permute-start(bf16[2,32,896]{2,1,0:T(8,128)(2,1)S(1)} %pad_maximum_fusion.4), channel_id=1, source_target_pairs={{0,64},{16,80},{32,96},{48,112},{64,0},{80,16},{96,32},{112,48},{1... | collective-permute-start | bytes 344072 | tf_op jit(solution)/shard_map/ppermute | solution.py:32
  19.5 13.4 %all-to-all-start = ((bf16[4,2,2,64,256]{4,3,2,1,0:T(8,128)(2,1)}), bf16[4,2,2,64,256]{4,3,2,1,0:T(8,128)(2,1)S(1)}, u32[]{:S(2)}, u32[]{:S(2)}) async-start(bf16[4,2,2,64,256]{4,3,2,1,0:T(8,128)(2,1)} %broadcast_in_dim.16), calls=%async_computation | async-start | bytes 1048576 | tf_op jit(solution)/shard_map/all_to_all | solution.py:19
  33.0 12.7 %collective-permute-start.2 = (bf16[2,2,32,896]{3,2,1,0:T(8,128)(2,1)S(1)}, bf16[2,2,32,896]{3,2,1,0:T(8,128)(2,1)S(1)}, u32[]{:S(2)}, u32[]{:S(2)}) collective-permute-start(bf16[2,2,32,896]{3,2,1,0:T(8,128)(2,1)S(1)} %pad_maximum_fusion.2), channel_id=1, source_target_pairs={{0,32},{16,48},{32,0},{48,16},{64,96},{80,112},{96,64},{112,80},{1... | collective-permute-start | bytes 688136 | tf_op jit(solution)/shard_map/ppermute | solution.py:32
  38.6 0.8 copy-start.1
  41.4 28.1 %all-to-all-start.1 = ((bf16[4,256,896]{2,1,0:T(8,128)(2,1)}), bf16[4,256,896]{2,1,0:T(8,128)(2,1)S(1)}, u32[]{:S(2)}, u32[]{:S(2)}) async-start(bf16[4,256,896]{2,1,0:T(8,128)(2,1)} %bitcast.133), calls=%async_computation.1 | async-start | bytes 3670016 | tf_op jit(solution)/shard_map/all_to_all | solution.py:19
  45.8 16.4 %collective-permute-start.3 = (bf16[2,2,2,32,896]{4,3,2,1,0:T(8,128)(2,1)S(1)}, bf16[2,2,2,32,896]{4,3,2,1,0:T(8,128)(2,1)S(1)}, u32[]{:S(2)}, u32[]{:S(2)}) collective-permute-start(bf16[2,2,2,32,896]{4,3,2,1,0:T(8,128)(2,1)S(1)} %pad_maximum_fusion.1), channel_id=1, source_target_pairs={{0,16},{16,0},{32,48},{48,32},{64,80},{80,64},{96,112},{112,96},{1... | collective-permute-start | bytes 1376264 | tf_op jit(solution)/shard_map/ppermute | solution.py:32
  70.7 28.2 %all-to-all-start.2 = ((bf16[8,32,896]{2,1,0:T(8,128)(2,1)}), bf16[8,32,896]{2,1,0:T(8,128)(2,1)S(1)}, u32[]{:S(2)}, u32[]{:S(2)}) async-start(bf16[8,32,896]{2,1,0:T(8,128)(2,1)} %bitcast.23), calls=%async_computation.2 | async-start | bytes 917504 | tf_op jit(solution)/shard_map/all_to_all | solution.py:19
  81.3 32.4 %collective-permute-start.5 = (bf16[8,2,32,896]{3,2,1,0:T(8,128)(2,1)S(1)}, bf16[8,2,32,896]{3,2,1,0:T(8,128)(2,1)S(1)}, u32[]{:S(2)}, u32[]{:S(2)}) collective-permute-start(bf16[8,2,32,896]{3,2,1,0:T(8,128)(2,1)S(1)} %bitcast.138), channel_id=1, source_target_pairs={{0,384},{16,400},{32,416},{48,432},{64,448},{80,464},{96,480},{112... | collective-permute-start | bytes 2752520 | tf_op jit(solution)/shard_map/ppermute | solution.py:69
  84.4 33.2 %collective-permute-start.4 = (bf16[8,2,32,896]{3,2,1,0:T(8,128)(2,1)S(1)}, bf16[8,2,32,896]{3,2,1,0:T(8,128)(2,1)S(1)}, u32[]{:S(2)}, u32[]{:S(2)}) collective-permute-start(bf16[8,2,32,896]{3,2,1,0:T(8,128)(2,1)S(1)} %bitcast.139), channel_id=1, source_target_pairs={{0,128},{16,144},{32,160},{48,176},{64,192},{80,208},{96,224},{112... | collective-permute-start | bytes 2752520 | tf_op jit(solution)/shard_map/ppermute | solution.py:68
  99.8 34.1 %all-to-all-start.3 = ((bf16[8,32,896]{2,1,0:T(8,128)(2,1)}), bf16[8,32,896]{2,1,0:T(8,128)(2,1)}, u32[]{:S(2)}, u32[]{:S(2)}) async-start(bf16[8,32,896]{2,1,0:T(8,128)(2,1)} %broadcast_in_dim.17), calls=%async_computation.3 | async-start | bytes 917504 | tf_op jit(solution)/shard_map/all_to_all | solution.py:19
  114.5 25.5 %collective-permute-start.7 = (bf16[4,2,32,896]{3,2,1,0:T(8,128)(2,1)}, bf16[4,2,32,896]{3,2,1,0:T(8,128)(2,1)}, u32[]{:S(2)}, u32[]{:S(2)}) collective-permute-start(bf16[4,2,32,896]{3,2,1,0:T(8,128)(2,1)} %slice.35), channel_id=1, source_target_pairs={{0,384},{16,400},{32,416},{48,432},{64,448},{80,464},{96,480},{112... | collective-permute-start | bytes 1376264 | tf_op jit(solution)/shard_map/ppermute | solution.py:74
  117.7 15.4 %collective-permute-start.6 = (bf16[4,2,32,896]{3,2,1,0:T(8,128)(2,1)S(1)}, bf16[4,2,32,896]{3,2,1,0:T(8,128)(2,1)S(1)}, u32[]{:S(2)}, u32[]{:S(2)}) collective-permute-start(bf16[4,2,32,896]{3,2,1,0:T(8,128)(2,1)S(1)} %slice.34), channel_id=1, source_target_pairs={{0,128},{16,144},{32,160},{48,176},{64,192},{80,208},{96,224},{112... | collective-permute-start | bytes 1376264 | tf_op jit(solution)/shard_map/ppermute | solution.py:73
  136.4 26.5 %all-to-all-start.4 = ((bf16[4,8,32,896]{3,2,1,0:T(8,128)(2,1)}), bf16[4,8,32,896]{3,2,1,0:T(8,128)(2,1)S(1)}, u32[]{:S(2)}, u32[]{:S(2)}) async-start(bf16[4,8,32,896]{3,2,1,0:T(8,128)(2,1)} %broadcast_in_dim.18), calls=%async_computation.4 | async-start | bytes 3670016 | tf_op jit(solution)/shard_map/all_to_all | solution.py:19
  140.0 5.1 %copy-start.2 = (bf16[4,2,2,64,256]{4,3,2,1,0:T(8,128)(2,1)S(1)}, bf16[4,2,2,64,256]{4,3,2,1,0:T(8,128)(2,1)}, u32[]{:S(2)}) copy-start(bf16[4,2,2,64,256]{4,3,2,1,0:T(8,128)(2,1)} %copy-done.1) | copy-start | bytes 1572868
  140.0 5.1 %copy-start.6 = (bf16[896,256]{1,0:T(8,128)(2,1)S(1)}, bf16[896,256]{1,0:T(8,128)(2,1)}, u32[]{:S(2)}) copy-start(bf16[896,256]{1,0:T(8,128)(2,1)} %param.13) | copy-start | bytes 1376260
  150.5 16.0 %copy-start.3 = (bf16[256,896]{1,0:T(8,128)(2,1)S(1)}, bf16[256,896]{1,0:T(8,128)(2,1)}, u32[]{:S(2)}) copy-start(bf16[256,896]{1,0:T(8,128)(2,1)} %param.12) | copy-start | bytes 1376260
  150.5 16.7 %copy-start.4 = (bf16[256,896]{1,0:T(8,128)(2,1)S(1)}, bf16[256,896]{1,0:T(8,128)(2,1)}, u32[]{:S(2)}) copy-start(bf16[256,896]{1,0:T(8,128)(2,1)} %param.11) | copy-start | bytes 1376260
  168.8 13.8 %all-to-all-start.5 = ((bf16[8,2,64,256]{3,2,1,0:T(8,128)(2,1)}), bf16[8,2,64,256]{3,2,1,0:T(8,128)(2,1)S(1)}, u32[]{:S(2)}, u32[]{:S(2)}) async-start(bf16[8,2,64,256]{3,2,1,0:T(8,128)(2,1)} %bitcast.38), calls=%async_computation.5 | async-start | bytes 1048576 | tf_op jit(solution)/shard_map/all_to_all | solution.py:19
  176.7 15.2 %copy-start = (bf16[4,8,32,896]{3,2,1,0:T(8,128)(2,1)S(1)}, bf16[4,8,32,896]{3,2,1,0:T(8,128)(2,1)}, u32[]{:S(2)}) copy-start(bf16[4,8,32,896]{3,2,1,0:T(8,128)(2,1)} %get-tuple-element.17) | copy-start | bytes 5505028
  182.7 18.5 %collective-permute-start.8 = (f32[64,256]{1,0:T(8,128)S(1)}, f32[64,256]{1,0:T(8,128)S(1)}, u32[]{:S(2)}, u32[]{:S(2)}) collective-permute-start(f32[64,256]{1,0:T(8,128)S(1)} %select_bitcast_fusion.6), channel_id=1, source_target_pairs={{0,2},{1,3},{2,0},{3,1},{4,6},{5,7},{6,4},{7,5},{8,10},{9,11},{10,... | collective-permute-start | bytes 196616 | tf_op jit(solution)/shard_map/ppermute | solution.py:108

commit v8 on v7

--- a/solution.py
+++ b/solution.py
@@ -44,46 +44,50 @@
 
     both = jnp.stack([out_grad, tokens])
     both = pair(both, "tensor", ZH_SWAP, tensor // C % ZH, 1)
-    both = gather(both, "tensor", Y_GROUPS)
+    grads_y = gather(both[0], "tensor", Y_GROUPS)
 
     saved = jnp.stack([gate_pre, up_pre])
     saved = pair(saved, "dp", [(d, d ^ 4) for d in range(X * ZL)], z // 4, 0)
-    saved, both = lax.optimization_barrier((saved, both))
+    saved, grads_y = lax.optimization_barrier((saved, grads_y))
     saved = pair(saved, "dp", [(d, d ^ 2) for d in range(X * ZL)], z // 2 % 2, 1)
     saved = pair(saved, "dp", [(d, d ^ 1) for d in range(X * ZL)], z % 2, 2)
     saved = saved.reshape(ZL, 2, toks, hid)
 
-    grads_all = lax.all_gather(both[:, 0], "tensor", axis_index_groups=C_GROUPS)
+    grads_all = lax.all_gather(grads_y, "tensor", axis_index_groups=C_GROUPS)
     grads_all = grads_all.transpose(1, 2, 0, 3, 4).reshape(n, feats)
 
     partial = jnp.einsum(
         "nd,fd->nf", grads_all, down_weight, preferred_element_type=jnp.float32
     ).astype(jnp.bfloat16)
-    inputs, _ = lax.optimization_barrier((both[:, 1], partial))
-    tokens_all = lax.all_gather(inputs, "tensor", axis_index_groups=C_GROUPS)
-    tokens_all = tokens_all.transpose(1, 2, 0, 3, 4).reshape(n, feats)
     partial = add_up(partial.reshape(X, ZL * toks, hid), "dp", X_GROUPS).astype(jnp.bfloat16)
-    partial, saved = lax.optimization_barrier((partial, saved))
+    partial, saved, inputs = lax.optimization_barrier((partial, saved, both[1]))
+
+    tokens_y = lax.all_gather(inputs, "tensor", axis_index_groups=Y_GROUPS)
 
     from_down = lax.ppermute(saved, "dp", X_UP)
     from_up = lax.ppermute(saved, "dp", X_DOWN)
 
     hidden = add_up(partial.reshape(ZL, toks, hid), "dp", Z_GROUPS).astype(jnp.bfloat16)
 
+    hidden, tokens_y = lax.optimization_barrier((hidden, tokens_y))
+    tokens_all = lax.all_gather(tokens_y, "tensor", axis_index_groups=C_GROUPS)
+    tokens_all = tokens_all.transpose(1, 2, 0, 3, 4).reshape(n, feats)
+
     far_low = lax.ppermute(from_down[: ZL // 2], "dp", X_UP)
     far_high = lax.ppermute(from_up[ZL // 2 :], "dp", X_DOWN)
 
     hidden = gather(hidden, "dp", Z_GROUPS)
-    hidden = gather(hidden, "dp", X_GROUPS).reshape(n, hid).astype(jnp.float32)
 
     full = jnp.broadcast_to(saved[None], (X,) + saved.shape)
-    for block, start, half in (
-        (from_down, (x + X - 1) % X, 0),
-        (from_up, (x + 1) % X, 0),
-        (far_low, (x + 2) % X, 0),
-        (far_high, (x + 2) % X, ZL // 2),
+    for block, start in (
+        (from_down, (x + X - 1) % X),
+        (from_up, (x + 1) % X),
+        (far_low, (x + 2) % X),
     ):
-        full = lax.dynamic_update_slice(full, block[None], (start, half, 0, 0, 0))
+        full = lax.dynamic_update_slice(full, block[None], (start, 0, 0, 0, 0))
+    full = lax.dynamic_update_slice(full, far_high[None], ((x + 2) % X, ZL // 2, 0, 0, 0))
+
+    hidden = gather(hidden, "dp", X_GROUPS).reshape(n, hid).astype(jnp.float32)
     gate_all = full[:, :, 0].reshape(n, hid)
     up_all = full[:, :, 1].reshape(n, hid)
 
@@ -91,10 +95,11 @@
     up_float = up_all.astype(jnp.float32)
     gate_sigmoid = 1.0 / (1.0 + jnp.exp(-gate_float))
     active = (gate_float * gate_sigmoid * up_float).astype(jnp.bfloat16)
-    gate_grad = (
-        hidden * up_float * gate_sigmoid * (1.0 + gate_float * (1.0 - gate_sigmoid))
-    ).astype(jnp.bfloat16)
-    up_grad = (hidden * gate_float * gate_sigmoid).astype(jnp.bfloat16)
+    gate_factor = up_float * gate_sigmoid * (1.0 + gate_float * (1.0 - gate_sigmoid))
+    up_factor = gate_float * gate_sigmoid
+    gate_factor, up_factor = lax.optimization_barrier((gate_factor, up_factor))
+    gate_grad = (hidden * gate_factor).astype(jnp.bfloat16)
+    up_grad = (hidden * up_factor).astype(jnp.bfloat16)
 
     partial_in = jnp.einsum(
         "nf,df->nd", gate_grad, gate_weight, preferred_element_type=jnp.float32

time: 203 us -> 202 us (level)
  the two profiles are of different devices: /device:TPU:160 before, /device:TPU:33 now
where the time goes in v8:
time: 202 us; the launch traced here: 199 us
  starting transfers between devices  81.8 us (40%)
  waiting for transfers between devices  57.3 us (28%)
  other arithmetic  24 us (12%)
  blocking collectives  17.6 us (9%)
  matrix products  10.1 us (5%)
  local copies, waits for them, and re-layouts  7.57 us (4%)
    all_to_all x6, starting transfers between devices, exchange(): lax.all_to_all(blocks, axis, 0, 0, axis_index_groups=groups, tiled=True)  33.9 us
    all_to_all x6, waiting for transfers between devices, exchange(): lax.all_to_all(blocks, axis, 0, 0, axis_index_groups=groups, tiled=True)  30.3 us
    ppermute x4, starting transfers between devices, pair(): other = lax.ppermute(block, axis, perm)  26.3 us
    ppermute x4, waiting for transfers between devices, pair(): other = lax.ppermute(block, axis, perm)  16 us
    all_gather x1, blocking collectives, on_device(): tokens_y = lax.all_gather(inputs, 'tensor', axis_index_groups=Y_GROUPS)  10.9 us
    ppermute x1, starting transfers between devices, on_device(): lax.ppermute(sent, 'tensor', ZH_SWAP)  8.58 us
    mul x1, other arithmetic, on_device(): up_factor = gate_float * gate_sigmoid  7.29 us
    ppermute x1, waiting for transfers between devices, on_device(): far_low = lax.ppermute(from_down[:ZL // 2], 'dp', X_UP)  5.08 us
  transfers between devices with their start and end apart: 15, of which 10 were waited for; matrix products, arithmetic and copies ran while one was open for 14% of the time, Pallas kernels for 0%

profile of v8, /device:TPU:33, one launch (start us, length us, event | category | flops | bytes accessed | tf_op | source)
XLA Modules:
  0.0 199.5 jit_solution(9562858742303442842)
XLA Ops:
  1.5 14.5 %collective-permute-start.1 = (bf16[2,64,256]{2,1,0:T(8,128)(2,1)S(1)}, bf16[2,64,256]{2,1,0:T(8,128)(2,1)S(1)}, u32[]{:S(2)}, u32[]{:S(2)}) collective-permute-start(bf16[2,64,256]{2,1,0:T(8,128)(2,1)S(1)} %pad_maximum_fusion.5), channel_id=1, source_target_pairs={{0,2},{1,3},{2,0},{3,1},{4,6},{5,7},{6,4},{7,5},{8,10},{9,11},{10,... | collective-permute-start | bytes 196616 | tf_op jit(solution)/shard_map/ppermute | solution.py:32
  16.9 4.0 %collective-permute-start = (bf16[2,32,896]{2,1,0:T(8,128)(2,1)S(1)}, bf16[2,32,896]{2,1,0:T(8,128)(2,1)S(1)}, u32[]{:S(2)}, u32[]{:S(2)}) collective-permute-start(bf16[2,32,896]{2,1,0:T(8,128)(2,1)S(1)} %pad_maximum_fusion.3), channel_id=1, source_target_pairs={{0,64},{16,80},{32,96},{48,112},{64,0},{80,16},{96,32},{112,48},{1... | collective-permute-start | bytes 344072 | tf_op jit(solution)/shard_map/ppermute | solution.py:32
  22.5 4.2 %all-to-all-start = ((bf16[4,2,64,256]{3,2,1,0:T(8,128)(2,1)}), bf16[4,2,64,256]{3,2,1,0:T(8,128)(2,1)S(1)}, u32[]{:S(2)}, u32[]{:S(2)}) async-start(bf16[4,2,64,256]{3,2,1,0:T(8,128)(2,1)} %broadcast_in_dim.38), calls=%async_computation | async-start | bytes 524288 | tf_op jit(solution)/shard_map/all_to_all | solution.py:19
  26.7 5.5 %collective-permute-done = bf16[2,32,896]{2,1,0:T(8,128)(2,1)S(1)} collective-permute-done((bf16[2,32,896]{2,1,0:T(8,128)(2,1)S(1)}, bf16[2,32,896]{2,1,0:T(8,128)(2,1)S(1)}, u32[]{:S(2)}, u32[]{:S(2)}) %collective-permute-start) | collective-permute-done | bytes 114720 | tf_op jit(solution)/shard_map/ppermute | solution.py:32
  35.6 4.5 %all-gather = bf16[8,2,64,256]{3,2,1,0:T(8,128)(2,1)S(1)} all-gather(bf16[4,2,64,256]{3,2,1,0:T(8,128)(2,1)S(1)} %all-to-all-done), channel_id=2, replica_groups={{0,1},{2,3},{4,5},{6,7},{8,9},{10,11},{12,13},{14,15},{16,17},{18,19},{..., dimensions={0}, use_global_device_ids=true | all-gather | bytes 786432 | tf_op jit(solution)/shard_map/all_gather | solution.py:56
  42.1 4.0 %all-to-all-start.1 = ((bf16[4,256,896]{2,1,0:T(8,128)(2,1)}), bf16[4,256,896]{2,1,0:T(8,128)(2,1)S(1)}, u32[]{:S(2)}, u32[]{:S(2)}) async-start(bf16[4,256,896]{2,1,0:T(8,128)(2,1)} %bitcast.99), calls=%async_computation.1 | async-start | bytes 3670016 | tf_op jit(solution)/shard_map/all_to_all | solution.py:19
  46.3 5.3 %collective-permute-start.3 = (bf16[2,2,2,32,896]{4,3,2,1,0:T(8,128)(2,1)S(1)}, bf16[2,2,2,32,896]{4,3,2,1,0:T(8,128)(2,1)}, u32[]{:S(2)}, u32[]{:S(2)}) collective-permute-start(bf16[2,2,2,32,896]{4,3,2,1,0:T(8,128)(2,1)S(1)} %pad_maximum_fusion.1), channel_id=1, source_target_pairs={{0,16},{16,0},{32,48},{48,32},{64,80},{80,64},{96,112},{112,96},{1... | collective-permute-start | bytes 1376264 | tf_op jit(solution)/shard_map/ppermute | solution.py:32
  51.6 10.5 %collective-permute-done.3 = bf16[2,2,2,32,896]{4,3,2,1,0:T(8,128)(2,1)} collective-permute-done((bf16[2,2,2,32,896]{4,3,2,1,0:T(8,128)(2,1)S(1)}, bf16[2,2,2,32,896]{4,3,2,1,0:T(8,128)(2,1)}, u32[]{:S(2)}, u32[]{:S(2)}) %collective-permute-start.3) | collective-permute-done | bytes 458784 | tf_op jit(solution)/shard_map/ppermute | solution.py:32
  63.3 5.7 %all-to-all-done.1 = bf16[4,256,896]{2,1,0:T(8,128)(2,1)S(1)} async-done(((bf16[4,256,896]{2,1,0:T(8,128)(2,1)}), bf16[4,256,896]{2,1,0:T(8,128)(2,1)S(1)}, u32[]{:S(2)}, u32[]{:S(2)}) %all-to-all-start.1) | async-done | bytes 1835040 | tf_op jit(solution)/shard_map/all_to_all | solution.py:19
  70.2 7.6 %all-to-all-start.2 = ((bf16[8,32,896]{2,1,0:T(8,128)(2,1)}), bf16[8,32,896]{2,1,0:T(8,128)(2,1)}, u32[]{:S(2)}, u32[]{:S(2)}) async-start(bf16[8,32,896]{2,1,0:T(8,128)(2,1)} %bitcast.110), calls=%async_computation.2 | async-start | bytes 917504 | tf_op jit(solution)/shard_map/all_to_all | solution.py:19
  80.1 4.3 %collective-permute-start.5 = (bf16[8,2,32,896]{3,2,1,0:T(8,128)(2,1)S(1)}, bf16[8,2,32,896]{3,2,1,0:T(8,128)(2,1)S(1)}, u32[]{:S(2)}, u32[]{:S(2)}) collective-permute-start(bf16[8,2,32,896]{3,2,1,0:T(8,128)(2,1)S(1)} %bitcast.103), channel_id=1, source_target_pairs={{0,384},{16,400},{32,416},{48,432},{64,448},{80,464},{96,480},{112... | collective-permute-start | bytes 2752520 | tf_op jit(solution)/shard_map/ppermute | solution.py:68
  84.4 10.9 %all-gather.1 = bf16[8,64,256]{2,1,0:T(8,128)(2,1)} all-gather(bf16[2,64,256]{2,1,0:T(8,128)(2,1)S(1)} %get-tuple-element.16), channel_id=3, replica_groups={{0,4,8,12},{1,5,9,13},{2,6,10,14},{3,7,11,15},{16,20,24,28},{17,21,25,2..., dimensions={0}, use_global_device_ids=true | all-gather | bytes 327680 | tf_op jit(solution)/shard_map/all_gather | solution.py:65
  95.3 5.8 %all-to-all-done.2 = bf16[8,32,896]{2,1,0:T(8,128)(2,1)} async-done(((bf16[8,32,896]{2,1,0:T(8,128)(2,1)}), bf16[8,32,896]{2,1,0:T(8,128)(2,1)}, u32[]{:S(2)}, u32[]{:S(2)}) %all-to-all-start.2) | async-done | bytes 458784 | tf_op jit(solution)/shard_map/all_to_all | solution.py:19
  102.9 6.4 %all-to-all-start.3 = ((bf16[8,32,896]{2,1,0:T(8,128)(2,1)}), bf16[8,32,896]{2,1,0:T(8,128)(2,1)}, u32[]{:S(2)}, u32[]{:S(2)}) async-start(bf16[8,32,896]{2,1,0:T(8,128)(2,1)} %broadcast_in_dim.39), calls=%async_computation.3 | async-start | bytes 917504 | tf_op jit(solution)/shard_map/all_to_all | solution.py:19
  111.7 4.3 %collective-permute-start.7 = (bf16[4,2,32,896]{3,2,1,0:T(8,128)(2,1)S(1)}, bf16[4,2,32,896]{3,2,1,0:T(8,128)(2,1)S(1)}, u32[]{:S(2)}, u32[]{:S(2)}) collective-permute-start(bf16[4,2,32,896]{3,2,1,0:T(8,128)(2,1)S(1)} %slice.37), channel_id=1, source_target_pairs={{0,384},{16,400},{32,416},{48,432},{64,448},{80,464},{96,480},{112... | collective-permute-start | bytes 1376264 | tf_op jit(solution)/shard_map/ppermute | solution.py:77
  116.8 5.1 %collective-permute-done.6 = bf16[4,2,32,896]{3,2,1,0:T(8,128)(2,1)S(1)} collective-permute-done((bf16[4,2,32,896]{3,2,1,0:T(8,128)(2,1)S(1)}, bf16[4,2,32,896]{3,2,1,0:T(8,128)(2,1)S(1)}, u32[]{:S(2)}, u32[]{:S(2)}) %collective-permute-start.6) | collective-permute-done | bytes 458784 | tf_op jit(solution)/shard_map/ppermute | solution.py:76
  127.4 5.1 %all-to-all-done.3 = bf16[8,32,896]{2,1,0:T(8,128)(2,1)} async-done(((bf16[8,32,896]{2,1,0:T(8,128)(2,1)}), bf16[8,32,896]{2,1,0:T(8,128)(2,1)}, u32[]{:S(2)}, u32[]{:S(2)}) %all-to-all-start.3) | async-done | bytes 458784 | tf_op jit(solution)/shard_map/all_to_all | solution.py:19
  134.9 4.4 %all-to-all-start.4 = ((bf16[4,8,32,896]{3,2,1,0:T(8,128)(2,1)}), bf16[4,8,32,896]{3,2,1,0:T(8,128)(2,1)}, u32[]{:S(2)}, u32[]{:S(2)}) async-start(bf16[4,8,32,896]{3,2,1,0:T(8,128)(2,1)} %broadcast_in_dim.40), calls=%async_computation.4 | async-start | bytes 3670016 | tf_op jit(solution)/shard_map/all_to_all | solution.py:19
  139.3 7.3 %bitcast_multiply_fusion = (f32[1024,896]{1,0:T(8,128)}, f32[1024,896]{1,0:T(8,128)}) fusion(bf16[4,8,2,32,896]{4,3,2,1,0:T(8,128)(2,1)} %copy-done, f32[4,8,1,32,896]{4,3,2,1,0:T(8,128)} %slice_convert_fusion), kind=kLoop, calls=%fused_computation.4 | loop fusion | flops 9175040 | bytes 12845056 | tf_op jit(solution)/shard_map/mul | solution.py:99
  149.0 11.6 %all-to-all-done.4 = bf16[4,8,32,896]{3,2,1,0:T(8,128)(2,1)} async-done(((bf16[4,8,32,896]{3,2,1,0:T(8,128)(2,1)}), bf16[4,8,32,896]{3,2,1,0:T(8,128)(2,1)}, u32[]{:S(2)}, u32[]{:S(2)}) %all-to-all-start.4) | async-done | bytes 1835040 | tf_op jit(solution)/shard_map/all_to_all | solution.py:19
  160.6 4.3 %fusion.1 = (bf16[1024,896]{1,0:T(8,128)(2,1)S(1)}, bf16[1024,896]{1,0:T(8,128)(2,1)S(1)}) fusion(f32[1024,896]{1,0:T(8,128)} %get-tuple-element.21, bf16[4,8,32,896]{3,2,1,0:T(8,128)(2,1)} %all-to-all-done.4, f32[1024,896]{1,0:T(8,128)} %get-tuple-element.20), kind=kLoop, calls=%fused_computation.3 | loop fusion | flops 4587520 | bytes 12845056 | tf_op jit(solution)/shard_map/convert_element_type | solution.py:102
  167.3 7.2 %all-to-all-start.5 = ((bf16[8,2,64,256]{3,2,1,0:T(8,128)(2,1)}), bf16[8,2,64,256]{3,2,1,0:T(8,128)(2,1)S(1)}, u32[]{:S(2)}, u32[]{:S(2)}) async-start(bf16[8,2,64,256]{3,2,1,0:T(8,128)(2,1)} %bitcast.38), calls=%async_computation.5 | async-start | bytes 1048576 | tf_op jit(solution)/shard_map/all_to_all | solution.py:19
  184.0 8.6 %collective-permute-start.8 = (f32[64,256]{1,0:T(8,128)S(1)}, f32[64,256]{1,0:T(8,128)S(1)}, u32[]{:S(2)}, u32[]{:S(2)}) collective-permute-start(f32[64,256]{1,0:T(8,128)S(1)} %select_bitcast_fusion.6), channel_id=1, source_target_pairs={{0,2},{1,3},{2,0},{3,1},{4,6},{5,7},{6,4},{7,5},{8,10},{9,11},{10,... | collective-permute-start | bytes 196616 | tf_op jit(solution)/shard_map/ppermute | solution.py:113
  194.3 4.6 %collective-permute-done.8 = f32[64,256]{1,0:T(8,128)S(1)} collective-permute-done((f32[64,256]{1,0:T(8,128)S(1)}, f32[64,256]{1,0:T(8,128)S(1)}, u32[]{:S(2)}, u32[]{:S(2)}) %collective-permute-start.8) | collective-permute-done | bytes 65568 | tf_op jit(solution)/shard_map/ppermute | solution.py:113
  (67 shorter events, 42.7 us)
Async XLA Ops:
  0.6 39.5 %copy-start.9 = (bf16[896,256]{1,0:T(8,128)(2,1)S(1)}, bf16[896,256]{1,0:T(8,128)(2,1)}, u32[]{:S(2)}) copy-start(bf16[896,256]{1,0:T(8,128)(2,1)} %param.13) | copy-start | bytes 1376260
  1.5 19.5 %collective-permute-start.1 = (bf16[2,64,256]{2,1,0:T(8,128)(2,1)S(1)}, bf16[2,64,256]{2,1,0:T(8,128)(2,1)S(1)}, u32[]{:S(2)}, u32[]{:S(2)}) collective-permute-start(bf16[2,64,256]{2,1,0:T(8,128)(2,1)S(1)} %pad_maximum_fusion.5), channel_id=1, source_target_pairs={{0,2},{1,3},{2,0},{3,1},{4,6},{5,7},{6,4},{7,5},{8,10},{9,11},{10,... | collective-permute-start | bytes 196616 | tf_op jit(solution)/shard_map/ppermute | solution.py:32
  16.9 15.3 %collective-permute-start = (bf16[2,32,896]{2,1,0:T(8,128)(2,1)S(1)}, bf16[2,32,896]{2,1,0:T(8,128)(2,1)S(1)}, u32[]{:S(2)}, u32[]{:S(2)}) collective-permute-start(bf16[2,32,896]{2,1,0:T(8,128)(2,1)S(1)} %pad_maximum_fusion.3), channel_id=1, source_target_pairs={{0,64},{16,80},{32,96},{48,112},{64,0},{80,16},{96,32},{112,48},{1... | collective-permute-start | bytes 344072 | tf_op jit(solution)/shard_map/ppermute | solution.py:32
  22.5 10.6 %all-to-all-start = ((bf16[4,2,64,256]{3,2,1,0:T(8,128)(2,1)}), bf16[4,2,64,256]{3,2,1,0:T(8,128)(2,1)S(1)}, u32[]{:S(2)}, u32[]{:S(2)}) async-start(bf16[4,2,64,256]{3,2,1,0:T(8,128)(2,1)} %broadcast_in_dim.38), calls=%async_computation | async-start | bytes 524288 | tf_op jit(solution)/shard_map/all_to_all | solution.py:19
  33.1 13.0 %collective-permute-start.2 = (bf16[2,2,32,896]{3,2,1,0:T(8,128)(2,1)S(1)}, bf16[2,2,32,896]{3,2,1,0:T(8,128)(2,1)S(1)}, u32[]{:S(2)}, u32[]{:S(2)}) collective-permute-start(bf16[2,2,32,896]{3,2,1,0:T(8,128)(2,1)S(1)} %pad_maximum_fusion.2), channel_id=1, source_target_pairs={{0,32},{16,48},{32,0},{48,16},{64,96},{80,112},{96,64},{112,80},{1... | collective-permute-start | bytes 688136 | tf_op jit(solution)/shard_map/ppermute | solution.py:32
  42.1 27.0 %all-to-all-start.1 = ((bf16[4,256,896]{2,1,0:T(8,128)(2,1)}), bf16[4,256,896]{2,1,0:T(8,128)(2,1)S(1)}, u32[]{:S(2)}, u32[]{:S(2)}) async-start(bf16[4,256,896]{2,1,0:T(8,128)(2,1)} %bitcast.99), calls=%async_computation.1 | async-start | bytes 3670016 | tf_op jit(solution)/shard_map/all_to_all | solution.py:19
  46.3 15.9 %collective-permute-start.3 = (bf16[2,2,2,32,896]{4,3,2,1,0:T(8,128)(2,1)S(1)}, bf16[2,2,2,32,896]{4,3,2,1,0:T(8,128)(2,1)}, u32[]{:S(2)}, u32[]{:S(2)}) collective-permute-start(bf16[2,2,2,32,896]{4,3,2,1,0:T(8,128)(2,1)S(1)} %pad_maximum_fusion.1), channel_id=1, source_target_pairs={{0,16},{16,0},{32,48},{48,32},{64,80},{80,64},{96,112},{112,96},{1... | collective-permute-start | bytes 1376264 | tf_op jit(solution)/shard_map/ppermute | solution.py:32
  70.2 30.8 %all-to-all-start.2 = ((bf16[8,32,896]{2,1,0:T(8,128)(2,1)}), bf16[8,32,896]{2,1,0:T(8,128)(2,1)}, u32[]{:S(2)}, u32[]{:S(2)}) async-start(bf16[8,32,896]{2,1,0:T(8,128)(2,1)} %bitcast.110), calls=%async_computation.2 | async-start | bytes 917504 | tf_op jit(solution)/shard_map/all_to_all | solution.py:19
  77.9 31.5 %collective-permute-start.4 = (bf16[8,2,32,896]{3,2,1,0:T(8,128)(2,1)S(1)}, bf16[8,2,32,896]{3,2,1,0:T(8,128)(2,1)S(1)}, u32[]{:S(2)}, u32[]{:S(2)}) collective-permute-start(bf16[8,2,32,896]{3,2,1,0:T(8,128)(2,1)S(1)} %bitcast.102), channel_id=1, source_target_pairs={{0,128},{16,144},{32,160},{48,176},{64,192},{80,208},{96,224},{112... | collective-permute-start | bytes 2752520 | tf_op jit(solution)/shard_map/ppermute | solution.py:67
  80.1 31.5 %collective-permute-start.5 = (bf16[8,2,32,896]{3,2,1,0:T(8,128)(2,1)S(1)}, bf16[8,2,32,896]{3,2,1,0:T(8,128)(2,1)S(1)}, u32[]{:S(2)}, u32[]{:S(2)}) collective-permute-start(bf16[8,2,32,896]{3,2,1,0:T(8,128)(2,1)S(1)} %bitcast.103), channel_id=1, source_target_pairs={{0,384},{16,400},{32,416},{48,432},{64,448},{80,464},{96,480},{112... | collective-permute-start | bytes 2752520 | tf_op jit(solution)/shard_map/ppermute | solution.py:68
  102.9 29.6 %all-to-all-start.3 = ((bf16[8,32,896]{2,1,0:T(8,128)(2,1)}), bf16[8,32,896]{2,1,0:T(8,128)(2,1)}, u32[]{:S(2)}, u32[]{:S(2)}) async-start(bf16[8,32,896]{2,1,0:T(8,128)(2,1)} %broadcast_in_dim.39), calls=%async_computation.3 | async-start | bytes 917504 | tf_op jit(solution)/shard_map/all_to_all | solution.py:19
  109.4 12.4 %collective-permute-start.6 = (bf16[4,2,32,896]{3,2,1,0:T(8,128)(2,1)S(1)}, bf16[4,2,32,896]{3,2,1,0:T(8,128)(2,1)S(1)}, u32[]{:S(2)}, u32[]{:S(2)}) collective-permute-start(bf16[4,2,32,896]{3,2,1,0:T(8,128)(2,1)S(1)} %slice.36), channel_id=1, source_target_pairs={{0,128},{16,144},{32,160},{48,176},{64,192},{80,208},{96,224},{112... | collective-permute-start | bytes 1376264 | tf_op jit(solution)/shard_map/ppermute | solution.py:76
  111.7 11.6 %collective-permute-start.7 = (bf16[4,2,32,896]{3,2,1,0:T(8,128)(2,1)S(1)}, bf16[4,2,32,896]{3,2,1,0:T(8,128)(2,1)S(1)}, u32[]{:S(2)}, u32[]{:S(2)}) collective-permute-start(bf16[4,2,32,896]{3,2,1,0:T(8,128)(2,1)S(1)} %slice.37), channel_id=1, source_target_pairs={{0,384},{16,400},{32,416},{48,432},{64,448},{80,464},{96,480},{112... | collective-permute-start | bytes 1376264 | tf_op jit(solution)/shard_map/ppermute | solution.py:77
  134.9 25.7 %all-to-all-start.4 = ((bf16[4,8,32,896]{3,2,1,0:T(8,128)(2,1)}), bf16[4,8,32,896]{3,2,1,0:T(8,128)(2,1)}, u32[]{:S(2)}, u32[]{:S(2)}) async-start(bf16[4,8,32,896]{3,2,1,0:T(8,128)(2,1)} %broadcast_in_dim.40), calls=%async_computation.4 | async-start | bytes 3670016 | tf_op jit(solution)/shard_map/all_to_all | solution.py:19
  139.3 7.3 %copy-start.1 = (bf16[4,8,2,32,896]{4,3,2,1,0:T(8,128)(2,1)S(1)}, bf16[4,8,2,32,896]{4,3,2,1,0:T(8,128)(2,1)}, u32[]{:S(2)}) copy-start(bf16[4,8,2,32,896]{4,3,2,1,0:T(8,128)(2,1)} %copy-done) | copy-start | bytes 11010052
  149.0 15.9 %copy-start.4 = (bf16[256,896]{1,0:T(8,128)(2,1)S(1)}, bf16[256,896]{1,0:T(8,128)(2,1)}, u32[]{:S(2)}) copy-start(bf16[256,896]{1,0:T(8,128)(2,1)} %param.11) | copy-start | bytes 1376260
  149.0 16.7 %copy-start.6 = (bf16[256,896]{1,0:T(8,128)(2,1)S(1)}, bf16[256,896]{1,0:T(8,128)(2,1)}, u32[]{:S(2)}) copy-start(bf16[256,896]{1,0:T(8,128)(2,1)} %param.12) | copy-start | bytes 1376260
  164.9 2.4 %copy-start.2 = (bf16[1024,896]{1,0:T(8,128)(2,1)}, bf16[1024,896]{1,0:T(8,128)(2,1)S(1)}, u32[]{:S(2)}) copy-start(bf16[1024,896]{1,0:T(8,128)(2,1)S(1)} %get-tuple-element.24) | copy-start | bytes 5505028
  167.3 10.5 %copy-start.8 = (bf16[8,64,256]{2,1,0:T(8,128)(2,1)S(1)}, bf16[8,64,256]{2,1,0:T(8,128)(2,1)}, u32[]{:S(2)}) copy-start(bf16[8,64,256]{2,1,0:T(8,128)(2,1)} %all-gather.1) | copy-start | bytes 786436
  167.3 16.7 %all-to-all-start.5 = ((bf16[8,2,64,256]{3,2,1,0:T(8,128)(2,1)}), bf16[8,2,64,256]{3,2,1,0:T(8,128)(2,1)S(1)}, u32[]{:S(2)}, u32[]{:S(2)}) async-start(bf16[8,2,64,256]{3,2,1,0:T(8,128)(2,1)} %bitcast.38), calls=%async_computation.5 | async-start | bytes 1048576 | tf_op jit(solution)/shard_map/all_to_all | solution.py:19
  174.5 5.7 %copy-start.3 = (bf16[1024,896]{1,0:T(8,128)(2,1)S(1)}, bf16[1024,896]{1,0:T(8,128)(2,1)}, u32[]{:S(2)}) copy-start(bf16[1024,896]{1,0:T(8,128)(2,1)} %copy-done.2) | copy-start | bytes 5505028
  174.5 5.7 %copy-start.7 = (bf16[256,896]{1,0:T(8,128)(2,1)S(1)}, bf16[256,896]{1,0:T(8,128)(2,1)}, u32[]{:S(2)}) copy-start(bf16[256,896]{1,0:T(8,128)(2,1)} %param.12) | copy-start | bytes 1376260
  177.8 14.8 %copy-start.5 = (bf16[256,896]{1,0:T(8,128)(2,1)S(1)}, bf16[256,896]{1,0:T(8,128)(2,1)}, u32[]{:S(2)}) copy-start(bf16[256,896]{1,0:T(8,128)(2,1)} %param.11) | copy-start | bytes 1376260
  184.0 14.8 %collective-permute-start.8 = (f32[64,256]{1,0:T(8,128)S(1)}, f32[64,256]{1,0:T(8,128)S(1)}, u32[]{:S(2)}, u32[]{:S(2)}) collective-permute-start(f32[64,256]{1,0:T(8,128)S(1)} %select_bitcast_fusion.6), channel_id=1, source_target_pairs={{0,2},{1,3},{2,0},{3,1},{4,6},{5,7},{6,4},{7,5},{8,10},{9,11},{10,... | collective-permute-start | bytes 196616 | tf_op jit(solution)/shard_map/ppermute | solution.py:113
  (1 other events, 1.8 us)

commit v9 on v8

--- a/solution.py
+++ b/solution.py
@@ -48,7 +48,7 @@
 
     saved = jnp.stack([gate_pre, up_pre])
     saved = pair(saved, "dp", [(d, d ^ 4) for d in range(X * ZL)], z // 4, 0)
-    saved, grads_y = lax.optimization_barrier((saved, grads_y))
+    saved, _ = lax.optimization_barrier((saved, grads_y))
     saved = pair(saved, "dp", [(d, d ^ 2) for d in range(X * ZL)], z // 2 % 2, 1)
     saved = pair(saved, "dp", [(d, d ^ 1) for d in range(X * ZL)], z % 2, 2)
     saved = saved.reshape(ZL, 2, toks, hid)
@@ -97,7 +97,6 @@
     active = (gate_float * gate_sigmoid * up_float).astype(jnp.bfloat16)
     gate_factor = up_float * gate_sigmoid * (1.0 + gate_float * (1.0 - gate_sigmoid))
     up_factor = gate_float * gate_sigmoid
-    gate_factor, up_factor = lax.optimization_barrier((gate_factor, up_factor))
     gate_grad = (hidden * gate_factor).astype(jnp.bfloat16)
     up_grad = (hidden * up_factor).astype(jnp.bfloat16)
 

time: 202 us -> 202 us (level)
  local copies, waits for them, and re-layouts: 7.57 us -> 11.8 us
  waiting for transfers between devices: 57.3 us -> 54.7 us
    mul x1 -> x0, other arithmetic: 7.29 us -> none  [on_device(): up_factor = gate_float * gate_sigmoid]
    convert_element_type x0 -> x1, other arithmetic: none -> 3.9 us  [on_device(): gate_grad = (hidden * gate_factor).astype(jnp.bfloat16)]
    ppermute x1, waiting for transfers between devices: 5.08 us -> 2.31 us  [on_device(): far_low = lax.ppermute(from_down[:ZL // 2], 'dp', X_UP)]
    all_to_all x6, waiting for transfers between devices: 30.3 us -> 33 us  [exchange(): lax.all_to_all(blocks, axis, 0, 0, axis_index_groups=groups, tiled=True)]
    dynamic_update_slice x3, local copies, waits for them, and re-layouts: 0.33 us -> 2.86 us  [on_device(): full = lax.dynamic_update_slice(full, block[None], (start, 0, 0, 0, 0))]
  transfers between devices with their start and end apart: 15 -> 15, of which waited for: 10 -> 10; matrix products, arithmetic and copies ran while one was open for 14% -> 17% of each run, Pallas kernels for 0% -> 0%
where the time goes in v9:
time: 202 us; the launch traced here: 201 us
  starting transfers between devices  80.1 us (40%)
  waiting for transfers between devices  54.7 us (27%)
  other arithmetic  24.3 us (12%)
  blocking collectives  19.6 us (10%)
  local copies, waits for them, and re-layouts  11.8 us (6%)
  matrix products  9.45 us (5%)
    all_to_all x6, waiting for transfers between devices, exchange(): lax.all_to_all(blocks, axis, 0, 0, axis_index_groups=groups, tiled=True)  33 us
    all_to_all x6, starting transfers between devices, exchange(): lax.all_to_all(blocks, axis, 0, 0, axis_index_groups=groups, tiled=True)  32.5 us
    ppermute x4, starting transfers between devices, pair(): other = lax.ppermute(block, axis, perm)  25.7 us
    ppermute x4, waiting for transfers between devices, pair(): other = lax.ppermute(block, axis, perm)  15 us
    all_gather x1, blocking collectives, on_device(): tokens_y = lax.all_gather(inputs, 'tensor', axis_index_groups=Y_GROUPS)  10.7 us
    ppermute x1, starting transfers between devices, on_device(): lax.ppermute(sent, 'tensor', ZH_SWAP)  8.93 us
    broadcast_in_dim x3, local copies, waits for them, and re-layouts, gather(): copies = jnp.broadcast_to(block[None], (len(groups[0]),) + block.shape)  4.84 us
    all_gather x1, blocking collectives, on_device(): grads_all = lax.all_gather(grads_y, 'tensor', axis_index_groups=C_GROUPS)  4.75 us
  transfers between devices with their start and end apart: 15, of which 10 were waited for; matrix products, arithmetic and copies ran while one was open for 17% of the time, Pallas kernels for 0%

profile of v9, /device:TPU:33, one launch (start us, length us, event | category | flops | bytes accessed | tf_op | source)
XLA Modules:
  0.0 201.0 jit_solution(14742931174313199442)
XLA Ops:
  1.5 14.5 %collective-permute-start = (bf16[2,64,256]{2,1,0:T(8,128)(2,1)S(1)}, bf16[2,64,256]{2,1,0:T(8,128)(2,1)S(1)}, u32[]{:S(2)}, u32[]{:S(2)}) collective-permute-start(bf16[2,64,256]{2,1,0:T(8,128)(2,1)S(1)} %pad_maximum_fusion.5), channel_id=1, source_target_pairs={{0,2},{1,3},{2,0},{3,1},{4,6},{5,7},{6,4},{7,5},{8,10},{9,11},{10,... | collective-permute-start | bytes 196616 | tf_op jit(solution)/shard_map/ppermute | solution.py:32
  16.9 4.0 %collective-permute-start.1 = (bf16[2,32,896]{2,1,0:T(8,128)(2,1)S(1)}, bf16[2,32,896]{2,1,0:T(8,128)(2,1)S(1)}, u32[]{:S(2)}, u32[]{:S(2)}) collective-permute-start(bf16[2,32,896]{2,1,0:T(8,128)(2,1)S(1)} %pad_maximum_fusion.3), channel_id=1, source_target_pairs={{0,64},{16,80},{32,96},{48,112},{64,0},{80,16},{96,32},{112,48},{1... | collective-permute-start | bytes 344072 | tf_op jit(solution)/shard_map/ppermute | solution.py:32
  23.1 4.2 %all-to-all-start = ((bf16[4,2,64,256]{3,2,1,0:T(8,128)(2,1)}), bf16[4,2,64,256]{3,2,1,0:T(8,128)(2,1)S(1)}, u32[]{:S(2)}, u32[]{:S(2)}) async-start(bf16[4,2,64,256]{3,2,1,0:T(8,128)(2,1)} %broadcast_in_dim.38), calls=%async_computation | async-start | bytes 524288 | tf_op jit(solution)/shard_map/all_to_all | solution.py:19
  27.3 4.9 %collective-permute-done.1 = bf16[2,32,896]{2,1,0:T(8,128)(2,1)S(1)} collective-permute-done((bf16[2,32,896]{2,1,0:T(8,128)(2,1)S(1)}, bf16[2,32,896]{2,1,0:T(8,128)(2,1)S(1)}, u32[]{:S(2)}, u32[]{:S(2)}) %collective-permute-start.1) | collective-permute-done | bytes 114720 | tf_op jit(solution)/shard_map/ppermute | solution.py:32
  36.0 4.8 %all-gather = bf16[8,2,64,256]{3,2,1,0:T(8,128)(2,1)S(1)} all-gather(bf16[4,2,64,256]{3,2,1,0:T(8,128)(2,1)S(1)} %all-to-all-done), channel_id=2, replica_groups={{0,1},{2,3},{4,5},{6,7},{8,9},{10,11},{12,13},{14,15},{16,17},{18,19},{..., dimensions={0}, use_global_device_ids=true | all-gather | bytes 786432 | tf_op jit(solution)/shard_map/all_gather | solution.py:56
  42.8 4.0 %all-to-all-start.1 = ((bf16[4,256,896]{2,1,0:T(8,128)(2,1)}), bf16[4,256,896]{2,1,0:T(8,128)(2,1)S(1)}, u32[]{:S(2)}, u32[]{:S(2)}) async-start(bf16[4,256,896]{2,1,0:T(8,128)(2,1)} %bitcast.142), calls=%async_computation.1 | async-start | bytes 3670016 | tf_op jit(solution)/shard_map/all_to_all | solution.py:19
  46.9 4.3 %collective-permute-start.3 = (bf16[2,2,2,32,896]{4,3,2,1,0:T(8,128)(2,1)S(1)}, bf16[2,2,2,32,896]{4,3,2,1,0:T(8,128)(2,1)}, u32[]{:S(2)}, u32[]{:S(2)}) collective-permute-start(bf16[2,2,2,32,896]{4,3,2,1,0:T(8,128)(2,1)S(1)} %pad_maximum_fusion.1), channel_id=1, source_target_pairs={{0,16},{16,0},{32,48},{48,32},{64,80},{80,64},{96,112},{112,96},{1... | collective-permute-start | bytes 1376264 | tf_op jit(solution)/shard_map/ppermute | solution.py:32
  51.2 10.1 %collective-permute-done.3 = bf16[2,2,2,32,896]{4,3,2,1,0:T(8,128)(2,1)} collective-permute-done((bf16[2,2,2,32,896]{4,3,2,1,0:T(8,128)(2,1)S(1)}, bf16[2,2,2,32,896]{4,3,2,1,0:T(8,128)(2,1)}, u32[]{:S(2)}, u32[]{:S(2)}) %collective-permute-start.3) | collective-permute-done | bytes 458784 | tf_op jit(solution)/shard_map/ppermute | solution.py:32
  62.6 7.1 %all-to-all-done.1 = bf16[4,256,896]{2,1,0:T(8,128)(2,1)S(1)} async-done(((bf16[4,256,896]{2,1,0:T(8,128)(2,1)}), bf16[4,256,896]{2,1,0:T(8,128)(2,1)S(1)}, u32[]{:S(2)}, u32[]{:S(2)}) %all-to-all-start.1) | async-done | bytes 1835040 | tf_op jit(solution)/shard_map/all_to_all | solution.py:19
  70.9 7.6 %all-to-all-start.2 = ((bf16[8,32,896]{2,1,0:T(8,128)(2,1)}), bf16[8,32,896]{2,1,0:T(8,128)(2,1)}, u32[]{:S(2)}, u32[]{:S(2)}) async-start(bf16[8,32,896]{2,1,0:T(8,128)(2,1)} %bitcast.155), calls=%async_computation.2 | async-start | bytes 917504 | tf_op jit(solution)/shard_map/all_to_all | solution.py:19
  80.7 4.3 %collective-permute-start.5 = (bf16[8,2,32,896]{3,2,1,0:T(8,128)(2,1)S(1)}, bf16[8,2,32,896]{3,2,1,0:T(8,128)(2,1)S(1)}, u32[]{:S(2)}, u32[]{:S(2)}) collective-permute-start(bf16[8,2,32,896]{3,2,1,0:T(8,128)(2,1)S(1)} %bitcast.148), channel_id=1, source_target_pairs={{0,384},{16,400},{32,416},{48,432},{64,448},{80,464},{96,480},{112... | collective-permute-start | bytes 2752520 | tf_op jit(solution)/shard_map/ppermute | solution.py:68
  85.0 10.7 %all-gather.1 = bf16[8,64,256]{2,1,0:T(8,128)(2,1)S(1)} all-gather(bf16[2,64,256]{2,1,0:T(8,128)(2,1)} %get-tuple-element.12), channel_id=3, replica_groups={{0,4,8,12},{1,5,9,13},{2,6,10,14},{3,7,11,15},{16,20,24,28},{17,21,25,2..., dimensions={0}, use_global_device_ids=true | all-gather | bytes 327680 | tf_op jit(solution)/shard_map/all_gather | solution.py:65
  95.7 6.0 %all-to-all-done.2 = bf16[8,32,896]{2,1,0:T(8,128)(2,1)} async-done(((bf16[8,32,896]{2,1,0:T(8,128)(2,1)}), bf16[8,32,896]{2,1,0:T(8,128)(2,1)}, u32[]{:S(2)}, u32[]{:S(2)}) %all-to-all-start.2) | async-done | bytes 458784 | tf_op jit(solution)/shard_map/all_to_all | solution.py:19
  105.0 6.4 %all-to-all-start.3 = ((bf16[8,32,896]{2,1,0:T(8,128)(2,1)}), bf16[8,32,896]{2,1,0:T(8,128)(2,1)}, u32[]{:S(2)}, u32[]{:S(2)}) async-start(bf16[8,32,896]{2,1,0:T(8,128)(2,1)} %broadcast_in_dim.39), calls=%async_computation.3 | async-start | bytes 917504 | tf_op jit(solution)/shard_map/all_to_all | solution.py:19
  113.8 4.3 %collective-permute-start.7 = (bf16[4,2,32,896]{3,2,1,0:T(8,128)(2,1)S(1)}, bf16[4,2,32,896]{3,2,1,0:T(8,128)(2,1)S(1)}, u32[]{:S(2)}, u32[]{:S(2)}) collective-permute-start(bf16[4,2,32,896]{3,2,1,0:T(8,128)(2,1)S(1)} %slice.37), channel_id=1, source_target_pairs={{0,384},{16,400},{32,416},{48,432},{64,448},{80,464},{96,480},{112... | collective-permute-start | bytes 1376264 | tf_op jit(solution)/shard_map/ppermute | solution.py:77
  126.4 8.2 %all-to-all-done.3 = bf16[8,32,896]{2,1,0:T(8,128)(2,1)} async-done(((bf16[8,32,896]{2,1,0:T(8,128)(2,1)}), bf16[8,32,896]{2,1,0:T(8,128)(2,1)}, u32[]{:S(2)}, u32[]{:S(2)}) %all-to-all-start.3) | async-done | bytes 458784 | tf_op jit(solution)/shard_map/all_to_all | solution.py:19
  145.5 3.8 %slice_convert_fusion = f32[4,8,1,32,896]{4,3,2,1,0:T(8,128)} fusion(bf16[4,8,2,32,896]{4,3,2,1,0:T(8,128)(2,1)} %bitcast_dynamic-update-slice_fusion.2), kind=kLoop, calls=%fused_computation.34 | loop fusion | flops 917504 | bytes 5505024 | tf_op jit(solution)/shard_map/convert_element_type | solution.py:95
  149.4 4.2 %all-gather.2 = bf16[8,2,64,256]{3,2,1,0:T(8,128)(2,1)S(1)} all-gather(bf16[4,2,64,256]{3,2,1,0:T(8,128)(2,1)S(1)} %bitcast.157), channel_id=4, replica_groups={{0,1},{2,3},{4,5},{6,7},{8,9},{10,11},{12,13},{14,15},{16,17},{18,19},{..., dimensions={0}, use_global_device_ids=true | all-gather | bytes 786432 | tf_op jit(solution)/shard_map/all_gather | solution.py:73
  153.6 8.3 %all-to-all-done.4 = bf16[4,8,32,896]{3,2,1,0:T(8,128)(2,1)S(1)} async-done(((bf16[4,8,32,896]{3,2,1,0:T(8,128)(2,1)}), bf16[4,8,32,896]{3,2,1,0:T(8,128)(2,1)S(1)}, u32[]{:S(2)}, u32[]{:S(2)}) %all-to-all-start.4) | async-done | bytes 1835040 | tf_op jit(solution)/shard_map/all_to_all | solution.py:19
  161.8 3.9 %fusion.22 = (bf16[1024,896]{1,0:T(8,128)(2,1)S(1)}, bf16[1024,896]{1,0:T(8,128)(2,1)S(1)}) fusion(f32[4,8,1,32,896]{4,3,2,1,0:T(8,128)} %slice_convert_fusion, bf16[4,8,32,896]{3,2,1,0:T(8,128)(2,1)S(1)} %all-to-all-done.4, bf16[4,8,2,32,896]{4,3,2,1,0:T(8,128)(2,1)} %bitcast_dynamic-update-slice_fusion.2), kind=kLoop, calls=%fused_computation.28 | loop fusion | flops 13762560 | bytes 11010048 | tf_op jit(solution)/shard_map/convert_element_type | solution.py:100
  168.1 6.7 %all-to-all-start.5 = ((bf16[8,2,64,256]{3,2,1,0:T(8,128)(2,1)}), bf16[8,2,64,256]{3,2,1,0:T(8,128)(2,1)S(1)}, u32[]{:S(2)}, u32[]{:S(2)}) async-start(bf16[8,2,64,256]{3,2,1,0:T(8,128)(2,1)} %bitcast.41), calls=%async_computation.5 | async-start | bytes 1048576 | tf_op jit(solution)/shard_map/all_to_all | solution.py:19
  174.8 4.4 %fusion.11 = (bf16[4,8,32,896]{3,2,1,0:T(8,128)(2,1)S(1)}, bf16[4,8,32,896]{3,2,1,0:T(8,128)(2,1)}) fusion(bf16[4,8,32,896]{3,2,1,0:T(8,128)(2,1)S(1)} %all-to-all-done.4, bf16[4,8,2,32,896]{4,3,2,1,0:T(8,128)(2,1)} %bitcast_dynamic-update-slice_fusion.2), kind=kLoop, calls=%fused_computation.17 | loop fusion | flops 14680064 | bytes 9175040 | tf_op jit(solution)/shard_map/convert_element_type | solution.py:101
  184.4 8.9 %collective-permute-start.8 = (f32[64,256]{1,0:T(8,128)S(1)}, f32[64,256]{1,0:T(8,128)S(1)}, u32[]{:S(2)}, u32[]{:S(2)}) collective-permute-start(f32[64,256]{1,0:T(8,128)S(1)} %select_bitcast_fusion.6), channel_id=1, source_target_pairs={{0,2},{1,3},{2,0},{3,1},{4,6},{5,7},{6,4},{7,5},{8,10},{9,11},{10,... | collective-permute-start | bytes 196616 | tf_op jit(solution)/shard_map/ppermute | solution.py:112
  196.0 4.4 %collective-permute-done.8 = f32[64,256]{1,0:T(8,128)S(1)} collective-permute-done((f32[64,256]{1,0:T(8,128)S(1)}, f32[64,256]{1,0:T(8,128)S(1)}, u32[]{:S(2)}, u32[]{:S(2)}) %collective-permute-start.8) | collective-permute-done | bytes 65568 | tf_op jit(solution)/shard_map/ppermute | solution.py:112
  (57 shorter events, 49.9 us)
Async XLA Ops:
  0.6 40.1 %copy-start.3 = (bf16[896,256]{1,0:T(8,128)(2,1)S(1)}, bf16[896,256]{1,0:T(8,128)(2,1)}, u32[]{:S(2)}) copy-start(bf16[896,256]{1,0:T(8,128)(2,1)} %param.13) | copy-start | bytes 1376260
  1.5 19.5 %collective-permute-start = (bf16[2,64,256]{2,1,0:T(8,128)(2,1)S(1)}, bf16[2,64,256]{2,1,0:T(8,128)(2,1)S(1)}, u32[]{:S(2)}, u32[]{:S(2)}) collective-permute-start(bf16[2,64,256]{2,1,0:T(8,128)(2,1)S(1)} %pad_maximum_fusion.5), channel_id=1, source_target_pairs={{0,2},{1,3},{2,0},{3,1},{4,6},{5,7},{6,4},{7,5},{8,10},{9,11},{10,... | collective-permute-start | bytes 196616 | tf_op jit(solution)/shard_map/ppermute | solution.py:32
  16.9 15.3 %collective-permute-start.1 = (bf16[2,32,896]{2,1,0:T(8,128)(2,1)S(1)}, bf16[2,32,896]{2,1,0:T(8,128)(2,1)S(1)}, u32[]{:S(2)}, u32[]{:S(2)}) collective-permute-start(bf16[2,32,896]{2,1,0:T(8,128)(2,1)S(1)} %pad_maximum_fusion.3), channel_id=1, source_target_pairs={{0,64},{16,80},{32,96},{48,112},{64,0},{80,16},{96,32},{112,48},{1... | collective-permute-start | bytes 344072 | tf_op jit(solution)/shard_map/ppermute | solution.py:32
  23.1 10.0 %all-to-all-start = ((bf16[4,2,64,256]{3,2,1,0:T(8,128)(2,1)}), bf16[4,2,64,256]{3,2,1,0:T(8,128)(2,1)S(1)}, u32[]{:S(2)}, u32[]{:S(2)}) async-start(bf16[4,2,64,256]{3,2,1,0:T(8,128)(2,1)} %broadcast_in_dim.38), calls=%async_computation | async-start | bytes 524288 | tf_op jit(solution)/shard_map/all_to_all | solution.py:19
  33.1 13.7 %collective-permute-start.2 = (bf16[2,2,32,896]{3,2,1,0:T(8,128)(2,1)S(1)}, bf16[2,2,32,896]{3,2,1,0:T(8,128)(2,1)S(1)}, u32[]{:S(2)}, u32[]{:S(2)}) collective-permute-start(bf16[2,2,32,896]{3,2,1,0:T(8,128)(2,1)S(1)} %pad_maximum_fusion.2), channel_id=1, source_target_pairs={{0,32},{16,48},{32,0},{48,16},{64,96},{80,112},{96,64},{112,80},{1... | collective-permute-start | bytes 688136 | tf_op jit(solution)/shard_map/ppermute | solution.py:32
  42.8 27.0 %all-to-all-start.1 = ((bf16[4,256,896]{2,1,0:T(8,128)(2,1)}), bf16[4,256,896]{2,1,0:T(8,128)(2,1)S(1)}, u32[]{:S(2)}, u32[]{:S(2)}) async-start(bf16[4,256,896]{2,1,0:T(8,128)(2,1)} %bitcast.142), calls=%async_computation.1 | async-start | bytes 3670016 | tf_op jit(solution)/shard_map/all_to_all | solution.py:19
  46.9 14.5 %collective-permute-start.3 = (bf16[2,2,2,32,896]{4,3,2,1,0:T(8,128)(2,1)S(1)}, bf16[2,2,2,32,896]{4,3,2,1,0:T(8,128)(2,1)}, u32[]{:S(2)}, u32[]{:S(2)}) collective-permute-start(bf16[2,2,2,32,896]{4,3,2,1,0:T(8,128)(2,1)S(1)} %pad_maximum_fusion.1), channel_id=1, source_target_pairs={{0,16},{16,0},{32,48},{48,32},{64,80},{80,64},{96,112},{112,96},{1... | collective-permute-start | bytes 1376264 | tf_op jit(solution)/shard_map/ppermute | solution.py:32
  70.9 30.8 %all-to-all-start.2 = ((bf16[8,32,896]{2,1,0:T(8,128)(2,1)}), bf16[8,32,896]{2,1,0:T(8,128)(2,1)}, u32[]{:S(2)}, u32[]{:S(2)}) async-start(bf16[8,32,896]{2,1,0:T(8,128)(2,1)} %bitcast.155), calls=%async_computation.2 | async-start | bytes 917504 | tf_op jit(solution)/shard_map/all_to_all | solution.py:19
  78.5 32.9 %collective-permute-start.4 = (bf16[8,2,32,896]{3,2,1,0:T(8,128)(2,1)S(1)}, bf16[8,2,32,896]{3,2,1,0:T(8,128)(2,1)S(1)}, u32[]{:S(2)}, u32[]{:S(2)}) collective-permute-start(bf16[8,2,32,896]{3,2,1,0:T(8,128)(2,1)S(1)} %bitcast.147), channel_id=1, source_target_pairs={{0,128},{16,144},{32,160},{48,176},{64,192},{80,208},{96,224},{112... | collective-permute-start | bytes 2752520 | tf_op jit(solution)/shard_map/ppermute | solution.py:67
  80.7 33.0 %collective-permute-start.5 = (bf16[8,2,32,896]{3,2,1,0:T(8,128)(2,1)S(1)}, bf16[8,2,32,896]{3,2,1,0:T(8,128)(2,1)S(1)}, u32[]{:S(2)}, u32[]{:S(2)}) collective-permute-start(bf16[8,2,32,896]{3,2,1,0:T(8,128)(2,1)S(1)} %bitcast.148), channel_id=1, source_target_pairs={{0,384},{16,400},{32,416},{48,432},{64,448},{80,464},{96,480},{112... | collective-permute-start | bytes 2752520 | tf_op jit(solution)/shard_map/ppermute | solution.py:68
  105.0 29.6 %all-to-all-start.3 = ((bf16[8,32,896]{2,1,0:T(8,128)(2,1)}), bf16[8,32,896]{2,1,0:T(8,128)(2,1)}, u32[]{:S(2)}, u32[]{:S(2)}) async-start(bf16[8,32,896]{2,1,0:T(8,128)(2,1)} %broadcast_in_dim.39), calls=%async_computation.3 | async-start | bytes 917504 | tf_op jit(solution)/shard_map/all_to_all | solution.py:19
  111.5 13.2 %collective-permute-start.6 = (bf16[4,2,32,896]{3,2,1,0:T(8,128)(2,1)S(1)}, bf16[4,2,32,896]{3,2,1,0:T(8,128)(2,1)S(1)}, u32[]{:S(2)}, u32[]{:S(2)}) collective-permute-start(bf16[4,2,32,896]{3,2,1,0:T(8,128)(2,1)S(1)} %slice.36), channel_id=1, source_target_pairs={{0,128},{16,144},{32,160},{48,176},{64,192},{80,208},{96,224},{112... | collective-permute-start | bytes 1376264 | tf_op jit(solution)/shard_map/ppermute | solution.py:76
  113.8 11.8 %collective-permute-start.7 = (bf16[4,2,32,896]{3,2,1,0:T(8,128)(2,1)S(1)}, bf16[4,2,32,896]{3,2,1,0:T(8,128)(2,1)S(1)}, u32[]{:S(2)}, u32[]{:S(2)}) collective-permute-start(bf16[4,2,32,896]{3,2,1,0:T(8,128)(2,1)S(1)} %slice.37), channel_id=1, source_target_pairs={{0,384},{16,400},{32,416},{48,432},{64,448},{80,464},{96,480},{112... | collective-permute-start | bytes 1376264 | tf_op jit(solution)/shard_map/ppermute | solution.py:77
  137.1 24.7 %all-to-all-start.4 = ((bf16[4,8,32,896]{3,2,1,0:T(8,128)(2,1)}), bf16[4,8,32,896]{3,2,1,0:T(8,128)(2,1)S(1)}, u32[]{:S(2)}, u32[]{:S(2)}) async-start(bf16[4,8,32,896]{3,2,1,0:T(8,128)(2,1)} %broadcast_in_dim.40), calls=%async_computation.4 | async-start | bytes 3670016 | tf_op jit(solution)/shard_map/all_to_all | solution.py:19
  140.7 3.2 %copy-start.4 = (bf16[896,256]{1,0:T(8,128)(2,1)S(1)}, bf16[896,256]{1,0:T(8,128)(2,1)}, u32[]{:S(2)}) copy-start(bf16[896,256]{1,0:T(8,128)(2,1)} %param.13) | copy-start | bytes 1376260
  153.6 12.2 %copy-start.1 = (bf16[256,896]{1,0:T(8,128)(2,1)S(1)}, bf16[256,896]{1,0:T(8,128)(2,1)}, u32[]{:S(2)}) copy-start(bf16[256,896]{1,0:T(8,128)(2,1)} %param.12) | copy-start | bytes 1376260
  153.6 12.9 %copy-start.2 = (bf16[256,896]{1,0:T(8,128)(2,1)S(1)}, bf16[256,896]{1,0:T(8,128)(2,1)}, u32[]{:S(2)}) copy-start(bf16[256,896]{1,0:T(8,128)(2,1)} %param.11) | copy-start | bytes 1376260
  168.1 16.2 %all-to-all-start.5 = ((bf16[8,2,64,256]{3,2,1,0:T(8,128)(2,1)}), bf16[8,2,64,256]{3,2,1,0:T(8,128)(2,1)S(1)}, u32[]{:S(2)}, u32[]{:S(2)}) async-start(bf16[8,2,64,256]{3,2,1,0:T(8,128)(2,1)} %bitcast.41), calls=%async_computation.5 | async-start | bytes 1048576 | tf_op jit(solution)/shard_map/all_to_all | solution.py:19
  179.2 14.1 %copy-start = (bf16[4,8,32,896]{3,2,1,0:T(8,128)(2,1)S(1)}, bf16[4,8,32,896]{3,2,1,0:T(8,128)(2,1)}, u32[]{:S(2)}) copy-start(bf16[4,8,32,896]{3,2,1,0:T(8,128)(2,1)} %get-tuple-element.19) | copy-start | bytes 5505028
  184.4 16.0 %collective-permute-start.8 = (f32[64,256]{1,0:T(8,128)S(1)}, f32[64,256]{1,0:T(8,128)S(1)}, u32[]{:S(2)}, u32[]{:S(2)}) collective-permute-start(f32[64,256]{1,0:T(8,128)S(1)} %select_bitcast_fusion.6), channel_id=1, source_target_pairs={{0,2},{1,3},{2,0},{3,1},{4,6},{5,7},{6,4},{7,5},{8,10},{9,11},{10,... | collective-permute-start | bytes 196616 | tf_op jit(solution)/shard_map/ppermute | solution.py:112
